TPU v7x, 512 devices: a whole 4x4x16 slice. The times are simulated.
512 devices in a mesh: gy: 32 (over y, x, core), gz: 16 (over z).
Axes of the slice: x: 4, y: 4, z: 16, core: 2. Of those that a mesh axis runs over, the one named last changes fastest.
Arguments:
- fluid_state: float32 [5, 8, 2048, 2048], P(None, None, 'gy', 'gz'), may hold values from -1 to 3, as said below
- tracer_cell: int32 [32, 16, 16, 128], P('gy', 'gz'), may hold values from 0 to 4095
- tracer_owner: int32 [32, 16, 16], P('gy', 'gz'), may hold values from 0 to 15, as said below
- tracer_count: int32 [32, 16, 16], P('gy', 'gz'), may hold values from 32 to 128, as said below
- tracer_peak: float32 [32, 16, 16, 128], P('gy', 'gz'), may hold values from 0.5 to 2.5
Outputs:
- new_state: float32 [5, 8, 2048, 2048], P(None, None, ('gy', 'gz'))
- new_peak: float32 [32, 16, 16, 128], P('gy', 'gz')
Inputs may be any that keep to these rules, and one draw needn't show every extreme that they name: `fluid_state`: density from 0.5 to 3, velocities from -1 to 1, pressure from 0.5 to 2.5. `tracer_owner`: the blocks held at one index of gy and gz name every owner once. `tracer_count`: each count is 128 or lies between 32 and 64; at each index of gy one owner gets a full block from every index of gz.
All inputs are finite; a program needn't handle non-finite values.
Results may differ from a plain program's by a relative error of at most 0.000075.
Values sent between devices are 32-bit elements; how exact they have to be, the bound alone decides.
No kernel may reach another device: no remote copies, remote signals or barrier semaphores. Data moves between devices by JAX's collectives and lax.ppermute only.
A program may use at most 128 MiB of HBM per device.

v0:
```python
import jax
import jax.numpy as jnp
from jax import lax
from jax.sharding import PartitionSpec as P

GAMMA = 1.4
RATIO = 0.06


def extended_2(cells, sides, width):
    for axis, dim in sides:
        count = lax.axis_size(axis)
        head = lax.slice_in_dim(cells, 0, width, axis=dim)
        tail = lax.slice_in_dim(cells, cells.shape[dim] - width, cells.shape[dim], axis=dim)
        cells = jnp.concatenate(
            [
                lax.ppermute(tail, axis, [(i, (i + 1) % count) for i in range(count)]),
                cells,
                lax.ppermute(head, axis, [((i + 1) % count, i) for i in range(count)]),
            ],
            axis=dim,
        )
    return cells


def median_of(first, second, third):
    return jnp.maximum(jnp.minimum(first, second), jnp.minimum(jnp.maximum(first, second), third))


def slice_of(values, offset, length, along):
    return lax.slice_in_dim(values, offset, offset + length, axis=along)


def conserved(fields):
    density = fields[0]
    kinetic = (
        0.5 * density * (fields[1] * fields[1] + fields[2] * fields[2] + fields[3] * fields[3])
    )
    return jnp.stack(
        [
            density,
            density * fields[1],
            density * fields[2],
            density * fields[3],
            fields[4] / (GAMMA - 1.0) + kinetic,
        ]
    )


def primitive(totals):
    density = totals[0]
    vel_x = totals[1] / density
    vel_y = totals[2] / density
    vel_z = totals[3] / density
    kinetic = 0.5 * (totals[1] * vel_x + totals[2] * vel_y + totals[3] * vel_z)
    return jnp.stack([density, vel_x, vel_y, vel_z, (GAMMA - 1.0) * (totals[4] - kinetic)])


def physical_flux(fields, totals, normal):
    normal_vel = fields[normal]
    pieces = [totals[k] * normal_vel for k in range(5)]
    pieces[normal] = pieces[normal] + fields[4]
    pieces[4] = (totals[4] + fields[4]) * normal_vel
    return jnp.stack(pieces)


def advance(extended, along, normal):
    interior_n = extended.shape[along] - 6
    faces_n = interior_n + 3
    face_val = 7.0 / 12.0 * (
        slice_of(extended, 1, faces_n, along) + slice_of(extended, 2, faces_n, along)
    ) - 1.0 / 12.0 * (slice_of(extended, 0, faces_n, along) + slice_of(extended, 3, faces_n, along))
    lower_bound = jnp.minimum(
        slice_of(extended, 1, faces_n, along), slice_of(extended, 2, faces_n, along)
    )
    upper_bound = jnp.maximum(
        slice_of(extended, 1, faces_n, along), slice_of(extended, 2, faces_n, along)
    )
    face_val = jnp.minimum(jnp.maximum(face_val, lower_bound), upper_bound)
    centre = slice_of(extended, 2, interior_n + 2, along)
    left_gap = centre - slice_of(face_val, 0, interior_n + 2, along)
    right_gap = slice_of(face_val, 1, interior_n + 2, along) - centre
    edge_left = centre - median_of(0.0, left_gap, 2.0 * right_gap)
    edge_right = centre + median_of(0.0, right_gap, 2.0 * left_gap)
    state_left = slice_of(edge_right, 0, interior_n + 1, along)
    state_right = slice_of(edge_left, 1, interior_n + 1, along)
    totals_left = conserved(state_left)
    totals_right = conserved(state_right)
    sound_left = jnp.sqrt(GAMMA * state_left[4] / state_left[0])
    sound_right = jnp.sqrt(GAMMA * state_right[4] / state_right[0])
    slowest = jnp.minimum(
        jnp.minimum(state_left[normal] - sound_left, state_right[normal] - sound_right), 0.0
    )
    fastest = jnp.maximum(
        jnp.maximum(state_left[normal] + sound_left, state_right[normal] + sound_right), 0.0
    )
    flux_left = physical_flux(state_left, totals_left, normal)
    flux_right = physical_flux(state_right, totals_right, normal)
    face_flux = (
        fastest * flux_left
        - slowest * flux_right
        + slowest * fastest * (totals_right - totals_left)
    ) / (fastest - slowest)
    interior = conserved(slice_of(extended, 3, interior_n, along))
    updated = interior - RATIO * (
        slice_of(face_flux, 1, interior_n, along) - slice_of(face_flux, 0, interior_n, along)
    )
    return primitive(updated)


def wrap_pad(fields, along):
    length = fields.shape[along]
    return jnp.concatenate(
        [slice_of(fields, length - 3, 3, along), fields, slice_of(fields, 0, 3, along)], axis=along
    )


def sample_rows(flat_press, row_ids, col_ids):
    width = flat_press.shape[1]
    pick_z = (col_ids[:, None] == lax.broadcasted_iota(jnp.int32, (1, width), 1)).astype(
        jnp.float32
    )
    partial_value = lax.dot_general(
        pick_z,
        flat_press,
        (((1,), (1,)), ((), ())),
        precision=lax.Precision.HIGHEST,
        preferred_element_type=jnp.float32,
    )
    chosen = row_ids[:, None] == lax.broadcasted_iota(jnp.int32, (1, flat_press.shape[0]), 1)
    return jnp.sum(jnp.where(chosen, partial_value, 0.0), axis=1)


def on_device(fluid_state, tracer_cell, tracer_owner, tracer_count, tracer_peak):
    planes = fluid_state.shape[1]
    rows_y = fluid_state.shape[2]
    cols_z = fluid_state.shape[3]
    pencil_rows = rows_y // lax.axis_size("gz")
    margin = extended_2(fluid_state, (("gy", 2),), 3)
    blocks = advance(margin, 2, 2)
    new_state = advance(
        wrap_pad(lax.all_to_all(blocks, "gz", split_axis=2, concat_axis=3, tiled=True), 3), 3, 3
    )
    pressure = new_state[4]
    owners_row = tracer_owner[0, 0]
    cell_ids = tracer_cell[0, 0]
    peak_old = tracer_peak[0, 0]
    live_count = tracer_count[0, 0]
    blocks_n = owners_row.shape[0]
    select_mask = owners_row[None, :] == lax.broadcasted_iota(jnp.int32, (blocks_n, blocks_n), 0)
    weights = select_mask.astype(jnp.float32)
    send_cells = jnp.sum(jnp.where(select_mask[:, :, None], cell_ids[None], 0), axis=1)
    send_peaks = jnp.dot(
        weights, peak_old, precision=lax.Precision.HIGHEST, preferred_element_type=jnp.float32
    )
    flat_press = pressure.reshape(planes * pencil_rows, -1)
    got_cells = lax.all_to_all(send_cells, "gz", split_axis=0, concat_axis=0, tiled=True)
    got_peaks = lax.all_to_all(send_peaks, "gz", split_axis=0, concat_axis=0, tiled=True)

    def one_source(inputs_row):
        cell_row, peak_row, source = inputs_row
        row_ids = (
            cell_row // (pencil_rows * cols_z) * pencil_rows + cell_row // cols_z % pencil_rows
        )
        col_ids = source * cols_z + cell_row % cols_z
        return jnp.maximum(peak_row, sample_rows(flat_press, row_ids, col_ids))

    sources = jnp.arange(got_cells.shape[0], dtype=jnp.int32)
    lifted = lax.map(one_source, (got_cells, got_peaks, sources))
    returned = lax.all_to_all(lifted, "gz", split_axis=0, concat_axis=0, tiled=True)
    raised = jnp.dot(
        weights.T, returned, precision=lax.Precision.HIGHEST, preferred_element_type=jnp.float32
    )
    live_mask = lax.broadcasted_iota(jnp.int32, raised.shape, 1) < live_count[:, None]
    new_peak = jnp.where(live_mask, raised, 0.0)[None, None]
    return (new_state, new_peak)


def solution(mesh):
    in_specs = (
        P(None, None, "gy", "gz"),
        P("gy", "gz", None, None),
        P("gy", "gz", None),
        P("gy", "gz", None),
        P("gy", "gz", None, None),
    )
    out_specs = (P(None, None, ("gy", "gz"), None), P("gy", "gz", None, None))
    return jax.shard_map(
        on_device, mesh=mesh, in_specs=in_specs, out_specs=out_specs, check_vma=False
    )
```

profile of v0, /device:TPU:24, one launch (start us, length us, event | category | flops | bytes accessed | tf_op | source)
XLA Modules:
  0.0 225.2 jit_solution(6137243441111066515)
XLA Ops:
  0.6 2.1 copy.25
  2.8 1.9 collective-permute-start
  4.7 5.8 %collective-permute-start.1 = (f32[5,8,3,128]{3,1,0,2:T(8,128)S(1)}, f32[5,8,3,128]{3,1,0,2:T(8,128)S(1)}, u32[]{:S(2)}, u32[]{:S(2)}) collective-permute-start(f32[5,8,3,128]{3,1,0,2:T(8,128)S(1)} %get-tuple-element.177), channel_id=1, source_target_pairs={{16,0},{32,16},{48,32},{64,48},{80,64},{96,80},{112,96},{128,112},... | collective-permute-start | bytes 184328 | tf_op jit(solution)/shard_map/ppermute | solution.py:19
  10.7 1.2 copy-done.1
  11.9 0.8 constant_dynamic-update-slice_fusion.1
  14.8 0.8 add_divide_fusion.1
  16.5 0.7 constant_dynamic-update-slice_fusion.15
  17.3 0.7 constant_dynamic-update-slice_fusion.14
  18.0 0.7 constant_dynamic-update-slice_fusion.13
  18.8 0.8 fusion.26
  19.6 15.3 %all-to-all-start = ((f32[5,8,64,128]{3,1,0,2:T(8,128)}), f32[5,8,64,128]{3,1,0,2:T(8,128)S(1)}, u32[]{:S(2)}, u32[]{:S(2)}) async-start(f32[5,8,64,128]{3,1,0,2:T(8,128)} %fusion.26), calls=%async_computation | async-start | bytes 2621440 | tf_op jit(solution)/shard_map/all_to_all | solution.py:142
  36.4 60.8 %all-to-all-done = f32[5,8,64,128]{3,1,0,2:T(8,128)S(1)} async-done(((f32[5,8,64,128]{3,1,0,2:T(8,128)}), f32[5,8,64,128]{3,1,0,2:T(8,128)S(1)}, u32[]{:S(2)}, u32[]{:S(2)}) %all-to-all-start) | async-done | bytes 1310752 | tf_op jit(solution)/shard_map/all_to_all | solution.py:142
  97.2 6.2 %all-to-all-start.1 = ((f32[16,1,128]{2,1,0:T(1,128)}), f32[16,1,128]{2,1,0:T(1,128)S(1)}, u32[]{:S(2)}, u32[]{:S(2)}) async-start(f32[16,1,128]{2,1,0:T(1,128)} %bitcast.18), calls=%async_computation.1 | async-start | bytes 16384 | tf_op jit(solution)/shard_map/all_to_all | solution.py:158
  103.5 1.8 copy.40
  107.0 0.8 squeeze.29
  108.0 0.8 div.141
  109.3 0.7 fusion.34
  110.0 2.8 %concatenate.21 = f32[5,8,4,2054]{3,2,1,0:T(4,128)S(1)} concatenate(f32[5,8,4,3]{3,2,1,0:T(4,128)} %get-tuple-element.171, f32[5,8,4,2048]{3,2,1,0:T(4,128)S(1)} %all_to_all.40, f32[5,8,4,3]{3,2,1,0:T(4,128)} %get-tuple-element.170), dimensions={3} | concatenate | bytes 2629120 | tf_op jit(solution)/shard_map/concatenate | solution.py:113
  112.8 3.3 %fusion.8 = f32[5,8,4,2051]{3,2,1,0:T(4,128)S(1)} fusion(f32[5,8,4,2048]{3,2,1,0:T(4,128)S(1)} %all_to_all.40, f32[5,8,4,3]{3,2,1,0:T(4,128)} %get-tuple-element.171, f32[5,8,4,3]{3,2,1,0:T(4,128)} %get-tuple-element.170, f32[5,8,4,2054]{3,2,1,0:T(4,128)S(1)} %concatenate.21), kind=kLoop, calls=%fused_computation.29 | loop fusion | flops 3609760 | bytes 5252480 | tf_op jit(solution)/shard_map/min | solution.py:79
  116.1 1.5 maximum_add_fusion.1
  118.9 0.9 multiply_bitcast_fusion
  119.8 0.8 add_dynamic-update-slice_fusion
  120.5 0.9 multiply_dynamic-update-slice_fusion
  122.4 0.9 copy-done.4
  125.1 0.7 fusion.14
  125.8 0.9 fusion.33
  126.7 0.8 constant_dynamic-update-slice_fusion.31
  128.2 0.8 constant_dynamic-update-slice_fusion.30
  128.9 12.0 %all-to-all-start.2 = ((s32[16,1,128]{2,1,0:T(1,128)}), s32[16,1,128]{2,1,0:T(1,128)S(1)}, u32[]{:S(2)}, u32[]{:S(2)}) async-start(s32[16,1,128]{2,1,0:T(1,128)} %bitcast.22), calls=%async_computation.2 | async-start | bytes 16384 | tf_op jit(solution)/shard_map/all_to_all | solution.py:157
  141.0 0.8 constant_dynamic-update-slice_fusion.29
  141.8 11.7 %all-to-all-done.2 = s32[16,1,128]{2,1,0:T(1,128)S(1)} async-done(((s32[16,1,128]{2,1,0:T(1,128)}), s32[16,1,128]{2,1,0:T(1,128)S(1)}, u32[]{:S(2)}, u32[]{:S(2)}) %all-to-all-start.2) | async-done | bytes 8224 | tf_op jit(solution)/shard_map/all_to_all | solution.py:157
  153.4 55.2 %while.14 = (s32[]{:T(128)}, f32[16,128]{1,0:T(8,128)}, f32[16,128]{1,0:T(8,128)S(1)}, s32[16,128]{1,0:T(8,128)S(1)}, s32[16]{0:T(128)S(1)}, /*index=5*/f32[32,2048]{1,0:T(8,128)S(1)}, s32[1]{0:T(128)}) while((s32[]{:T(128)}, f32[16,128]{1,0:T(8,128)}, f32[16,128]{1,0:T(8,128)S(1)}, s32[16,128]{1,0:T(8,128)S(1)}, s32[16]{0:T(128)S(1)}, ...), condition=%wide.region_3.4_spmd.clone, body=%wide.region_1.3_spmd.sunk.clone | while | flops 100943360 | bytes 268925 | solution.py:169
  154.8 0.7 fusion.49
  155.6 1.3 dynamic_update_slice.10
  158.3 0.7 fusion.49
  159.0 1.3 dynamic_update_slice.10
  161.7 0.7 fusion.49
  162.5 1.3 dynamic_update_slice.10
  165.2 0.7 fusion.49
  165.9 1.3 dynamic_update_slice.10
  168.6 0.7 fusion.49
  169.4 1.3 dynamic_update_slice.10
  172.1 0.7 fusion.49
  172.8 1.3 dynamic_update_slice.10
  175.5 0.7 fusion.49
  176.3 1.3 dynamic_update_slice.10
  179.0 0.7 fusion.49
  179.8 1.3 dynamic_update_slice.10
  182.5 0.7 fusion.49
  183.2 1.3 dynamic_update_slice.10
  185.9 0.7 fusion.49
  186.7 1.3 dynamic_update_slice.10
  189.4 0.7 fusion.49
  190.1 1.3 dynamic_update_slice.10
  192.8 0.7 fusion.49
  193.6 1.3 dynamic_update_slice.10
  197.0 1.3 dynamic_update_slice.10
  200.5 1.3 dynamic_update_slice.10
  203.9 1.3 dynamic_update_slice.10
  207.4 1.3 dynamic_update_slice.10
  208.7 3.5 %all-to-all-start.3 = ((f32[16,1,128]{2,1,0:T(1,128)}), f32[16,1,128]{2,1,0:T(1,128)S(1)}, u32[]{:S(2)}, u32[]{:S(2)}) async-start(f32[16,1,128]{2,1,0:T(1,128)} %bitcast.24), calls=%async_computation.3 | async-start | bytes 16384 | tf_op jit(solution)/shard_map/all_to_all | solution.py:170
  212.2 0.9 multiply_dynamic-update-slice_fusion.12
  213.1 11.3 %all-to-all-done.3 = f32[16,1,128]{2,1,0:T(1,128)S(1)} async-done(((f32[16,1,128]{2,1,0:T(1,128)}), f32[16,1,128]{2,1,0:T(1,128)S(1)}, u32[]{:S(2)}, u32[]{:S(2)}) %all-to-all-start.3) | async-done | bytes 8224 | tf_op jit(solution)/shard_map/all_to_all | solution.py:170
  224.4 0.8 fusion.17
  (152 shorter events, 25.8 us)
Async XLA Ops:
  0.6 35.0 %copy-start = (f32[1,1,16,128]{3,2,1,0:T(8,128)S(1)}, f32[1,1,16,128]{3,2,1,0:T(8,128)}, u32[]{:S(2)}) copy-start(f32[1,1,16,128]{3,2,1,0:T(8,128)} %param.11) | copy-start | bytes 24580
  2.8 7.9 %collective-permute-start = (f32[5,8,3,128]{3,1,0,2:T(8,128)S(1)}, f32[5,8,3,128]{3,1,0,2:T(8,128)S(1)}, u32[]{:S(2)}, u32[]{:S(2)}) collective-permute-start(f32[5,8,3,128]{3,1,0,2:T(8,128)S(1)} %get-tuple-element.178), channel_id=1, source_target_pairs={{0,16},{16,32},{32,48},{48,64},{64,80},{80,96},{96,112},{112,128},... | collective-permute-start | bytes 184328 | tf_op jit(solution)/shard_map/ppermute | solution.py:17
  4.7 7.9 %collective-permute-start.1 = (f32[5,8,3,128]{3,1,0,2:T(8,128)S(1)}, f32[5,8,3,128]{3,1,0,2:T(8,128)S(1)}, u32[]{:S(2)}, u32[]{:S(2)}) collective-permute-start(f32[5,8,3,128]{3,1,0,2:T(8,128)S(1)} %get-tuple-element.177), channel_id=1, source_target_pairs={{16,0},{32,16},{48,32},{64,48},{80,64},{96,80},{112,96},{128,112},... | collective-permute-start | bytes 184328 | tf_op jit(solution)/shard_map/ppermute | solution.py:19
  10.5 1.3 copy-start.1
  19.6 15.3 %copy-start.7 = (s32[1,1,16]{2,1,0:T(1,128)S(1)}, s32[1,1,16]{2,1,0:T(1,128)}, u32[]{:S(2)}) copy-start(s32[1,1,16]{2,1,0:T(1,128)} %param.9) | copy-start | bytes 196
  19.6 15.4 %copy-start.6 = (s32[1,1,16,128]{3,2,1,0:T(8,128)S(1)}, s32[1,1,16,128]{3,2,1,0:T(8,128)}, u32[]{:S(2)}) copy-start(s32[1,1,16,128]{3,2,1,0:T(8,128)} %param.8) | copy-start | bytes 24580
  19.6 77.6 %all-to-all-start = ((f32[5,8,64,128]{3,1,0,2:T(8,128)}), f32[5,8,64,128]{3,1,0,2:T(8,128)S(1)}, u32[]{:S(2)}, u32[]{:S(2)}) async-start(f32[5,8,64,128]{3,1,0,2:T(8,128)} %fusion.26), calls=%async_computation | async-start | bytes 2621440 | tf_op jit(solution)/shard_map/all_to_all | solution.py:142
  97.2 31.8 %all-to-all-start.1 = ((f32[16,1,128]{2,1,0:T(1,128)}), f32[16,1,128]{2,1,0:T(1,128)S(1)}, u32[]{:S(2)}, u32[]{:S(2)}) async-start(f32[16,1,128]{2,1,0:T(1,128)} %bitcast.18), calls=%async_computation.1 | async-start | bytes 16384 | tf_op jit(solution)/shard_map/all_to_all | solution.py:158
  106.8 2.1 copy-start.2
  122.0 1.3 copy-start.4
  122.2 1.2 copy-start.3
  123.3 1.0 copy-start.5
  128.9 24.5 %all-to-all-start.2 = ((s32[16,1,128]{2,1,0:T(1,128)}), s32[16,1,128]{2,1,0:T(1,128)S(1)}, u32[]{:S(2)}, u32[]{:S(2)}) async-start(s32[16,1,128]{2,1,0:T(1,128)} %bitcast.22), calls=%async_computation.2 | async-start | bytes 16384 | tf_op jit(solution)/shard_map/all_to_all | solution.py:157
  153.4 71.0 %copy-start.8 = (s32[1,1,16]{2,1,0:T(1,128)S(1)}, s32[1,1,16]{2,1,0:T(1,128)}, u32[]{:S(2)}) copy-start(s32[1,1,16]{2,1,0:T(1,128)} %param.10) | copy-start | bytes 196
  208.7 15.8 %all-to-all-start.3 = ((f32[16,1,128]{2,1,0:T(1,128)}), f32[16,1,128]{2,1,0:T(1,128)S(1)}, u32[]{:S(2)}, u32[]{:S(2)}) async-start(f32[16,1,128]{2,1,0:T(1,128)} %bitcast.24), calls=%async_computation.3 | async-start | bytes 16384 | tf_op jit(solution)/shard_map/all_to_all | solution.py:170
where the time goes:
time: 227 us; the launch traced here: 225 us
  waiting for transfers between devices  83.8 us (37%)
  local copies, waits for them, and re-layouts  48.6 us (21%)
  starting transfers between devices  44.7 us (20%)
  other arithmetic  22.4 us (10%)
  matrix products  13.3 us (6%)
  loops' own time  11.4 us (5%)
    all_to_all x1, waiting for transfers between devices, on_device(): lax.all_to_all(blocks, 'gz', split_axis=2, concat_axis=3, tiled=True)  60.8 us
    dynamic_update_slice x16, local copies, waits for them, and re-layouts, on_device(): lifted = lax.map(one_source, (got_cells, got_peaks, sources))  20.8 us
    all_to_all x1, starting transfers between devices, on_device(): lax.all_to_all(blocks, 'gz', split_axis=2, concat_axis=3, tiled=True)  15.3 us
    all_to_all x1, starting transfers between devices, on_device(): lax.all_to_all(send_cells, 'gz', split_axis=0, concat_axis=0, tiled=True)  12 us
    dot_general x16, matrix products, sample_rows(): lax.dot_general(pick_z, flat_press, (((1,), (1,)), ((), ())), precision=l...  11.7 us
    all_to_all x1, waiting for transfers between devices, on_device(): lax.all_to_all(send_cells, 'gz', split_axis=0, concat_axis=0, tiled=True)  11.7 us
    another operation x1, loops' own time, on_device(): lifted = lax.map(one_source, (got_cells, got_peaks, sources))  11.4 us
    all_to_all x1, waiting for transfers between devices, on_device(): lax.all_to_all(lifted, 'gz', split_axis=0, concat_axis=0, tiled=True)  11.3 us
  transfers between devices with their start and end apart: 6, of which 3 were waited for; matrix products, arithmetic and copies ran while one was open for 12% of the time, Pallas kernels for 0%

commit v1 on v0

v1 whole, which is shorter than its diff:
```python
import jax
import jax.numpy as jnp
from jax import lax
from jax.experimental import pallas as pl
from jax.experimental.pallas import tpu as pltpu
from jax.sharding import PartitionSpec as P

GAMMA = 1.4
RATIO = 0.06
LANES = 128


def median_of(first, second, third):
    return jnp.maximum(jnp.minimum(first, second), jnp.minimum(jnp.maximum(first, second), third))


def face_of(before, left, right, after):
    out = []
    for b, l, r, a in zip(before, left, right, after):
        mid = (7.0 / 12.0) * (l + r) - (1.0 / 12.0) * (b + a)
        out.append(jnp.minimum(jnp.maximum(mid, jnp.minimum(l, r)), jnp.maximum(l, r)))
    return out


def edges_of(centre, face_left, face_right):
    left, right = [], []
    for a, fl, fr in zip(centre, face_left, face_right):
        triple = 3.0 * a
        left.append(median_of(a, fl, triple - 2.0 * fr))
        right.append(median_of(a, fr, triple - 2.0 * fl))
    return left, right


def inverse(value):
    guess = pl.reciprocal(value, approx=True)
    return guess * (2.0 - value * guess)


def flux_of(left, right, normal):
    rho_l, p_l, u_l = left[0], left[4], left[normal]
    rho_r, p_r, u_r = right[0], right[4], right[normal]
    c_l = jnp.sqrt(GAMMA * p_l * inverse(rho_l))
    c_r = jnp.sqrt(GAMMA * p_r * inverse(rho_r))
    slow = jnp.minimum(jnp.minimum(u_l - c_l, u_r - c_r), 0.0)
    fast = jnp.maximum(jnp.maximum(u_l + c_l, u_r + c_r), 0.0)
    scale = RATIO * inverse(fast - slow)
    a_l = fast * scale
    a_r = -slow * scale
    w_l = a_l * (u_l - slow)
    w_r = a_r * (u_r - fast)
    q_l = rho_l * w_l
    q_r = rho_r * w_r
    flux = [q_l + q_r] + [q_l * left[k] + q_r * right[k] for k in (1, 2, 3)]
    flux[normal] = flux[normal] + (a_l * p_l + a_r * p_r)
    square_l = left[1] * left[1] + left[2] * left[2] + left[3] * left[3]
    square_r = right[1] * right[1] + right[2] * right[2] + right[3] * right[3]
    heat = p_l * (2.5 * w_l + a_l * u_l) + p_r * (2.5 * w_r + a_r * u_r)
    flux.append(0.5 * (q_l * square_l + q_r * square_r) + heat)
    return flux


def updated(state, flux_left, flux_right):
    rho, vx, vy, vz, p = state
    mom = [rho * v for v in (vx, vy, vz)]
    energy = 2.5 * p + 0.5 * (mom[0] * vx + mom[1] * vy + mom[2] * vz)
    totals = [
        t - (r - l) for t, l, r in zip([rho] + mom + [energy], flux_left, flux_right)
    ]
    inv = inverse(totals[0])
    vel = [totals[k] * inv for k in (1, 2, 3)]
    kinetic = 0.5 * (totals[1] * vel[0] + totals[2] * vel[1] + totals[3] * vel[2])
    return [totals[0]] + vel + [0.4 * (totals[4] - kinetic)]


def lane_after(here, following, lane):
    return [
        pltpu.roll(jnp.where(lane == 0, f, h), LANES - 1, 1) for h, f in zip(here, following)
    ]


def lane_before(here, previous, lane):
    return [
        pltpu.roll(jnp.where(lane == LANES - 1, p, h), 1, 1) for h, p in zip(here, previous)
    ]


def sweep_y_kernel(fluid_ref, low_ref, high_ref, middle_ref, edge_ref):
    rows_y = fluid_ref.shape[1] // 8
    blocks = middle_ref.shape[0]
    lane = lax.broadcasted_iota(jnp.int32, (8, LANES), 1)

    def row(y):
        return [fluid_ref[k, pl.ds(y, 8, stride=rows_y), :] for k in range(5)]

    def low(i):
        return [low_ref[i, k] for k in range(5)]

    def high(i):
        return [high_ref[i, k] for k in range(5)]

    def block(h, carry, load, packed):
        flux, right, face, c0, c1, c2 = carry
        first, second = packed
        for sub in range(4):
            c3 = load(sub)
            face_next = face_of(c0, c1, c2, c3)
            left_next, right_next = edges_of(c1, face, face_next)
            flux_next = flux_of(right, left_next, 2)
            new = updated(c0, flux, flux_next)
            spot = 4 * (h * 4 + sub) % LANES
            group = lane // 4 == spot // 4
            for k in range(5):
                middle_ref[h, k, pl.ds(sub, 8, stride=4), :] = new[k]
            first = [
                jnp.where(group, pltpu.roll(v, spot, 1), f) for v, f in zip(new, first)
            ]
            second = [
                jnp.where(group, pltpu.roll(v, (spot + 4) % LANES, 1), s)
                for v, s in zip(new, second)
            ]
            flux, right, face, c0, c1, c2 = flux_next, right_next, face_next, c1, c2, c3
        return (flux, right, face, c0, c1, c2), (first, second)

    m3, m2, m1 = low(0), low(1), low(2)
    c0, c1, c2 = row(0), row(1), row(2)
    face_a = face_of(m3, m2, m1, c0)
    face_b = face_of(m2, m1, c0, c1)
    face_c = face_of(m1, c0, c1, c2)
    _, right_a = edges_of(m1, face_a, face_b)
    left_b, right_b = edges_of(c0, face_b, face_c)
    carry = (flux_of(right_a, left_b, 2), right_b, face_c, c0, c1, c2)
    zeros = [jnp.zeros((8, LANES), jnp.float32) for _ in range(5)]
    half = blocks // 2

    def step(h, state):
        return block(h, state[0], lambda sub: row(4 * h + sub + 3), state[1])

    carry, packed = lax.fori_loop(0, half, step, (carry, (zeros, zeros)))
    for k in range(5):
        edge_ref[0, 0, k] = packed[0][k]
        edge_ref[1, 0, k] = packed[1][k]
    carry, packed = lax.fori_loop(half, blocks - 1, step, (carry, (zeros, zeros)))

    def last(sub):
        return row(rows_y - 1) if sub == 0 else high(sub - 1)

    carry, packed = block(blocks - 1, carry, last, packed)
    for k in range(5):
        edge_ref[0, 1, k] = packed[0][k]
        edge_ref[1, 1, k] = packed[1][k]


def sweep_y(fluid, low, high, blocks):
    nx, ny, nz = fluid.shape[1:]
    return pl.pallas_call(
        sweep_y_kernel,
        out_shape=(
            jax.ShapeDtypeStruct((blocks, 5, nx * ny // blocks, nz), jnp.float32),
            jax.ShapeDtypeStruct((2, 2, 5, nx, nz), jnp.float32),
        ),
        in_specs=[pl.BlockSpec(memory_space=pltpu.VMEM)] * 3,
        out_specs=(pl.BlockSpec(memory_space=pltpu.VMEM),) * 2,
        compiler_params=pltpu.CompilerParams(vmem_limit_bytes=16 * 1024 * 1024),
        cost_estimate=pl.CostEstimate(
            flops=20_000_000, bytes_accessed=2_700_000, transcendentals=0
        ),
        name="sweep_y",
    )(fluid.reshape(5, nx * ny, nz), low, high)


def sweep_z_kernel(lines_ref, out_ref):
    tiles = lines_ref.shape[0]
    lane = lax.broadcasted_iota(jnp.int32, (8, LANES), 1)
    memo = {}

    def once(fn):
        def cached(t):
            key = (fn.__name__, t % tiles)
            if key not in memo:
                memo[key] = fn(t % tiles)
            return memo[key]

        return cached

    @once
    def cell(t):
        return [lines_ref[t, k] for k in range(5)]

    @once
    def after(t):
        return lane_after(cell(t), cell(t + 1), lane)

    @once
    def face(t):
        second = [
            pltpu.roll(jnp.where(lane < 2, f, h), LANES - 2, 1)
            for h, f in zip(cell(t), cell(t + 1))
        ]
        return face_of(lane_before(cell(t), cell(t - 1), lane), cell(t), after(t), second)

    @once
    def edges(t):
        return edges_of(cell(t), lane_before(face(t), face(t - 1), lane), face(t))

    @once
    def flux(t):
        return flux_of(edges(t)[1], lane_after(edges(t)[0], edges(t + 1)[0], lane), 3)

    for t in range(tiles):
        new = updated(cell(t), lane_before(flux(t), flux(t - 1), lane), flux(t))
        for k in range(5):
            for half in range(2):
                out_ref[k, half, :, t * LANES : (t + 1) * LANES] = new[k][4 * half : 4 * half + 4]


def sweep_z(lines, nx):
    tiles, _, rows, _ = lines.shape
    sub = rows // nx
    return pl.pallas_call(
        sweep_z_kernel,
        grid=(rows // 8,),
        out_shape=jax.ShapeDtypeStruct((5, nx, sub, tiles * LANES), jnp.float32),
        in_specs=[pl.BlockSpec((tiles, 5, 8, LANES), lambda q: (0, 0, q, 0))],
        out_specs=pl.BlockSpec((5, 2, sub, tiles * LANES), lambda q: (0, q, 0, 0)),
        compiler_params=pltpu.CompilerParams(vmem_limit_bytes=16 * 1024 * 1024),
        cost_estimate=pl.CostEstimate(
            flops=20_000_000, bytes_accessed=2_700_000, transcendentals=0
        ),
        name="sweep_z",
    )(lines)


def tracers_kernel(owner_ref, count_ref, middle_ref, low_ref, high_ref, cell_ref, peak_ref,
                   out_ref, press_ref):
    blocks, _, rows, _ = middle_ref.shape
    lane = lax.broadcasted_iota(jnp.int32, (8, LANES), 1)

    def owner_rows(h, _):
        for sub in range(4):
            spot = 4 * (h * 4 + sub)
            part = spot // LANES
            spot = spot % LANES
            here = [middle_ref[h, k, pl.ds(sub, 8, stride=4), :] for k in range(5)]
            prev = [pltpu.roll(low_ref[part, k], (2 * LANES - 4 - spot) % LANES, 1) for k in range(5)]
            foll = [pltpu.roll(high_ref[part, k], (LANES - spot) % LANES, 1) for k in range(5)]
            second = [
                pltpu.roll(jnp.where(lane < 2, f, c), LANES - 2, 1) for c, f in zip(here, foll)
            ]
            after = lane_after(here, foll, lane)
            face = face_of(lane_before(here, prev, lane), here, after, second)
            face_prev = face_of(
                [pltpu.roll(c, 1, 1) for c in prev],
                prev,
                lane_after(prev, here, lane),
                [pltpu.roll(jnp.where(lane < 2, c, p), LANES - 2, 1) for p, c in zip(prev, here)],
            )
            face_foll = face_of(
                lane_before(foll, here, lane),
                foll,
                [pltpu.roll(c, LANES - 1, 1) for c in foll],
                [pltpu.roll(c, LANES - 2, 1) for c in foll],
            )
            left, right = edges_of(here, lane_before(face, face_prev, lane), face)
            _, right_prev = edges_of(
                prev, [pltpu.roll(c, 1, 1) for c in face_prev], face_prev
            )
            left_foll, _ = edges_of(foll, lane_before(face_foll, face, lane), face_foll)
            flux = flux_of(right, lane_after(left, left_foll, lane), 3)
            flux_prev = flux_of(right_prev, lane_after(right_prev, left, lane), 3)
            new = updated(here, lane_before(flux, flux_prev, lane), flux)
            press_ref[h, pl.ds(sub, 8, stride=4), :] = new[4]
        return 0

    lax.fori_loop(0, blocks, owner_rows, 0)
    row_ids = lax.broadcasted_iota(jnp.int32, (rows, LANES), 0)
    lane_row = lax.broadcasted_iota(jnp.int32, (1, LANES), 1)
    for j in range(blocks):
        cells = cell_ref[j : j + 1, :]
        table = press_ref[owner_ref[j]]
        z_ids = jnp.broadcast_to(cells % LANES, (rows, LANES))
        picked = jnp.take_along_axis(table, z_ids, axis=1, mode="promise_in_bounds")
        chosen = jnp.broadcast_to(cells // LANES, (rows, LANES)) == row_ids
        sampled = jnp.sum(jnp.where(chosen, picked, 0.0), axis=0, keepdims=True)
        raised = jnp.maximum(peak_ref[j : j + 1, :], sampled)
        out_ref[j : j + 1, :] = jnp.where(lane_row < count_ref[j], raised, 0.0)


def tracers(middle, low, high, owner, count, cells, peaks):
    blocks, _, rows, _ = middle.shape
    return pl.pallas_call(
        tracers_kernel,
        out_shape=jax.ShapeDtypeStruct(peaks.shape, jnp.float32),
        in_specs=[pl.BlockSpec(memory_space=pltpu.SMEM)] * 2
        + [pl.BlockSpec(memory_space=pltpu.VMEM)] * 5,
        out_specs=pl.BlockSpec(memory_space=pltpu.VMEM),
        scratch_shapes=[pltpu.VMEM((blocks, rows, LANES), jnp.float32)],
        compiler_params=pltpu.CompilerParams(vmem_limit_bytes=16 * 1024 * 1024),
        cost_estimate=pl.CostEstimate(
            flops=60_000_000, bytes_accessed=1_400_000, transcendentals=0
        ),
        name="tracers",
    )(owner, count, middle, low, high, cells, peaks)


def shifted(values, axis, step):
    count = lax.axis_size(axis)
    return lax.ppermute(values, axis, [(i, (i + step) % count) for i in range(count)])


def on_device(fluid_state, tracer_cell, tracer_owner, tracer_count, tracer_peak):
    nx, ny = fluid_state.shape[1:3]
    blocks = lax.axis_size("gz")
    head = jnp.transpose(fluid_state[:, :, :3], (2, 0, 1, 3))
    tail = jnp.transpose(fluid_state[:, :, ny - 3 :], (2, 0, 1, 3))
    low = shifted(tail, "gy", 1)
    high = shifted(head, "gy", -1)
    middle, edge = sweep_y(fluid_state, low, high, blocks)
    lines = lax.all_to_all(middle, "gz", split_axis=0, concat_axis=0, tiled=True)
    z_high = shifted(edge[0], "gz", -1)
    z_low = shifted(edge[1], "gz", 1)
    new_peak = tracers(
        middle, z_low, z_high, tracer_owner[0, 0], tracer_count[0, 0], tracer_cell[0, 0],
        tracer_peak[0, 0],
    )
    new_state = sweep_z(lines, nx)
    return (new_state, new_peak[None, None])


def solution(mesh):
    in_specs = (
        P(None, None, "gy", "gz"),
        P("gy", "gz", None, None),
        P("gy", "gz", None),
        P("gy", "gz", None),
        P("gy", "gz", None, None),
    )
    out_specs = (P(None, None, ("gy", "gz"), None), P("gy", "gz", None, None))
    return jax.shard_map(
        on_device, mesh=mesh, in_specs=in_specs, out_specs=out_specs, check_vma=False
    )
```

time: 227 us -> 114 us (0.50)
  local copies, waits for them, and re-layouts: 48.6 us -> 2.38 us
  waiting for transfers between devices: 83.8 us -> 54.3 us
  Pallas kernels: 0 us -> 25.8 us
  other arithmetic: 22.4 us -> 0 us
  starting transfers between devices: 44.7 us -> 30.1 us
  matrix products: 13.3 us -> 0 us
  loops' own time: 11.4 us -> 0 us
    all_to_all x4 -> x1, waiting for transfers between devices: 83.8 us -> 0.01 us  [on_device(): lax.all_to_all(middle, 'gz', split_axis=0, concat_axis=0, tiled=True)]
    ppermute x2 -> x4, waiting for transfers between devices: 0.01 us -> 54.3 us  [shifted(): lax.ppermute(values, axis, [(i, (i + step) % count) for i in range(count)])]
    pallas_call x0 -> x3, Pallas kernels: none -> 25.8 us  [the longest x1 12.8 us: tracers(): pl.pallas_call(tracers_kernel, out_shape=jax.ShapeDtypeStruct(peaks.shape...]
    all_to_all x4 -> x1, starting transfers between devices: 37 us -> 15.3 us  [on_device(): lax.all_to_all(middle, 'gz', split_axis=0, concat_axis=0, tiled=True)]
    dynamic_update_slice x16 -> x0, local copies, waits for them, and re-layouts: 20.8 us -> none  [on_device(): lifted = lax.map(one_source, (got_cells, got_peaks, sources))]
    dot_general x18 -> x0, matrix products: 13.3 us -> none  [the longest x16 11.7 us: sample_rows(): lax.dot_general(pick_z, flat_press, (((1,), (1,)), ((), ())), precision=l...]
    another operation x1 -> x0, loops' own time: 11.4 us -> none  [on_device(): lifted = lax.map(one_source, (got_cells, got_peaks, sources))]
    dynamic_slice x16 -> x0, local copies, waits for them, and re-layouts: 10.7 us -> none  [on_device(): lifted = lax.map(one_source, (got_cells, got_peaks, sources))]
  transfers between devices with their start and end apart: 6 -> 5, of which waited for: 3 -> 2; matrix products, arithmetic and copies ran while one was open for 12% -> 0% of each run, Pallas kernels for 0% -> 11%
where the time goes in v1:
time: 114 us; the launch traced here: 113 us
  waiting for transfers between devices  54.3 us (48%)
  starting transfers between devices  30.1 us (26%)
  Pallas kernels  25.8 us (23%)
  local copies, waits for them, and re-layouts  2.38 us (2%)
    ppermute x4, waiting for transfers between devices, shifted(): lax.ppermute(values, axis, [(i, (i + step) % count) for i in range(count)])  54.3 us
    all_to_all x1, starting transfers between devices, on_device(): lax.all_to_all(middle, 'gz', split_axis=0, concat_axis=0, tiled=True)  15.3 us
    ppermute x4, starting transfers between devices, shifted(): lax.ppermute(values, axis, [(i, (i + step) % count) for i in range(count)])  14.7 us
    pallas_call x1, Pallas kernels, tracers(): pl.pallas_call(tracers_kernel, out_shape=jax.ShapeDtypeStruct(peaks.shape...  12.8 us
    pallas_call x1, Pallas kernels, sweep_z(): pl.pallas_call(sweep_z_kernel, grid=(rows // 8,), out_shape=jax.ShapeDtyp...  8.12 us
    pallas_call x1, Pallas kernels, sweep_y(): pl.pallas_call(sweep_y_kernel, out_shape=(jax.ShapeDtypeStruct((blocks, 5...  4.88 us
  transfers between devices with their start and end apart: 5, of which 2 were waited for; matrix products, arithmetic and copies ran while one was open for 0% of the time, Pallas kernels for 11%

profile of v1, /device:TPU:24, one launch (start us, length us, event | category | flops | bytes accessed | tf_op | source)
XLA Modules:
  0.0 113.3 jit_solution(9467762954640656691)
XLA Ops:
  0.6 1.0 fusion
  1.7 1.9 %collective-permute-start = (f32[3,5,8,128]{3,2,1,0:T(8,128)S(1)}, f32[3,5,8,128]{3,2,1,0:T(8,128)S(1)}, u32[]{:S(2)}, u32[]{:S(2)}) collective-permute-start(f32[3,5,8,128]{3,2,1,0:T(8,128)S(1)} %bitcast.21), channel_id=1, source_target_pairs={{0,16},{16,32},{32,48},{48,64},{64,80},{80,96},{96,112},{112,128},... | collective-permute-start | bytes 184328 | tf_op jit(solution)/shard_map/ppermute | solution.py:307
  3.6 5.8 %collective-permute-start.1 = (f32[3,5,8,128]{3,2,1,0:T(8,128)S(1)}, f32[3,5,8,128]{3,2,1,0:T(8,128)S(1)}, u32[]{:S(2)}, u32[]{:S(2)}) collective-permute-start(f32[3,5,8,128]{3,2,1,0:T(8,128)S(1)} %bitcast.22), channel_id=1, source_target_pairs={{0,496},{16,0},{32,16},{48,32},{64,48},{80,64},{96,80},{112,96},{1... | collective-permute-start | bytes 184328 | tf_op jit(solution)/shard_map/ppermute | solution.py:307
  9.4 0.0 collective-permute-done.low_ref
  9.4 1.8 %collective-permute-done.1.high_ref = f32[3,5,8,128]{3,2,1,0:T(8,128)S(1)} collective-permute-done((f32[3,5,8,128]{3,2,1,0:T(8,128)S(1)}, f32[3,5,8,128]{3,2,1,0:T(8,128)S(1)}, u32[]{:S(2)}, u32[]{:S(2)}) %collective-permute-start.1) | collective-permute-done | bytes 61472 | tf_op jit(solution)/shard_map/ppermute | solution.py:307
  11.2 0.0 copy-start
  11.2 1.3 %copy-done = f32[5,8,64,128]{3,2,1,0:T(8,128)S(1)} copy-done((f32[5,8,64,128]{3,2,1,0:T(8,128)S(1)}, f32[5,8,64,128]{3,2,1,0:T(8,128)}, u32[]{:S(2)}) %copy-start) | copy-done | bytes 1310744
  12.5 4.9 %sweep_y.1 = (f32[16,5,32,128]{3,2,1,0:T(8,128)}, f32[2,2,5,8,128]{4,3,2,1,0:T(8,128)S(1)}) custom-call(f32[5,512,128]{2,1,0:T(8,128)S(1)} %bitcast.16, f32[3,5,8,128]{3,2,1,0:T(8,128)S(1)} %collective-permute-done.low_ref, f32[3,5,8,128]{3,2,1,0:T(8,128)S(1)} %collective-permute-done.1.high_ref), custom_call_target="tpu_custom_call" | custom-call | flops 20000000 | bytes 2700000 | tf_op jit(solution)/shard_map/sweep_y/pallas_call | solution.py:155
  17.4 0.0 copy-start.1
  17.4 0.0 copy-start.2
  17.4 0.0 copy-start.3
  17.4 0.0 copy-start.4
  17.4 15.3 %all-to-all-start = ((f32[16,5,32,128]{3,2,1,0:T(8,128)}), f32[16,5,32,128]{3,2,1,0:T(8,128)S(1)}, u32[]{:S(2)}, u32[]{:S(2)}) async-start(f32[16,5,32,128]{3,2,1,0:T(8,128)} %get-tuple-element.4.middle_ref), calls=%async_computation | async-start | bytes 2621440 | tf_op jit(solution)/shard_map/all_to_all | solution.py:318
  32.8 3.8 %collective-permute-start.2 = (f32[2,5,8,128]{3,2,1,0:T(8,128)S(1)}, f32[2,5,8,128]{3,2,1,0:T(8,128)S(1)}, u32[]{:S(2)}, u32[]{:S(2)}) collective-permute-start(f32[2,5,8,128]{3,2,1,0:T(8,128)S(1)} %get-tuple-element.9), channel_id=1, source_target_pairs={{0,1},{1,2},{2,3},{3,4},{4,5},{5,6},{6,7},{7,8},{8,9},{9,10},{10,1... | collective-permute-start | bytes 122888 | tf_op jit(solution)/shard_map/ppermute | solution.py:307
  36.6 3.2 %collective-permute-start.3 = (f32[2,5,8,128]{3,2,1,0:T(8,128)S(1)}, f32[2,5,8,128]{3,2,1,0:T(8,128)S(1)}, u32[]{:S(2)}, u32[]{:S(2)}) collective-permute-start(f32[2,5,8,128]{3,2,1,0:T(8,128)S(1)} %get-tuple-element.8), channel_id=1, source_target_pairs={{0,15},{1,0},{2,1},{3,2},{4,3},{5,4},{6,5},{7,6},{8,7},{9,8},{10,9... | collective-permute-start | bytes 122888 | tf_op jit(solution)/shard_map/ppermute | solution.py:307
  39.9 52.5 %collective-permute-done.2.low_ref = f32[2,5,8,128]{3,2,1,0:T(8,128)S(1)} collective-permute-done((f32[2,5,8,128]{3,2,1,0:T(8,128)S(1)}, f32[2,5,8,128]{3,2,1,0:T(8,128)S(1)}, u32[]{:S(2)}, u32[]{:S(2)}) %collective-permute-start.2) | collective-permute-done | bytes 40992 | tf_op jit(solution)/shard_map/ppermute | solution.py:307
  92.4 0.0 collective-permute-done.3.high_ref
  92.4 0.0 copy-done.1
  92.4 0.0 copy-done.2
  92.4 0.0 copy-done.3
  92.4 0.0 copy-done.4
  92.4 12.8 %tracers.1 = f32[16,128]{1,0:T(8,128)} custom-call(s32[16]{0:T(128)S(1)} %bitcast.19, s32[16]{0:T(128)S(1)} %bitcast.20, f32[16,5,32,128]{3,2,1,0:T(8,128)} %get-tuple-element.4.middle_ref, f32[2,5,8,128]{3,2,1,0:T(8,128)S(1)} %collective-permute-done.2.low_ref, f32[2,5,8,128]{3,2,1,0:T(8,128)S(1)} %collective-permute-done.3.high_ref, ...), custom_call_target="tpu_custom_call" | custom-call | flops 60000000 | bytes 1400000 | tf_op jit(solution)/shard_map/tracers/pallas_call | solution.py:290
  105.2 0.0 all-to-all-done.lines_ref
  105.2 8.1 %sweep_z.1 = f32[5,8,4,2048]{3,2,1,0:T(4,128)} custom-call(f32[16,5,32,128]{3,2,1,0:T(8,128)S(1)} %all-to-all-done.lines_ref), custom_call_target="tpu_custom_call" | custom-call | flops 20000000 | bytes 2700000 | tf_op jit(solution)/shard_map/sweep_z/pallas_call | solution.py:219
  (3 shorter events, 0.0 us)
Async XLA Ops:
  1.7 7.7 %collective-permute-start = (f32[3,5,8,128]{3,2,1,0:T(8,128)S(1)}, f32[3,5,8,128]{3,2,1,0:T(8,128)S(1)}, u32[]{:S(2)}, u32[]{:S(2)}) collective-permute-start(f32[3,5,8,128]{3,2,1,0:T(8,128)S(1)} %bitcast.21), channel_id=1, source_target_pairs={{0,16},{16,32},{32,48},{48,64},{64,80},{80,96},{96,112},{112,128},... | collective-permute-start | bytes 184328 | tf_op jit(solution)/shard_map/ppermute | solution.py:307
  3.6 7.6 %collective-permute-start.1 = (f32[3,5,8,128]{3,2,1,0:T(8,128)S(1)}, f32[3,5,8,128]{3,2,1,0:T(8,128)S(1)}, u32[]{:S(2)}, u32[]{:S(2)}) collective-permute-start(f32[3,5,8,128]{3,2,1,0:T(8,128)S(1)} %bitcast.22), channel_id=1, source_target_pairs={{0,496},{16,0},{32,16},{48,32},{64,48},{80,64},{96,80},{112,96},{1... | collective-permute-start | bytes 184328 | tf_op jit(solution)/shard_map/ppermute | solution.py:307
  11.2 1.3 %copy-start = (f32[5,8,64,128]{3,2,1,0:T(8,128)S(1)}, f32[5,8,64,128]{3,2,1,0:T(8,128)}, u32[]{:S(2)}) copy-start(f32[5,8,64,128]{3,2,1,0:T(8,128)} %param.5) | copy-start | bytes 3932164
  17.4 74.9 %copy-start.1 = (s32[1,1,16,128]{3,2,1,0:T(8,128)S(1)}, s32[1,1,16,128]{3,2,1,0:T(8,128)}, u32[]{:S(2)}) copy-start(s32[1,1,16,128]{3,2,1,0:T(8,128)} %param.6) | copy-start | bytes 24580
  17.4 74.9 %copy-start.2 = (f32[1,1,16,128]{3,2,1,0:T(8,128)S(1)}, f32[1,1,16,128]{3,2,1,0:T(8,128)}, u32[]{:S(2)}) copy-start(f32[1,1,16,128]{3,2,1,0:T(8,128)} %param.9) | copy-start | bytes 24580
  17.4 74.9 %copy-start.3 = (s32[1,1,16]{2,1,0:T(1,128)S(1)}, s32[1,1,16]{2,1,0:T(1,128)}, u32[]{:S(2)}) copy-start(s32[1,1,16]{2,1,0:T(1,128)} %param.7) | copy-start | bytes 196
  17.4 75.0 %copy-start.4 = (s32[1,1,16]{2,1,0:T(1,128)S(1)}, s32[1,1,16]{2,1,0:T(1,128)}, u32[]{:S(2)}) copy-start(s32[1,1,16]{2,1,0:T(1,128)} %param.8) | copy-start | bytes 196
  17.4 87.7 %all-to-all-start = ((f32[16,5,32,128]{3,2,1,0:T(8,128)}), f32[16,5,32,128]{3,2,1,0:T(8,128)S(1)}, u32[]{:S(2)}, u32[]{:S(2)}) async-start(f32[16,5,32,128]{3,2,1,0:T(8,128)} %get-tuple-element.4.middle_ref), calls=%async_computation | async-start | bytes 2621440 | tf_op jit(solution)/shard_map/all_to_all | solution.py:318
  32.8 59.6 %collective-permute-start.2 = (f32[2,5,8,128]{3,2,1,0:T(8,128)S(1)}, f32[2,5,8,128]{3,2,1,0:T(8,128)S(1)}, u32[]{:S(2)}, u32[]{:S(2)}) collective-permute-start(f32[2,5,8,128]{3,2,1,0:T(8,128)S(1)} %get-tuple-element.9), channel_id=1, source_target_pairs={{0,1},{1,2},{2,3},{3,4},{4,5},{5,6},{6,7},{7,8},{8,9},{9,10},{10,1... | collective-permute-start | bytes 122888 | tf_op jit(solution)/shard_map/ppermute | solution.py:307
  36.6 55.7 %collective-permute-start.3 = (f32[2,5,8,128]{3,2,1,0:T(8,128)S(1)}, f32[2,5,8,128]{3,2,1,0:T(8,128)S(1)}, u32[]{:S(2)}, u32[]{:S(2)}) collective-permute-start(f32[2,5,8,128]{3,2,1,0:T(8,128)S(1)} %get-tuple-element.8), channel_id=1, source_target_pairs={{0,15},{1,0},{2,1},{3,2},{4,3},{5,4},{6,5},{7,6},{8,7},{9,8},{10,9... | collective-permute-start | bytes 122888 | tf_op jit(solution)/shard_map/ppermute | solution.py:307

commit v2 on v1

v2 whole, which is shorter than its diff:
```python
import jax
import jax.numpy as jnp
from jax import lax
from jax.experimental import pallas as pl
from jax.experimental.pallas import tpu as pltpu
from jax.sharding import PartitionSpec as P

GAMMA = 1.4
RATIO = 0.06
LANES = 128


def median_of(first, second, third):
    return jnp.maximum(jnp.minimum(first, second), jnp.minimum(jnp.maximum(first, second), third))


def face_of(before, left, right, after):
    out = []
    for b, l, r, a in zip(before, left, right, after):
        mid = (7.0 / 12.0) * (l + r) - (1.0 / 12.0) * (b + a)
        out.append(jnp.minimum(jnp.maximum(mid, jnp.minimum(l, r)), jnp.maximum(l, r)))
    return out


def edges_of(centre, face_left, face_right):
    left, right = [], []
    for a, fl, fr in zip(centre, face_left, face_right):
        triple = 3.0 * a
        left.append(median_of(a, fl, triple - 2.0 * fr))
        right.append(median_of(a, fr, triple - 2.0 * fl))
    return left, right


def inverse(value):
    return pl.reciprocal(value, approx=True)


def sound(rho, p):
    heat = GAMMA * p
    return heat * lax.rsqrt(jnp.maximum(heat * rho, 1e-30))


def flux_of(left, right, normal):
    rho_l, p_l, u_l = left[0], left[4], left[normal]
    rho_r, p_r, u_r = right[0], right[4], right[normal]
    c_l = sound(rho_l, p_l)
    c_r = sound(rho_r, p_r)
    slow = jnp.minimum(jnp.minimum(u_l - c_l, u_r - c_r), 0.0)
    fast = jnp.maximum(jnp.maximum(u_l + c_l, u_r + c_r), 0.0)
    scale = RATIO * inverse(fast - slow)
    a_l = fast * scale
    a_r = slow * scale
    w_l = a_l * (u_l - slow)
    w_r = a_r * (u_r - fast)
    q_l = rho_l * w_l
    q_r = rho_r * w_r
    flux = [q_l - q_r] + [q_l * left[k] - q_r * right[k] for k in (1, 2, 3)]
    push_l = a_l * p_l
    push_r = a_r * p_r
    flux[normal] = flux[normal] + (push_l - push_r)
    square_l = left[1] * left[1] + left[2] * left[2] + left[3] * left[3]
    square_r = right[1] * right[1] + right[2] * right[2] + right[3] * right[3]
    flux.append(
        0.2 * (q_l * square_l - q_r * square_r)
        + 0.4 * (push_l * u_l - push_r * u_r)
        + (p_l * w_l - p_r * w_r)
    )
    return flux


def updated(state, flux_left, flux_right):
    rho, vx, vy, vz, p = state
    change = [r - l for l, r in zip(flux_left, flux_right)]
    mom = [rho * v for v in (vx, vy, vz)]
    twice = mom[0] * vx + mom[1] * vy + mom[2] * vz
    rho_new = rho - change[0]
    mom_new = [m - d for m, d in zip(mom, change[1:4])]
    inv = inverse(rho_new)
    vel = [m * inv for m in mom_new]
    twice_new = mom_new[0] * vel[0] + mom_new[1] * vel[1] + mom_new[2] * vel[2]
    return [rho_new] + vel + [p - change[4] + 0.2 * (twice - twice_new)]


def lane_after(here, following, lane):
    return [
        pltpu.roll(jnp.where(lane == 0, f, h), LANES - 1, 1) for h, f in zip(here, following)
    ]


def lane_before(here, previous, lane):
    return [
        pltpu.roll(jnp.where(lane == LANES - 1, p, h), 1, 1) for h, p in zip(here, previous)
    ]


def sweep_y_kernel(fluid_ref, low_ref, high_ref, middle_ref, cells_ref, new_ref, in_sem, out_sem):
    nx, rows_y = fluid_ref.shape[1:3]
    blocks = middle_ref.shape[0]
    chunks = 4
    depth = rows_y // chunks
    copies = []
    for c in range(chunks):
        part = pl.ds(c * depth, depth)
        copies.append(
            pltpu.make_async_copy(
                fluid_ref.at[:, :, part, :], cells_ref.at[:, :, part, :], in_sem.at[c]
            )
        )
        copies[c].start()
    flat_ref = cells_ref.reshape(5, nx * rows_y, LANES)

    def row(y):
        return [flat_ref[k, pl.ds(y, nx, stride=rows_y), :] for k in range(5)]

    def low(i):
        return [low_ref[i, k] for k in range(5)]

    def high(i):
        return [high_ref[i, k] for k in range(5)]

    def block(h, carry, load):
        flux, right, face, c0, c1, c2 = carry
        for sub in range(4):
            c3 = load(sub)
            face_next = face_of(c0, c1, c2, c3)
            left_next, right_next = edges_of(c1, face, face_next)
            flux_next = flux_of(right, left_next, 2)
            new = updated(c0, flux, flux_next)
            for k in range(5):
                new_ref[h, k, pl.ds(sub, 8, stride=4), :] = new[k]
            flux, right, face, c0, c1, c2 = flux_next, right_next, face_next, c1, c2, c3
        return flux, right, face, c0, c1, c2

    def step(h, carry):
        return block(h, carry, lambda sub: row(4 * h + sub + 3))

    def send(i, first, count):
        part = pl.ds(first, count)
        copy = pltpu.make_async_copy(new_ref.at[part], middle_ref.at[part], out_sem.at[i])
        copy.start()
        return copy

    copies[0].wait()
    m3, m2, m1 = low(0), low(1), low(2)
    c0, c1, c2 = row(0), row(1), row(2)
    face_a = face_of(m3, m2, m1, c0)
    face_b = face_of(m2, m1, c0, c1)
    face_c = face_of(m1, c0, c1, c2)
    _, right_a = edges_of(m1, face_a, face_b)
    left_b, right_b = edges_of(c0, face_b, face_c)
    carry = (flux_of(right_a, left_b, 2), right_b, face_c, c0, c1, c2)
    first = 0
    sent = []
    for c in range(chunks):
        until = (c + 1) * blocks // chunks - 1
        carry = lax.fori_loop(first, until, step, carry)
        sent.append(send(c, first, until - first))
        first = until
        if c + 1 < chunks:
            copies[c + 1].wait()

    def last(sub):
        return row(rows_y - 1) if sub == 0 else high(sub - 1)

    block(blocks - 1, carry, last)
    sent.append(send(chunks, blocks - 1, 1))
    for copy in sent:
        copy.wait()


def sweep_y(fluid, low, high, blocks):
    nx, ny, nz = fluid.shape[1:]
    rows = nx * ny // blocks
    return pl.pallas_call(
        sweep_y_kernel,
        out_shape=jax.ShapeDtypeStruct((blocks, 5, rows, nz), jnp.float32),
        in_specs=[pl.BlockSpec(memory_space=pl.ANY)] + [pl.BlockSpec(memory_space=pltpu.VMEM)] * 2,
        out_specs=pl.BlockSpec(memory_space=pl.ANY),
        scratch_shapes=[
            pltpu.VMEM((5, nx, ny, nz), jnp.float32),
            pltpu.VMEM((blocks, 5, rows, nz), jnp.float32),
            pltpu.SemaphoreType.DMA((4,)),
            pltpu.SemaphoreType.DMA((5,)),
        ],
        compiler_params=pltpu.CompilerParams(vmem_limit_bytes=16 * 1024 * 1024),
        cost_estimate=pl.CostEstimate(
            flops=20_000_000, bytes_accessed=2_700_000, transcendentals=0
        ),
        name="sweep_y",
    )(fluid, low, high)


def sweep_z_kernel(lines_ref, out_ref, face_ref, left_ref, right_ref, flux_ref):
    tiles = lines_ref.shape[0]
    lane = lax.broadcasted_iota(jnp.int32, (8, LANES), 1)

    spot = pl.multiple_of(pl.program_id(0) * 8, 8)

    def get(ref, t):
        if ref is lines_ref:
            return [ref[t % tiles, k, pl.ds(spot, 8), :] for k in range(5)]
        return [ref[t % tiles, k] for k in range(5)]

    def put(ref, t, values):
        for k in range(5):
            ref[t, k] = values[k]

    for t in range(tiles):
        before, here, following = [get(lines_ref, t + d) for d in (-1, 0, 1)]
        second = [
            pltpu.roll(jnp.where(lane < 2, f, h), LANES - 2, 1) for h, f in zip(here, following)
        ]
        put(face_ref, t, face_of(
            lane_before(here, before, lane), here, lane_after(here, following, lane), second
        ))
    for t in range(tiles):
        face = get(face_ref, t)
        left, right = edges_of(
            get(lines_ref, t), lane_before(face, get(face_ref, t - 1), lane), face
        )
        put(left_ref, t, left)
        put(right_ref, t, right)
    for t in range(tiles):
        follow = lane_after(get(left_ref, t), get(left_ref, t + 1), lane)
        put(flux_ref, t, flux_of(get(right_ref, t), follow, 3))
    for t in range(tiles):
        flux = get(flux_ref, t)
        new = updated(get(lines_ref, t), lane_before(flux, get(flux_ref, t - 1), lane), flux)
        for k in range(5):
            for half in range(2):
                out_ref[k, half, :, t * LANES : (t + 1) * LANES] = new[k][4 * half : 4 * half + 4]


def sweep_z(lines, nx):
    tiles, _, rows, _ = lines.shape
    sub = rows // nx
    return pl.pallas_call(
        sweep_z_kernel,
        grid=(rows // 8,),
        out_shape=jax.ShapeDtypeStruct((5, nx, sub, tiles * LANES), jnp.float32),
        in_specs=[pl.BlockSpec(memory_space=pltpu.VMEM)],
        out_specs=pl.BlockSpec((5, 2, sub, tiles * LANES), lambda q: (0, q, 0, 0)),
        scratch_shapes=[pltpu.VMEM((tiles, 5, 8, LANES), jnp.float32)] * 4,
        compiler_params=pltpu.CompilerParams(vmem_limit_bytes=16 * 1024 * 1024),
        cost_estimate=pl.CostEstimate(
            flops=20_000_000, bytes_accessed=2_700_000, transcendentals=0
        ),
        name="sweep_z",
    )(lines)


def lines_of(states):
    def after(values):
        return [pltpu.roll(v, LANES - 1, 1) for v in values]

    def before(values):
        return [pltpu.roll(v, 1, 1) for v in values]

    nexts = [after(s) for s in states]
    faces = [face_of(before(s), s, n, after(n)) for s, n in zip(states, nexts)]
    edges = [edges_of(s, before(f), f) for s, f in zip(states, faces)]
    fluxes = [flux_of(right, after(left), 3) for left, right in edges]
    return [updated(s, before(f), f) for s, f in zip(states, fluxes)]


def inner_kernel(owner_ref, middle_ref, cell_ref, sample_ref, edge_ref, low_ref, high_ref, press_ref):
    blocks, _, rows, _ = middle_ref.shape
    lane = lax.broadcasted_iota(jnp.int32, (8, LANES), 1)

    def eight(j, _):
        ends = [jnp.zeros((8, LANES), jnp.float32) for _ in range(5)]
        for part in range(2):
            h = 2 * j + part
            states = [
                [middle_ref[h, k, pl.ds(sub, 8, stride=4), :] for k in range(5)] for sub in range(4)
            ]
            for sub, new in enumerate(lines_of(states)):
                press_ref[h, pl.ds(sub, 8, stride=4), :] = new[4]
            for sub, state in enumerate(states):
                g = 4 * part + sub
                ends = [
                    jnp.where(lane // 16 == g, pltpu.roll(v, (16 * g + 8) % LANES, 1), e)
                    for v, e in zip(state, ends)
                ]
        for k in range(5):
            edge_ref[j, k] = ends[k]
        return 0

    lax.fori_loop(0, blocks // 2, eight, 0)
    for part in range(blocks // 8):
        for k in range(5):
            low = edge_ref[4 * part, k]
            high = low
            for r in range(4):
                ends = edge_ref[4 * part + r, k]
                mine = lane % 16 // 4 == r
                low = jnp.where(mine, pltpu.roll(ends, (LANES + 4 * r - 8) % LANES, 1), low)
                high = jnp.where(mine, pltpu.roll(ends, (LANES + 4 * r - 4) % LANES, 1), high)
            low_ref[part, k] = low
            high_ref[part, k] = high
    row_ids = lax.broadcasted_iota(jnp.int32, (rows, LANES), 0)
    for j in range(blocks):
        cells = cell_ref[j : j + 1, :]
        z_ids = jnp.broadcast_to(cells % LANES, (rows, LANES))
        picked = jnp.take_along_axis(
            press_ref[owner_ref[j]], z_ids, axis=1, mode="promise_in_bounds"
        )
        chosen = jnp.broadcast_to(cells // LANES, (rows, LANES)) == row_ids
        sample_ref[j : j + 1, :] = jnp.sum(jnp.where(chosen, picked, 0.0), axis=0, keepdims=True)


def inner_samples(owner, middle, cells):
    blocks, _, rows, _ = middle.shape
    parts = blocks // 8
    return pl.pallas_call(
        inner_kernel,
        out_shape=(
            jax.ShapeDtypeStruct(cells.shape, jnp.float32),
            jax.ShapeDtypeStruct((blocks // 2, 5, 8, LANES), jnp.float32),
            jax.ShapeDtypeStruct((parts, 5, 8, LANES), jnp.float32),
            jax.ShapeDtypeStruct((parts, 5, 8, LANES), jnp.float32),
        ),
        in_specs=[pl.BlockSpec(memory_space=pltpu.SMEM)]
        + [pl.BlockSpec(memory_space=pltpu.VMEM)] * 2,
        out_specs=(pl.BlockSpec(memory_space=pltpu.VMEM),) * 4,
        scratch_shapes=[pltpu.VMEM((blocks, rows, LANES), jnp.float32)],
        compiler_params=pltpu.CompilerParams(vmem_limit_bytes=16 * 1024 * 1024),
        cost_estimate=pl.CostEstimate(
            flops=20_000_000, bytes_accessed=1_600_000, transcendentals=0
        ),
        name="inner_samples",
    )(owner, middle, cells)


def tracers_kernel(owner_ref, count_ref, sample_ref, edge_ref, low_ref, high_ref, cell_ref, peak_ref,
                   out_ref, table_ref):
    blocks = sample_ref.shape[0]
    lane = lax.broadcasted_iota(jnp.int32, (8, LANES), 1)
    upper = lane % 16 < 8
    batch = 8
    for start in range(0, blocks // 2, batch):
        states = []
        for j in range(start, start + batch):
            part, r = j // 4, j % 4
            ends = [edge_ref[j, k] for k in range(5)]
            below = [pltpu.roll(low_ref[part, k], (LANES + 4 - 4 * r) % LANES, 1) for k in range(5)]
            above = [pltpu.roll(high_ref[part, k], (LANES + 8 - 4 * r) % LANES, 1) for k in range(5)]
            states.append([jnp.where(upper, b, e) for b, e in zip(below, ends)])
            states.append([jnp.where(upper, e, a) for a, e in zip(above, ends)])
        new = lines_of(states)
        for i in range(batch):
            table_ref[start + i] = jnp.where(upper, new[2 * i + 1][4], new[2 * i][4])
    planes = lax.broadcasted_iota(jnp.int32, (8, LANES), 0)
    cells = cell_ref[...]
    z_ids = cells % LANES
    outer = (z_ids < 3) | (z_ids >= LANES - 3)
    sampled = []
    for j in range(blocks):
        owner = owner_ref[j]
        ids = 16 * (4 * (owner % 2) + cells[j : j + 1] // LANES % 4) + (z_ids[j : j + 1] + 8) % 16
        ids = jnp.broadcast_to(ids, (8, LANES))
        picked = jnp.take_along_axis(table_ref[owner // 2], ids, axis=1, mode="promise_in_bounds")
        chosen = jnp.broadcast_to(cells[j : j + 1] // (4 * LANES), (8, LANES)) == planes
        sampled.append(jnp.sum(jnp.where(chosen, picked, 0.0), axis=0, keepdims=True))
    sampled = jnp.where(outer, jnp.concatenate(sampled, axis=0), sample_ref[...])
    slot = lax.broadcasted_iota(jnp.int32, (1, LANES), 1)
    raised = jnp.maximum(peak_ref[...], sampled)
    for j in range(blocks):
        out_ref[j : j + 1, :] = jnp.where(slot < count_ref[j], raised[j : j + 1, :], 0.0)


def tracers(owner, count, sample, edge, low, high, cells, peaks):
    blocks = sample.shape[0]
    return pl.pallas_call(
        tracers_kernel,
        out_shape=jax.ShapeDtypeStruct(peaks.shape, jnp.float32),
        in_specs=[pl.BlockSpec(memory_space=pltpu.SMEM)] * 2
        + [pl.BlockSpec(memory_space=pltpu.VMEM)] * 6,
        out_specs=pl.BlockSpec(memory_space=pltpu.VMEM),
        scratch_shapes=[pltpu.VMEM((blocks // 2, 8, LANES), jnp.float32)],
        compiler_params=pltpu.CompilerParams(vmem_limit_bytes=16 * 1024 * 1024),
        cost_estimate=pl.CostEstimate(
            flops=5_000_000, bytes_accessed=800_000, transcendentals=0
        ),
        name="tracers",
    )(owner, count, sample, edge, low, high, cells, peaks)


def shifted(values, axis, step):
    count = lax.axis_size(axis)
    return lax.ppermute(values, axis, [(i, (i + step) % count) for i in range(count)])


def on_device(fluid_state, tracer_cell, tracer_owner, tracer_count, tracer_peak):
    nx, ny = fluid_state.shape[1:3]
    blocks = lax.axis_size("gz")
    head = jnp.transpose(fluid_state[:, :, :3], (2, 0, 1, 3))
    tail = jnp.transpose(fluid_state[:, :, ny - 3 :], (2, 0, 1, 3))
    low = shifted(tail, "gy", 1)
    high = shifted(head, "gy", -1)
    middle = sweep_y(fluid_state, low, high, blocks)
    lines = lax.all_to_all(middle, "gz", split_axis=0, concat_axis=0, tiled=True)
    owner, cells = tracer_owner[0, 0], tracer_cell[0, 0]
    sample, edge, z_head, z_tail = inner_samples(owner, middle, cells)
    above = shifted(z_head, "gz", -1)
    below = shifted(z_tail, "gz", 1)
    new_peak = tracers(
        owner, tracer_count[0, 0], sample, edge, below, above, cells, tracer_peak[0, 0]
    )
    new_state = sweep_z(lines, nx)
    return (new_state, new_peak[None, None])


def solution(mesh):
    in_specs = (
        P(None, None, "gy", "gz"),
        P("gy", "gz", None, None),
        P("gy", "gz", None),
        P("gy", "gz", None),
        P("gy", "gz", None, None),
    )
    out_specs = (P(None, None, ("gy", "gz"), None), P("gy", "gz", None, None))
    return jax.shard_map(
        on_device, mesh=mesh, in_specs=in_specs, out_specs=out_specs, check_vma=False
    )
```

time: 114 us -> 99.4 us (0.87)
  Pallas kernels: 25.8 us -> 15.5 us
  waiting for transfers between devices: 54.3 us -> 50.4 us
    pallas_call x1, Pallas kernels: 12.8 us -> 2.07 us  [tracers(): pl.pallas_call(tracers_kernel, out_shape=jax.ShapeDtypeStruct(peaks.shape...]
    ppermute x4, waiting for transfers between devices: 54.3 us -> 48.5 us  [shifted(): lax.ppermute(values, axis, [(i, (i + step) % count) for i in range(count)])]
    pallas_call x1 -> x2, Pallas kernels: 4.88 us -> 9.36 us  [the longest x1 5.83 us: inner_samples(): pl.pallas_call(inner_kernel, out_shape=(jax.ShapeDtypeStruct(cells.shape,...]
    pallas_call x1, Pallas kernels: 8.12 us -> 4.07 us  [sweep_z(): pl.pallas_call(sweep_z_kernel, grid=(rows // 8,), out_shape=jax.ShapeDtyp...]
    all_to_all x1, waiting for transfers between devices: 0.01 us -> 1.96 us  [on_device(): lax.all_to_all(middle, 'gz', split_axis=0, concat_axis=0, tiled=True)]
  transfers between devices with their start and end apart: 5 -> 5, of which waited for: 2 -> 3; matrix products, arithmetic and copies ran while one was open for 0% -> 0% of each run, Pallas kernels for 11% -> 8%
where the time goes in v2:
time: 99.4 us; the launch traced here: 99 us
  waiting for transfers between devices  50.4 us (51%)
  starting transfers between devices  29.9 us (30%)
  Pallas kernels  15.5 us (16%)
  local copies, waits for them, and re-layouts  2.38 us (2%)
    ppermute x4, waiting for transfers between devices, shifted(): lax.ppermute(values, axis, [(i, (i + step) % count) for i in range(count)])  48.5 us
    all_to_all x1, starting transfers between devices, on_device(): lax.all_to_all(middle, 'gz', split_axis=0, concat_axis=0, tiled=True)  15.2 us
    ppermute x4, starting transfers between devices, shifted(): lax.ppermute(values, axis, [(i, (i + step) % count) for i in range(count)])  14.7 us
    pallas_call x1, Pallas kernels, inner_samples(): pl.pallas_call(inner_kernel, out_shape=(jax.ShapeDtypeStruct(cells.shape,...  5.83 us
    pallas_call x1, Pallas kernels, sweep_z(): pl.pallas_call(sweep_z_kernel, grid=(rows // 8,), out_shape=jax.ShapeDtyp...  4.07 us
    pallas_call x1, Pallas kernels, sweep_y(): pl.pallas_call(sweep_y_kernel, out_shape=jax.ShapeDtypeStruct((blocks, 5,...  3.53 us
    pallas_call x1, Pallas kernels, tracers(): pl.pallas_call(tracers_kernel, out_shape=jax.ShapeDtypeStruct(peaks.shape...  2.07 us
  transfers between devices with their start and end apart: 5, of which 3 were waited for; matrix products, arithmetic and copies ran while one was open for 0% of the time, Pallas kernels for 8%

profile of v2, /device:TPU:24, one launch (start us, length us, event | category | flops | bytes accessed | tf_op | source)
XLA Modules:
  0.0 99.0 jit_solution(12947685954264947380)
XLA Ops:
  0.6 1.0 %fusion = (f32[5,8,3,128]{3,2,1,0:T(4,128)S(1)}, f32[5,8,3,128]{3,2,1,0:T(4,128)S(1)}) fusion(f32[5,8,64,128]{3,2,1,0:T(8,128)} %fluid_ref.1), kind=kLoop, calls=%fused_computation.2 | loop fusion | bytes 245760 | tf_op jit(solution)/shard_map/slice | solution.py:397
  1.7 1.9 %collective-permute-start = (f32[3,5,8,128]{3,2,1,0:T(8,128)S(1)}, f32[3,5,8,128]{3,2,1,0:T(8,128)S(1)}, u32[]{:S(2)}, u32[]{:S(2)}) collective-permute-start(f32[3,5,8,128]{3,2,1,0:T(8,128)S(1)} %bitcast.17), channel_id=1, source_target_pairs={{0,16},{16,32},{32,48},{48,64},{64,80},{80,96},{96,112},{112,128},... | collective-permute-start | bytes 184328 | tf_op jit(solution)/shard_map/ppermute | solution.py:391
  3.6 5.8 %collective-permute-start.1 = (f32[3,5,8,128]{3,2,1,0:T(8,128)S(1)}, f32[3,5,8,128]{3,2,1,0:T(8,128)S(1)}, u32[]{:S(2)}, u32[]{:S(2)}) collective-permute-start(f32[3,5,8,128]{3,2,1,0:T(8,128)S(1)} %bitcast.18), channel_id=1, source_target_pairs={{0,496},{16,0},{32,16},{48,32},{64,48},{80,64},{96,80},{112,96},{1... | collective-permute-start | bytes 184328 | tf_op jit(solution)/shard_map/ppermute | solution.py:391
  9.4 0.0 collective-permute-done.low_ref
  9.4 1.8 %collective-permute-done.1.high_ref = f32[3,5,8,128]{3,2,1,0:T(8,128)S(1)} collective-permute-done((f32[3,5,8,128]{3,2,1,0:T(8,128)S(1)}, f32[3,5,8,128]{3,2,1,0:T(8,128)S(1)}, u32[]{:S(2)}, u32[]{:S(2)}) %collective-permute-start.1) | collective-permute-done | bytes 61472 | tf_op jit(solution)/shard_map/ppermute | solution.py:391
  11.2 0.0 copy-start
  11.2 1.3 %copy-done = f32[5,8,64,128]{3,2,1,0:T(8,128)S(1)} copy-done((f32[5,8,64,128]{3,2,1,0:T(8,128)S(1)}, f32[5,8,64,128]{3,2,1,0:T(8,128)}, u32[]{:S(2)}) %copy-start) | copy-done | bytes 1310744
  12.5 3.5 %sweep_y.1.middle_ref = f32[16,5,32,128]{3,2,1,0:T(8,128)} custom-call(f32[5,8,64,128]{3,2,1,0:T(8,128)S(1)} %copy-done, f32[3,5,8,128]{3,2,1,0:T(8,128)S(1)} %collective-permute-done.low_ref, f32[3,5,8,128]{3,2,1,0:T(8,128)S(1)} %collective-permute-done.1.high_ref), custom_call_target="tpu_custom_call" | custom-call | flops 20000000 | bytes 2700000 | tf_op jit(solution)/shard_map/sweep_y/pallas_call | solution.py:174
  16.1 0.0 copy-start.1
  16.1 0.0 copy-start.3
  16.1 15.2 %all-to-all-start = ((f32[16,5,32,128]{3,2,1,0:T(8,128)}), f32[16,5,32,128]{3,2,1,0:T(8,128)S(1)}, u32[]{:S(2)}, u32[]{:S(2)}) async-start(f32[16,5,32,128]{3,2,1,0:T(8,128)} %sweep_y.1.middle_ref), calls=%async_computation | async-start | bytes 2621440 | tf_op jit(solution)/shard_map/all_to_all | solution.py:402
  31.3 0.0 copy-start.2
  31.3 0.0 copy-start.4
  31.3 0.0 copy-done.1
  31.3 0.0 copy-done.3
  31.4 5.8 %inner_samples.1 = (f32[16,128]{1,0:T(8,128)S(1)}, f32[8,5,8,128]{3,2,1,0:T(8,128)S(1)}, f32[2,5,8,128]{3,2,1,0:T(8,128)S(1)}, f32[2,5,8,128]{3,2,1,0:T(8,128)S(1)}) custom-call(s32[16]{0:T(128)S(1)} %bitcast.14, f32[16,5,32,128]{3,2,1,0:T(8,128)} %sweep_y.1.middle_ref, s32[16,128]{1,0:T(8,128)S(1)} %bitcast.11), custom_call_target="tpu_custom_call" | custom-call | flops 20000000 | bytes 1600000 | tf_op jit(solution)/shard_map/inner_samples/pallas_call | solution.py:315
  37.2 3.8 %collective-permute-start.2 = (f32[2,5,8,128]{3,2,1,0:T(8,128)S(1)}, f32[2,5,8,128]{3,2,1,0:T(8,128)S(1)}, u32[]{:S(2)}, u32[]{:S(2)}) collective-permute-start(f32[2,5,8,128]{3,2,1,0:T(8,128)S(1)} %get-tuple-element.8), channel_id=1, source_target_pairs={{0,1},{1,2},{2,3},{3,4},{4,5},{5,6},{6,7},{7,8},{8,9},{9,10},{10,1... | collective-permute-start | bytes 122888 | tf_op jit(solution)/shard_map/ppermute | solution.py:391
  41.0 3.2 %collective-permute-start.3 = (f32[2,5,8,128]{3,2,1,0:T(8,128)S(1)}, f32[2,5,8,128]{3,2,1,0:T(8,128)S(1)}, u32[]{:S(2)}, u32[]{:S(2)}) collective-permute-start(f32[2,5,8,128]{3,2,1,0:T(8,128)S(1)} %get-tuple-element.9), channel_id=1, source_target_pairs={{0,15},{1,0},{2,1},{3,2},{4,3},{5,4},{6,5},{7,6},{8,7},{9,8},{10,9... | collective-permute-start | bytes 122888 | tf_op jit(solution)/shard_map/ppermute | solution.py:391
  44.3 46.6 %collective-permute-done.2.low_ref = f32[2,5,8,128]{3,2,1,0:T(8,128)S(1)} collective-permute-done((f32[2,5,8,128]{3,2,1,0:T(8,128)S(1)}, f32[2,5,8,128]{3,2,1,0:T(8,128)S(1)}, u32[]{:S(2)}, u32[]{:S(2)}) %collective-permute-start.2) | collective-permute-done | bytes 40992 | tf_op jit(solution)/shard_map/ppermute | solution.py:391
  90.9 0.0 collective-permute-done.3.high_ref
  90.9 0.0 copy-done.2
  90.9 0.0 copy-done.4
  90.9 2.1 %tracers.1 = f32[16,128]{1,0:T(8,128)} custom-call(s32[16]{0:T(128)S(1)} %bitcast.15, s32[16]{0:T(128)S(1)} %bitcast.16, f32[16,128]{1,0:T(8,128)S(1)} %get-tuple-element.6.sample_ref, f32[8,5,8,128]{3,2,1,0:T(8,128)S(1)} %get-tuple-element.7.edge_ref, f32[2,5,8,128]{3,2,1,0:T(8,128)S(1)} %collective-permute-done.2.low_ref, ...), custom_call_target="tpu_custom_call" | custom-call | flops 5000000 | bytes 800000 | tf_op jit(solution)/shard_map/tracers/pallas_call | solution.py:374
  93.0 2.0 %all-to-all-done.lines_ref = f32[16,5,32,128]{3,2,1,0:T(8,128)S(1)} async-done(((f32[16,5,32,128]{3,2,1,0:T(8,128)}), f32[16,5,32,128]{3,2,1,0:T(8,128)S(1)}, u32[]{:S(2)}, u32[]{:S(2)}) %all-to-all-start) | async-done | bytes 1310752 | tf_op jit(solution)/shard_map/all_to_all | solution.py:402
  94.9 4.1 %sweep_z.1 = f32[5,8,4,2048]{3,2,1,0:T(4,128)} custom-call(f32[16,5,32,128]{3,2,1,0:T(8,128)S(1)} %all-to-all-done.lines_ref), custom_call_target="tpu_custom_call" | custom-call | flops 20000000 | bytes 2700000 | tf_op jit(solution)/shard_map/sweep_z/pallas_call | solution.py:237
  (2 shorter events, 0.0 us)
Async XLA Ops:
  1.7 7.7 %collective-permute-start = (f32[3,5,8,128]{3,2,1,0:T(8,128)S(1)}, f32[3,5,8,128]{3,2,1,0:T(8,128)S(1)}, u32[]{:S(2)}, u32[]{:S(2)}) collective-permute-start(f32[3,5,8,128]{3,2,1,0:T(8,128)S(1)} %bitcast.17), channel_id=1, source_target_pairs={{0,16},{16,32},{32,48},{48,64},{64,80},{80,96},{96,112},{112,128},... | collective-permute-start | bytes 184328 | tf_op jit(solution)/shard_map/ppermute | solution.py:391
  3.6 7.6 %collective-permute-start.1 = (f32[3,5,8,128]{3,2,1,0:T(8,128)S(1)}, f32[3,5,8,128]{3,2,1,0:T(8,128)S(1)}, u32[]{:S(2)}, u32[]{:S(2)}) collective-permute-start(f32[3,5,8,128]{3,2,1,0:T(8,128)S(1)} %bitcast.18), channel_id=1, source_target_pairs={{0,496},{16,0},{32,16},{48,32},{64,48},{80,64},{96,80},{112,96},{1... | collective-permute-start | bytes 184328 | tf_op jit(solution)/shard_map/ppermute | solution.py:391
  11.2 1.3 %copy-start = (f32[5,8,64,128]{3,2,1,0:T(8,128)S(1)}, f32[5,8,64,128]{3,2,1,0:T(8,128)}, u32[]{:S(2)}) copy-start(f32[5,8,64,128]{3,2,1,0:T(8,128)} %fluid_ref.1) | copy-start | bytes 3932164
  16.1 15.3 %copy-start.1 = (s32[1,1,16,128]{3,2,1,0:T(8,128)S(1)}, s32[1,1,16,128]{3,2,1,0:T(8,128)}, u32[]{:S(2)}) copy-start(s32[1,1,16,128]{3,2,1,0:T(8,128)} %param.6) | copy-start | bytes 24580
  16.1 15.3 %copy-start.3 = (s32[1,1,16]{2,1,0:T(1,128)S(1)}, s32[1,1,16]{2,1,0:T(1,128)}, u32[]{:S(2)}) copy-start(s32[1,1,16]{2,1,0:T(1,128)} %param.7) | copy-start | bytes 196
  16.1 78.8 %all-to-all-start = ((f32[16,5,32,128]{3,2,1,0:T(8,128)}), f32[16,5,32,128]{3,2,1,0:T(8,128)S(1)}, u32[]{:S(2)}, u32[]{:S(2)}) async-start(f32[16,5,32,128]{3,2,1,0:T(8,128)} %sweep_y.1.middle_ref), calls=%async_computation | async-start | bytes 2621440 | tf_op jit(solution)/shard_map/all_to_all | solution.py:402
  31.3 59.6 %copy-start.2 = (f32[1,1,16,128]{3,2,1,0:T(8,128)S(1)}, f32[1,1,16,128]{3,2,1,0:T(8,128)}, u32[]{:S(2)}) copy-start(f32[1,1,16,128]{3,2,1,0:T(8,128)} %param.9) | copy-start | bytes 24580
  31.3 59.6 %copy-start.4 = (s32[1,1,16]{2,1,0:T(1,128)S(1)}, s32[1,1,16]{2,1,0:T(1,128)}, u32[]{:S(2)}) copy-start(s32[1,1,16]{2,1,0:T(1,128)} %param.8) | copy-start | bytes 196
  37.2 53.7 %collective-permute-start.2 = (f32[2,5,8,128]{3,2,1,0:T(8,128)S(1)}, f32[2,5,8,128]{3,2,1,0:T(8,128)S(1)}, u32[]{:S(2)}, u32[]{:S(2)}) collective-permute-start(f32[2,5,8,128]{3,2,1,0:T(8,128)S(1)} %get-tuple-element.8), channel_id=1, source_target_pairs={{0,1},{1,2},{2,3},{3,4},{4,5},{5,6},{6,7},{7,8},{8,9},{9,10},{10,1... | collective-permute-start | bytes 122888 | tf_op jit(solution)/shard_map/ppermute | solution.py:391
  41.0 49.9 %collective-permute-start.3 = (f32[2,5,8,128]{3,2,1,0:T(8,128)S(1)}, f32[2,5,8,128]{3,2,1,0:T(8,128)S(1)}, u32[]{:S(2)}, u32[]{:S(2)}) collective-permute-start(f32[2,5,8,128]{3,2,1,0:T(8,128)S(1)} %get-tuple-element.9), channel_id=1, source_target_pairs={{0,15},{1,0},{2,1},{3,2},{4,3},{5,4},{6,5},{7,6},{8,7},{9,8},{10,9... | collective-permute-start | bytes 122888 | tf_op jit(solution)/shard_map/ppermute | solution.py:391

commit v3 on v2

--- a/solution.py
+++ b/solution.py
@@ -93,11 +93,12 @@
     ]
 
 
-def sweep_y_kernel(fluid_ref, low_ref, high_ref, middle_ref, cells_ref, new_ref, in_sem, out_sem):
+def sweep_y_kernel(fluid_ref, outer_ref, inner_ref, middle_ref, cells_ref, new_ref, in_sem, out_sem):
     nx, rows_y = fluid_ref.shape[1:3]
     blocks = middle_ref.shape[0]
     chunks = 4
     depth = rows_y // chunks
+    odd = lax.axis_index("gy") % 2 == 1
     copies = []
     for c in range(chunks):
         part = pl.ds(c * depth, depth)
@@ -113,10 +114,10 @@
         return [flat_ref[k, pl.ds(y, nx, stride=rows_y), :] for k in range(5)]
 
     def low(i):
-        return [low_ref[i, k] for k in range(5)]
+        return [jnp.where(odd, inner_ref[i, k], outer_ref[i, k]) for k in range(5)]
 
     def high(i):
-        return [high_ref[i, k] for k in range(5)]
+        return [jnp.where(odd, outer_ref[i, k], inner_ref[i, k]) for k in range(5)]
 
     def block(h, carry, load):
         flux, right, face, c0, c1, c2 = carry
@@ -153,7 +154,7 @@
     sent = []
     for c in range(chunks):
         until = (c + 1) * blocks // chunks - 1
-        carry = lax.fori_loop(first, until, step, carry)
+        carry = lax.fori_loop(first, until, step, carry, unroll=True)
         sent.append(send(c, first, until - first))
         first = until
         if c + 1 < chunks:
@@ -168,7 +169,7 @@
         copy.wait()
 
 
-def sweep_y(fluid, low, high, blocks):
+def sweep_y(fluid, outer, inner, blocks):
     nx, ny, nz = fluid.shape[1:]
     rows = nx * ny // blocks
     return pl.pallas_call(
@@ -182,65 +183,87 @@
             pltpu.SemaphoreType.DMA((4,)),
             pltpu.SemaphoreType.DMA((5,)),
         ],
-        compiler_params=pltpu.CompilerParams(vmem_limit_bytes=16 * 1024 * 1024),
+        compiler_params=pltpu.CompilerParams(vmem_limit_bytes=52 * 1024 * 1024),
         cost_estimate=pl.CostEstimate(
             flops=20_000_000, bytes_accessed=2_700_000, transcendentals=0
         ),
         name="sweep_y",
-    )(fluid, low, high)
-
-
-def sweep_z_kernel(lines_ref, out_ref, face_ref, left_ref, right_ref, flux_ref):
-    tiles = lines_ref.shape[0]
+    )(fluid, outer, inner)
+
+
+def sweep_z_kernel(lines_ref, out_ref, face_ref, left_ref, right_ref, flux_ref, new_ref, out_sem):
+    tiles, _, rows, _ = lines_ref.shape
+    steps = rows // 8
     lane = lax.broadcasted_iota(jnp.int32, (8, LANES), 1)
 
-    spot = pl.multiple_of(pl.program_id(0) * 8, 8)
-
-    def get(ref, t):
-        if ref is lines_ref:
-            return [ref[t % tiles, k, pl.ds(spot, 8), :] for k in range(5)]
-        return [ref[t % tiles, k] for k in range(5)]
-
-    def put(ref, t, values):
+    def cell(q, t):
+        return [lines_ref[t % tiles, k, pl.ds(8 * q, 8), :] for k in range(5)]
+
+    def get(ref, q, t):
+        return [ref[q % 2, t % tiles, k] for k in range(5)]
+
+    def put(ref, q, t, values):
         for k in range(5):
-            ref[t, k] = values[k]
-
-    for t in range(tiles):
-        before, here, following = [get(lines_ref, t + d) for d in (-1, 0, 1)]
+            ref[q % 2, t, k] = values[k]
+
+    def stage_face(q, t):
+        before, here, following = [cell(q, t + d) for d in (-1, 0, 1)]
         second = [
             pltpu.roll(jnp.where(lane < 2, f, h), LANES - 2, 1) for h, f in zip(here, following)
         ]
-        put(face_ref, t, face_of(
+        put(face_ref, q, t, face_of(
             lane_before(here, before, lane), here, lane_after(here, following, lane), second
         ))
-    for t in range(tiles):
-        face = get(face_ref, t)
+
+    def stage_edges(q, t):
+        face = get(face_ref, q, t)
         left, right = edges_of(
-            get(lines_ref, t), lane_before(face, get(face_ref, t - 1), lane), face
+            cell(q, t), lane_before(face, get(face_ref, q, t - 1), lane), face
         )
-        put(left_ref, t, left)
-        put(right_ref, t, right)
-    for t in range(tiles):
-        follow = lane_after(get(left_ref, t), get(left_ref, t + 1), lane)
-        put(flux_ref, t, flux_of(get(right_ref, t), follow, 3))
-    for t in range(tiles):
-        flux = get(flux_ref, t)
-        new = updated(get(lines_ref, t), lane_before(flux, get(flux_ref, t - 1), lane), flux)
+        put(left_ref, q, t, left)
+        put(right_ref, q, t, right)
+
+    def stage_flux(q, t):
+        follow = lane_after(get(left_ref, q, t), get(left_ref, q, t + 1), lane)
+        put(flux_ref, q, t, flux_of(get(right_ref, q, t), follow, 3))
+
+    def stage_new(q, t):
+        flux = get(flux_ref, q, t)
+        new = updated(cell(q, t), lane_before(flux, get(flux_ref, q, t - 1), lane), flux)
         for k in range(5):
             for half in range(2):
-                out_ref[k, half, :, t * LANES : (t + 1) * LANES] = new[k][4 * half : 4 * half + 4]
+                place = pl.ds(t * LANES, LANES)
+                new_ref[k, 2 * q + half, :, place] = new[k][4 * half : 4 * half + 4]
+
+    sent = []
+    stages = (stage_face, stage_edges, stage_flux, stage_new)
+    for step in range(steps + 3):
+        for start in range(0, tiles, 4):
+            for age, stage in enumerate(stages):
+                q = step - age
+                if 0 <= q < steps:
+                    for t in range(start, start + 4):
+                        stage(q, t)
+        q = step - 3
+        if q >= 0:
+            part = pl.ds(2 * q, 2)
+            copy = pltpu.make_async_copy(new_ref.at[:, part], out_ref.at[:, part], out_sem.at[q])
+            copy.start()
+            sent.append(copy)
+    for copy in sent:
+        copy.wait()
 
 
 def sweep_z(lines, nx):
     tiles, _, rows, _ = lines.shape
-    sub = rows // nx
+    shape = (5, nx, rows // nx, tiles * LANES)
     return pl.pallas_call(
         sweep_z_kernel,
-        grid=(rows // 8,),
-        out_shape=jax.ShapeDtypeStruct((5, nx, sub, tiles * LANES), jnp.float32),
+        out_shape=jax.ShapeDtypeStruct(shape, jnp.float32),
         in_specs=[pl.BlockSpec(memory_space=pltpu.VMEM)],
-        out_specs=pl.BlockSpec((5, 2, sub, tiles * LANES), lambda q: (0, q, 0, 0)),
-        scratch_shapes=[pltpu.VMEM((tiles, 5, 8, LANES), jnp.float32)] * 4,
+        out_specs=pl.BlockSpec(memory_space=pl.ANY),
+        scratch_shapes=[pltpu.VMEM((2, tiles, 5, 8, LANES), jnp.float32)] * 4
+        + [pltpu.VMEM(shape, jnp.float32), pltpu.SemaphoreType.DMA((rows // 8,))],
         compiler_params=pltpu.CompilerParams(vmem_limit_bytes=16 * 1024 * 1024),
         cost_estimate=pl.CostEstimate(
             flops=20_000_000, bytes_accessed=2_700_000, transcendentals=0
@@ -263,41 +286,46 @@
     return [updated(s, before(f), f) for s, f in zip(states, fluxes)]
 
 
-def inner_kernel(owner_ref, middle_ref, cell_ref, sample_ref, edge_ref, low_ref, high_ref, press_ref):
+def inner_kernel(owner_ref, middle_ref, cell_ref, sample_ref, own_ref, up_ref, down_ref, press_ref):
     blocks, _, rows, _ = middle_ref.shape
     lane = lax.broadcasted_iota(jnp.int32, (8, LANES), 1)
-
-    def eight(j, _):
-        ends = [jnp.zeros((8, LANES), jnp.float32) for _ in range(5)]
-        for part in range(2):
-            h = 2 * j + part
-            states = [
-                [middle_ref[h, k, pl.ds(sub, 8, stride=4), :] for k in range(5)] for sub in range(4)
-            ]
-            for sub, new in enumerate(lines_of(states)):
-                press_ref[h, pl.ds(sub, 8, stride=4), :] = new[4]
-            for sub, state in enumerate(states):
-                g = 4 * part + sub
-                ends = [
-                    jnp.where(lane // 16 == g, pltpu.roll(v, (16 * g + 8) % LANES, 1), e)
-                    for v, e in zip(state, ends)
-                ]
-        for k in range(5):
-            edge_ref[j, k] = ends[k]
+    lower = lane < LANES // 2
+
+    def line(h, sub, k):
+        return middle_ref[h, k, pl.ds(sub, 8, stride=4), :]
+
+    def four(h, _):
+        states = [[line(h, sub, k) for k in range(5)] for sub in range(4)]
+        for sub, new in enumerate(lines_of(states)):
+            press_ref[h, pl.ds(sub, 8, stride=4), :] = new[4]
         return 0
 
-    lax.fori_loop(0, blocks // 2, eight, 0)
-    for part in range(blocks // 8):
-        for k in range(5):
-            low = edge_ref[4 * part, k]
-            high = low
-            for r in range(4):
-                ends = edge_ref[4 * part + r, k]
-                mine = lane % 16 // 4 == r
-                low = jnp.where(mine, pltpu.roll(ends, (LANES + 4 * r - 8) % LANES, 1), low)
-                high = jnp.where(mine, pltpu.roll(ends, (LANES + 4 * r - 4) % LANES, 1), high)
-            low_ref[part, k] = low
-            high_ref[part, k] = high
+    lax.fori_loop(0, blocks, four, 0)
+    ends = list(range(6)) + list(range(LANES - 6, LANES))
+    group = 4
+    for k in range(5):
+
+        def gather(i, found):
+            found = list(found)
+            for at in range(4 * group):
+                y = 4 * group * i + at
+                moved = pltpu.roll(line(group * i + at // 4, at % 4, k), y, 1)
+                for n, z in enumerate(ends):
+                    found[n] = jnp.where(lane == (y + z) % LANES, moved, found[n])
+            return tuple(found)
+
+        zeros = (jnp.zeros((8, LANES), jnp.float32),) * len(ends)
+        found = lax.fori_loop(0, blocks // group, gather, zeros)
+        low = [pltpu.roll(found[z], (LANES - z) % LANES, 1) for z in range(6)]
+        high = [pltpu.roll(found[6 + n], (LANES // 2 + 6 - n) % LANES, 1) for n in range(6)]
+        own = high[:3] + [jnp.where(lower, l, h) for l, h in zip(low[:3], high[3:])] + low[3:]
+        for j in range(9):
+            own_ref[j, k] = own[j]
+        turned = [pltpu.roll(v, LANES // 2, 1) for v in (own[3], own[5])]
+        up_ref[0, k] = jnp.where(lower, turned[0], own[4])
+        down_ref[0, k] = jnp.where(lower, own[4], turned[0])
+        up_ref[1, k] = turned[1]
+        down_ref[1, k] = turned[1]
     row_ids = lax.broadcasted_iota(jnp.int32, (rows, LANES), 0)
     for j in range(blocks):
         cells = cell_ref[j : j + 1, :]
@@ -311,14 +339,13 @@
 
 def inner_samples(owner, middle, cells):
     blocks, _, rows, _ = middle.shape
-    parts = blocks // 8
     return pl.pallas_call(
         inner_kernel,
         out_shape=(
             jax.ShapeDtypeStruct(cells.shape, jnp.float32),
-            jax.ShapeDtypeStruct((blocks // 2, 5, 8, LANES), jnp.float32),
-            jax.ShapeDtypeStruct((parts, 5, 8, LANES), jnp.float32),
-            jax.ShapeDtypeStruct((parts, 5, 8, LANES), jnp.float32),
+            jax.ShapeDtypeStruct((9, 5, 8, LANES), jnp.float32),
+            jax.ShapeDtypeStruct((2, 5, 8, LANES), jnp.float32),
+            jax.ShapeDtypeStruct((2, 5, 8, LANES), jnp.float32),
         ),
         in_specs=[pl.BlockSpec(memory_space=pltpu.SMEM)]
         + [pl.BlockSpec(memory_space=pltpu.VMEM)] * 2,
@@ -332,58 +359,59 @@
     )(owner, middle, cells)
 
 
-def tracers_kernel(owner_ref, count_ref, sample_ref, edge_ref, low_ref, high_ref, cell_ref, peak_ref,
-                   out_ref, table_ref):
+def tracers_kernel(owner_ref, count_ref, sample_ref, own_ref, below_ref, above_ref, cell_ref, peak_ref,
+                   out_ref):
     blocks = sample_ref.shape[0]
     lane = lax.broadcasted_iota(jnp.int32, (8, LANES), 1)
-    upper = lane % 16 < 8
-    batch = 8
-    for start in range(0, blocks // 2, batch):
-        states = []
-        for j in range(start, start + batch):
-            part, r = j // 4, j % 4
-            ends = [edge_ref[j, k] for k in range(5)]
-            below = [pltpu.roll(low_ref[part, k], (LANES + 4 - 4 * r) % LANES, 1) for k in range(5)]
-            above = [pltpu.roll(high_ref[part, k], (LANES + 8 - 4 * r) % LANES, 1) for k in range(5)]
-            states.append([jnp.where(upper, b, e) for b, e in zip(below, ends)])
-            states.append([jnp.where(upper, e, a) for a, e in zip(above, ends)])
-        new = lines_of(states)
-        for i in range(batch):
-            table_ref[start + i] = jnp.where(upper, new[2 * i + 1][4], new[2 * i][4])
+    lower = lane < LANES // 2
+
+    def ends(ref, k):
+        first = ref[0, k]
+        return [first, pltpu.roll(first, LANES // 2, 1), ref[1, k]]
+
+    states = [[own_ref[j, k] for k in range(5)] for j in range(9)]
+    for k in range(5):
+        for j, (b, a) in enumerate(zip(ends(below_ref, k), ends(above_ref, k))):
+            states[j][k] = jnp.where(lower, b, states[j][k])
+            states[6 + j][k] = jnp.where(lower, states[6 + j][k], a)
+    faces = [face_of(*states[j : j + 4]) for j in range(6)]
+    edges = [edges_of(states[j + 2], faces[j], faces[j + 1]) for j in range(5)]
+    fluxes = [flux_of(edges[j][1], edges[j + 1][0], 3) for j in range(4)]
+    tables = [updated(states[j + 3], fluxes[j], fluxes[j + 1])[4] for j in range(3)]
     planes = lax.broadcasted_iota(jnp.int32, (8, LANES), 0)
     cells = cell_ref[...]
     z_ids = cells % LANES
-    outer = (z_ids < 3) | (z_ids >= LANES - 3)
+    upper = z_ids >= LANES - 3
+    place = jnp.where(upper, z_ids - (LANES - 3), z_ids)
+    offset = cells // LANES % 4 + jnp.where(upper, LANES // 2, 0)
     sampled = []
     for j in range(blocks):
-        owner = owner_ref[j]
-        ids = 16 * (4 * (owner % 2) + cells[j : j + 1] // LANES % 4) + (z_ids[j : j + 1] + 8) % 16
-        ids = jnp.broadcast_to(ids, (8, LANES))
-        picked = jnp.take_along_axis(table_ref[owner // 2], ids, axis=1, mode="promise_in_bounds")
+        ids = jnp.broadcast_to(offset[j : j + 1] + 4 * owner_ref[j], (8, LANES))
+        spot = jnp.broadcast_to(place[j : j + 1], (8, LANES))
+        picked = [jnp.take_along_axis(t, ids, axis=1, mode="promise_in_bounds") for t in tables]
+        value = jnp.where(spot == 0, picked[0], jnp.where(spot == 1, picked[1], picked[2]))
         chosen = jnp.broadcast_to(cells[j : j + 1] // (4 * LANES), (8, LANES)) == planes
-        sampled.append(jnp.sum(jnp.where(chosen, picked, 0.0), axis=0, keepdims=True))
-    sampled = jnp.where(outer, jnp.concatenate(sampled, axis=0), sample_ref[...])
+        sampled.append(jnp.sum(jnp.where(chosen, value, 0.0), axis=0, keepdims=True))
+    sampled = jnp.where(place < 3, jnp.concatenate(sampled, axis=0), sample_ref[...])
     slot = lax.broadcasted_iota(jnp.int32, (1, LANES), 1)
     raised = jnp.maximum(peak_ref[...], sampled)
     for j in range(blocks):
         out_ref[j : j + 1, :] = jnp.where(slot < count_ref[j], raised[j : j + 1, :], 0.0)
 
 
-def tracers(owner, count, sample, edge, low, high, cells, peaks):
-    blocks = sample.shape[0]
+def tracers(owner, count, sample, own, below, above, cells, peaks):
     return pl.pallas_call(
         tracers_kernel,
         out_shape=jax.ShapeDtypeStruct(peaks.shape, jnp.float32),
         in_specs=[pl.BlockSpec(memory_space=pltpu.SMEM)] * 2
         + [pl.BlockSpec(memory_space=pltpu.VMEM)] * 6,
         out_specs=pl.BlockSpec(memory_space=pltpu.VMEM),
-        scratch_shapes=[pltpu.VMEM((blocks // 2, 8, LANES), jnp.float32)],
         compiler_params=pltpu.CompilerParams(vmem_limit_bytes=16 * 1024 * 1024),
         cost_estimate=pl.CostEstimate(
-            flops=5_000_000, bytes_accessed=800_000, transcendentals=0
+            flops=2_000_000, bytes_accessed=400_000, transcendentals=0
         ),
         name="tracers",
-    )(owner, count, sample, edge, low, high, cells, peaks)
+    )(owner, count, sample, own, below, above, cells, peaks)
 
 
 def shifted(values, axis, step):
@@ -396,16 +424,20 @@
     blocks = lax.axis_size("gz")
     head = jnp.transpose(fluid_state[:, :, :3], (2, 0, 1, 3))
     tail = jnp.transpose(fluid_state[:, :, ny - 3 :], (2, 0, 1, 3))
-    low = shifted(tail, "gy", 1)
-    high = shifted(head, "gy", -1)
-    middle = sweep_y(fluid_state, low, high, blocks)
+    count = lax.axis_size("gy")
+    odd = lax.axis_index("gy") % 2 == 1
+    inner = [(i, i ^ 1) for i in range(count)]
+    outer = [((i + 1) % count, ((i ^ 1) + 1) % count) for i in range(count)]
+    got_inner = lax.ppermute(jnp.where(odd, head, tail), "gy", inner)
+    got_outer = lax.ppermute(jnp.where(odd, tail, head), "gy", outer)
+    middle = sweep_y(fluid_state, got_outer, got_inner, blocks)
     lines = lax.all_to_all(middle, "gz", split_axis=0, concat_axis=0, tiled=True)
     owner, cells = tracer_owner[0, 0], tracer_cell[0, 0]
-    sample, edge, z_head, z_tail = inner_samples(owner, middle, cells)
-    above = shifted(z_head, "gz", -1)
-    below = shifted(z_tail, "gz", 1)
+    sample, own, up, down = inner_samples(owner, middle, cells)
+    above = shifted(down, "gz", -1)
+    below = shifted(up, "gz", 1)
     new_peak = tracers(
-        owner, tracer_count[0, 0], sample, edge, below, above, cells, tracer_peak[0, 0]
+        owner, tracer_count[0, 0], sample, own, below, above, cells, tracer_peak[0, 0]
     )
     new_state = sweep_z(lines, nx)
     return (new_state, new_peak[None, None])

time: 99.4 us -> 96.2 us (0.968)
  waiting for transfers between devices: 50.4 us -> 45.5 us
  Pallas kernels: 15.5 us -> 20 us
  starting transfers between devices: 29.9 us -> 28.5 us
  local copies, waits for them, and re-layouts: 2.38 us -> 1.06 us
    ppermute x4 -> x2, starting transfers between devices: 14.7 us -> 7.05 us  [shifted(): lax.ppermute(values, axis, [(i, (i + step) % count) for i in range(count)])]
    ppermute x4 -> x2, waiting for transfers between devices: 48.5 us -> 41.9 us  [shifted(): lax.ppermute(values, axis, [(i, (i + step) % count) for i in range(count)])]
    ppermute x0 -> x2, starting transfers between devices: none -> 6.21 us  [the longest x1 4.29 us: on_device(): got_outer = lax.ppermute(jnp.where(odd, tail, head), 'gy', outer)]
    pallas_call x1, Pallas kernels: 5.83 us -> 11.1 us  [inner_samples(): pl.pallas_call(inner_kernel, out_shape=(jax.ShapeDtypeStruct(cells.shape,...]
    ppermute x0 -> x2, waiting for transfers between devices: none -> 1.43 us  [the longest x1 1.43 us: on_device(): got_outer = lax.ppermute(jnp.where(odd, tail, head), 'gy', outer)]
    unnamed x12 -> x8, local copies, waits for them, and re-layouts: 1.35 us -> 0.03 us
  transfers between devices with their start and end apart: 5 -> 5, of which waited for: 3 -> 3; matrix products, arithmetic and copies ran while one was open for 0% -> 0% of each run, Pallas kernels for 8% -> 13%
where the time goes in v3:
time: 96.2 us; the launch traced here: 95.8 us
  waiting for transfers between devices  45.5 us (47%)
  starting transfers between devices  28.5 us (30%)
  Pallas kernels  20 us (21%)
  local copies, waits for them, and re-layouts  1.06 us (1%)
    ppermute x2, waiting for transfers between devices, shifted(): lax.ppermute(values, axis, [(i, (i + step) % count) for i in range(count)])  41.9 us
    all_to_all x1, starting transfers between devices, on_device(): lax.all_to_all(middle, 'gz', split_axis=0, concat_axis=0, tiled=True)  15.2 us
    pallas_call x1, Pallas kernels, inner_samples(): pl.pallas_call(inner_kernel, out_shape=(jax.ShapeDtypeStruct(cells.shape,...  11.1 us
    ppermute x2, starting transfers between devices, shifted(): lax.ppermute(values, axis, [(i, (i + step) % count) for i in range(count)])  7.05 us
    ppermute x1, starting transfers between devices, on_device(): got_outer = lax.ppermute(jnp.where(odd, tail, head), 'gy', outer)  4.29 us
    pallas_call x1, Pallas kernels, sweep_y(): pl.pallas_call(sweep_y_kernel, out_shape=jax.ShapeDtypeStruct((blocks, 5,...  3.98 us
    pallas_call x1, Pallas kernels, sweep_z(): pl.pallas_call(sweep_z_kernel, out_shape=jax.ShapeDtypeStruct(shape, jnp....  3.39 us
    all_to_all x1, waiting for transfers between devices, on_device(): lax.all_to_all(middle, 'gz', split_axis=0, concat_axis=0, tiled=True)  2.18 us
  transfers between devices with their start and end apart: 5, of which 3 were waited for; matrix products, arithmetic and copies ran while one was open for 0% of the time, Pallas kernels for 13%

profile of v3, /device:TPU:24, one launch (start us, length us, event | category | flops | bytes accessed | tf_op | source)
XLA Modules:
  0.0 95.8 jit_solution(3369649203193287433)
XLA Ops:
  0.6 1.0 %fusion = (f32[5,8,3,128]{3,2,1,0:T(4,128)S(1)}, f32[5,8,3,128]{3,2,1,0:T(4,128)S(1)}) fusion(f32[5,8,64,128]{3,2,1,0:T(8,128)} %fluid_ref.1), kind=kLoop, calls=%fused_computation.2 | loop fusion | bytes 245760 | tf_op jit(solution)/shard_map/slice | solution.py:426
  1.7 4.3 %collective-permute-start = (f32[3,5,8,128]{3,2,1,0:T(8,128)S(1)}, f32[3,5,8,128]{3,2,1,0:T(8,128)S(1)}, u32[]{:S(2)}, u32[]{:S(2)}) collective-permute-start(f32[3,5,8,128]{3,2,1,0:T(8,128)S(1)} %get-tuple-element.13), channel_id=1, source_target_pairs={{16,32},{32,16},{48,64},{64,48},{80,96},{96,80},{112,128},{128,112... | collective-permute-start | bytes 184328 | tf_op jit(solution)/shard_map/ppermute | solution.py:432
  6.0 1.9 %collective-permute-start.1 = (f32[3,5,8,128]{3,2,1,0:T(8,128)S(1)}, f32[3,5,8,128]{3,2,1,0:T(8,128)S(1)}, u32[]{:S(2)}, u32[]{:S(2)}) collective-permute-start(f32[3,5,8,128]{3,2,1,0:T(8,128)S(1)} %get-tuple-element.12), channel_id=1, source_target_pairs={{0,16},{16,0},{32,48},{48,32},{64,80},{80,64},{96,112},{112,96},{1... | collective-permute-start | bytes 184328 | tf_op jit(solution)/shard_map/ppermute | solution.py:431
  7.9 1.4 %collective-permute-done.outer_ref = f32[3,5,8,128]{3,2,1,0:T(8,128)S(1)} collective-permute-done((f32[3,5,8,128]{3,2,1,0:T(8,128)S(1)}, f32[3,5,8,128]{3,2,1,0:T(8,128)S(1)}, u32[]{:S(2)}, u32[]{:S(2)}) %collective-permute-start) | collective-permute-done | bytes 61472 | tf_op jit(solution)/shard_map/ppermute | solution.py:432
  9.3 0.0 collective-permute-done.1.inner_ref
  9.4 4.0 %sweep_y.1.middle_ref = f32[16,5,32,128]{3,2,1,0:T(8,128)} custom-call(f32[5,8,64,128]{3,2,1,0:T(8,128)} %fluid_ref.1, f32[3,5,8,128]{3,2,1,0:T(8,128)S(1)} %collective-permute-done.outer_ref, f32[3,5,8,128]{3,2,1,0:T(8,128)S(1)} %collective-permute-done.1.inner_ref), custom_call_target="tpu_custom_call" | custom-call | flops 20000000 | bytes 2700000 | tf_op jit(solution)/shard_map/sweep_y/pallas_call | solution.py:175
  13.3 0.0 copy-start
  13.3 0.0 copy-start.2
  13.4 15.2 %all-to-all-start = ((f32[16,5,32,128]{3,2,1,0:T(8,128)}), f32[16,5,32,128]{3,2,1,0:T(8,128)S(1)}, u32[]{:S(2)}, u32[]{:S(2)}) async-start(f32[16,5,32,128]{3,2,1,0:T(8,128)} %sweep_y.1.middle_ref), calls=%async_computation | async-start | bytes 2621440 | tf_op jit(solution)/shard_map/all_to_all | solution.py:434
  28.6 0.0 copy-start.1
  28.6 0.0 copy-start.3
  28.6 0.0 copy-done
  28.6 0.0 copy-done.2
  28.6 11.1 %inner_samples.1 = (f32[16,128]{1,0:T(8,128)S(1)}, f32[9,5,8,128]{3,2,1,0:T(8,128)S(1)}, f32[2,5,8,128]{3,2,1,0:T(8,128)S(1)}, f32[2,5,8,128]{3,2,1,0:T(8,128)S(1)}) custom-call(s32[16]{0:T(128)S(1)} %bitcast.12, f32[16,5,32,128]{3,2,1,0:T(8,128)} %sweep_y.1.middle_ref, s32[16,128]{1,0:T(8,128)S(1)} %bitcast.9), custom_call_target="tpu_custom_call" | custom-call | flops 20000000 | bytes 1600000 | tf_op jit(solution)/shard_map/inner_samples/pallas_call | solution.py:342
  39.7 3.8 %collective-permute-start.2 = (f32[2,5,8,128]{3,2,1,0:T(8,128)S(1)}, f32[2,5,8,128]{3,2,1,0:T(8,128)S(1)}, u32[]{:S(2)}, u32[]{:S(2)}) collective-permute-start(f32[2,5,8,128]{3,2,1,0:T(8,128)S(1)} %get-tuple-element.8), channel_id=1, source_target_pairs={{0,1},{1,2},{2,3},{3,4},{4,5},{5,6},{6,7},{7,8},{8,9},{9,10},{10,1... | collective-permute-start | bytes 122888 | tf_op jit(solution)/shard_map/ppermute | solution.py:419
  43.6 3.2 %collective-permute-start.3 = (f32[2,5,8,128]{3,2,1,0:T(8,128)S(1)}, f32[2,5,8,128]{3,2,1,0:T(8,128)S(1)}, u32[]{:S(2)}, u32[]{:S(2)}) collective-permute-start(f32[2,5,8,128]{3,2,1,0:T(8,128)S(1)} %get-tuple-element.9), channel_id=1, source_target_pairs={{0,15},{1,0},{2,1},{3,2},{4,3},{5,4},{6,5},{7,6},{8,7},{9,8},{10,9... | collective-permute-start | bytes 122888 | tf_op jit(solution)/shard_map/ppermute | solution.py:419
  46.8 41.9 %collective-permute-done.2.below_ref = f32[2,5,8,128]{3,2,1,0:T(8,128)S(1)} collective-permute-done((f32[2,5,8,128]{3,2,1,0:T(8,128)S(1)}, f32[2,5,8,128]{3,2,1,0:T(8,128)S(1)}, u32[]{:S(2)}, u32[]{:S(2)}) %collective-permute-start.2) | collective-permute-done | bytes 40992 | tf_op jit(solution)/shard_map/ppermute | solution.py:419
  88.7 0.0 collective-permute-done.3.above_ref
  88.7 0.0 copy-done.1
  88.7 0.0 copy-done.3
  88.7 1.5 %tracers.1 = f32[16,128]{1,0:T(8,128)} custom-call(s32[16]{0:T(128)S(1)} %bitcast.13, s32[16]{0:T(128)S(1)} %bitcast.14, f32[16,128]{1,0:T(8,128)S(1)} %get-tuple-element.6.sample_ref, f32[9,5,8,128]{3,2,1,0:T(8,128)S(1)} %get-tuple-element.7.own_ref, f32[2,5,8,128]{3,2,1,0:T(8,128)S(1)} %collective-permute-done.2.below_ref, ...), custom_call_target="tpu_custom_call" | custom-call | flops 2000000 | bytes 400000 | tf_op jit(solution)/shard_map/tracers/pallas_call | solution.py:403
  90.2 2.2 %all-to-all-done.lines_ref = f32[16,5,32,128]{3,2,1,0:T(8,128)S(1)} async-done(((f32[16,5,32,128]{3,2,1,0:T(8,128)}), f32[16,5,32,128]{3,2,1,0:T(8,128)S(1)}, u32[]{:S(2)}, u32[]{:S(2)}) %all-to-all-start) | async-done | bytes 1310752 | tf_op jit(solution)/shard_map/all_to_all | solution.py:434
  92.4 3.4 %sweep_z.1 = f32[5,8,4,2048]{3,2,1,0:T(4,128)} custom-call(f32[16,5,32,128]{3,2,1,0:T(8,128)S(1)} %all-to-all-done.lines_ref), custom_call_target="tpu_custom_call" | custom-call | flops 20000000 | bytes 2700000 | tf_op jit(solution)/shard_map/sweep_z/pallas_call | solution.py:260
  (1 shorter events, 0.0 us)
Async XLA Ops:
  1.7 7.7 %collective-permute-start = (f32[3,5,8,128]{3,2,1,0:T(8,128)S(1)}, f32[3,5,8,128]{3,2,1,0:T(8,128)S(1)}, u32[]{:S(2)}, u32[]{:S(2)}) collective-permute-start(f32[3,5,8,128]{3,2,1,0:T(8,128)S(1)} %get-tuple-element.13), channel_id=1, source_target_pairs={{16,32},{32,16},{48,64},{64,48},{80,96},{96,80},{112,128},{128,112... | collective-permute-start | bytes 184328 | tf_op jit(solution)/shard_map/ppermute | solution.py:432
  6.0 3.4 %collective-permute-start.1 = (f32[3,5,8,128]{3,2,1,0:T(8,128)S(1)}, f32[3,5,8,128]{3,2,1,0:T(8,128)S(1)}, u32[]{:S(2)}, u32[]{:S(2)}) collective-permute-start(f32[3,5,8,128]{3,2,1,0:T(8,128)S(1)} %get-tuple-element.12), channel_id=1, source_target_pairs={{0,16},{16,0},{32,48},{48,32},{64,80},{80,64},{96,112},{112,96},{1... | collective-permute-start | bytes 184328 | tf_op jit(solution)/shard_map/ppermute | solution.py:431
  13.3 15.3 %copy-start = (s32[1,1,16,128]{3,2,1,0:T(8,128)S(1)}, s32[1,1,16,128]{3,2,1,0:T(8,128)}, u32[]{:S(2)}) copy-start(s32[1,1,16,128]{3,2,1,0:T(8,128)} %param.6) | copy-start | bytes 24580
  13.3 15.3 %copy-start.2 = (s32[1,1,16]{2,1,0:T(1,128)S(1)}, s32[1,1,16]{2,1,0:T(1,128)}, u32[]{:S(2)}) copy-start(s32[1,1,16]{2,1,0:T(1,128)} %param.7) | copy-start | bytes 196
  13.4 79.0 %all-to-all-start = ((f32[16,5,32,128]{3,2,1,0:T(8,128)}), f32[16,5,32,128]{3,2,1,0:T(8,128)S(1)}, u32[]{:S(2)}, u32[]{:S(2)}) async-start(f32[16,5,32,128]{3,2,1,0:T(8,128)} %sweep_y.1.middle_ref), calls=%async_computation | async-start | bytes 2621440 | tf_op jit(solution)/shard_map/all_to_all | solution.py:434
  28.6 60.1 %copy-start.1 = (f32[1,1,16,128]{3,2,1,0:T(8,128)S(1)}, f32[1,1,16,128]{3,2,1,0:T(8,128)}, u32[]{:S(2)}) copy-start(f32[1,1,16,128]{3,2,1,0:T(8,128)} %param.9) | copy-start | bytes 24580
  28.6 60.1 %copy-start.3 = (s32[1,1,16]{2,1,0:T(1,128)S(1)}, s32[1,1,16]{2,1,0:T(1,128)}, u32[]{:S(2)}) copy-start(s32[1,1,16]{2,1,0:T(1,128)} %param.8) | copy-start | bytes 196
  39.7 49.0 %collective-permute-start.2 = (f32[2,5,8,128]{3,2,1,0:T(8,128)S(1)}, f32[2,5,8,128]{3,2,1,0:T(8,128)S(1)}, u32[]{:S(2)}, u32[]{:S(2)}) collective-permute-start(f32[2,5,8,128]{3,2,1,0:T(8,128)S(1)} %get-tuple-element.8), channel_id=1, source_target_pairs={{0,1},{1,2},{2,3},{3,4},{4,5},{5,6},{6,7},{7,8},{8,9},{9,10},{10,1... | collective-permute-start | bytes 122888 | tf_op jit(solution)/shard_map/ppermute | solution.py:419
  43.6 45.1 %collective-permute-start.3 = (f32[2,5,8,128]{3,2,1,0:T(8,128)S(1)}, f32[2,5,8,128]{3,2,1,0:T(8,128)S(1)}, u32[]{:S(2)}, u32[]{:S(2)}) collective-permute-start(f32[2,5,8,128]{3,2,1,0:T(8,128)S(1)} %get-tuple-element.9), channel_id=1, source_target_pairs={{0,15},{1,0},{2,1},{3,2},{4,3},{5,4},{6,5},{7,6},{8,7},{9,8},{10,9... | collective-permute-start | bytes 122888 | tf_op jit(solution)/shard_map/ppermute | solution.py:419

commit v4 on v3

--- a/solution.py
+++ b/solution.py
@@ -93,22 +93,12 @@
     ]
 
 
-def sweep_y_kernel(fluid_ref, outer_ref, inner_ref, middle_ref, cells_ref, new_ref, in_sem, out_sem):
+def sweep_y_kernel(fluid_ref, outer_ref, inner_ref, middle_ref, new_ref, out_sem):
     nx, rows_y = fluid_ref.shape[1:3]
     blocks = middle_ref.shape[0]
     chunks = 4
-    depth = rows_y // chunks
     odd = lax.axis_index("gy") % 2 == 1
-    copies = []
-    for c in range(chunks):
-        part = pl.ds(c * depth, depth)
-        copies.append(
-            pltpu.make_async_copy(
-                fluid_ref.at[:, :, part, :], cells_ref.at[:, :, part, :], in_sem.at[c]
-            )
-        )
-        copies[c].start()
-    flat_ref = cells_ref.reshape(5, nx * rows_y, LANES)
+    flat_ref = fluid_ref.reshape(5, nx * rows_y, LANES)
 
     def row(y):
         return [flat_ref[k, pl.ds(y, nx, stride=rows_y), :] for k in range(5)]
@@ -141,7 +131,6 @@
         copy.start()
         return copy
 
-    copies[0].wait()
     m3, m2, m1 = low(0), low(1), low(2)
     c0, c1, c2 = row(0), row(1), row(2)
     face_a = face_of(m3, m2, m1, c0)
@@ -157,8 +146,6 @@
         carry = lax.fori_loop(first, until, step, carry, unroll=True)
         sent.append(send(c, first, until - first))
         first = until
-        if c + 1 < chunks:
-            copies[c + 1].wait()
 
     def last(sub):
         return row(rows_y - 1) if sub == 0 else high(sub - 1)
@@ -167,6 +154,25 @@
     sent.append(send(chunks, blocks - 1, 1))
     for copy in sent:
         copy.wait()
+
+
+def stage_kernel(fluid_ref, out_ref, sem):
+    copy = pltpu.make_async_copy(fluid_ref, out_ref, sem)
+    copy.start()
+    copy.wait()
+
+
+def staged(fluid):
+    return pl.pallas_call(
+        stage_kernel,
+        out_shape=jax.ShapeDtypeStruct(fluid.shape, jnp.float32),
+        in_specs=[pl.BlockSpec(memory_space=pl.ANY)],
+        out_specs=pl.BlockSpec(memory_space=pltpu.VMEM),
+        scratch_shapes=[pltpu.SemaphoreType.DMA],
+        compiler_params=pltpu.CompilerParams(vmem_limit_bytes=int(51.5 * 1024 * 1024)),
+        cost_estimate=pl.CostEstimate(flops=0, bytes_accessed=2_700_000, transcendentals=0),
+        name="stage",
+    )(fluid)
 
 
 def sweep_y(fluid, outer, inner, blocks):
@@ -175,15 +181,13 @@
     return pl.pallas_call(
         sweep_y_kernel,
         out_shape=jax.ShapeDtypeStruct((blocks, 5, rows, nz), jnp.float32),
-        in_specs=[pl.BlockSpec(memory_space=pl.ANY)] + [pl.BlockSpec(memory_space=pltpu.VMEM)] * 2,
+        in_specs=[pl.BlockSpec(memory_space=pltpu.VMEM)] * 3,
         out_specs=pl.BlockSpec(memory_space=pl.ANY),
         scratch_shapes=[
-            pltpu.VMEM((5, nx, ny, nz), jnp.float32),
             pltpu.VMEM((blocks, 5, rows, nz), jnp.float32),
-            pltpu.SemaphoreType.DMA((4,)),
             pltpu.SemaphoreType.DMA((5,)),
         ],
-        compiler_params=pltpu.CompilerParams(vmem_limit_bytes=52 * 1024 * 1024),
+        compiler_params=pltpu.CompilerParams(vmem_limit_bytes=16 * 1024 * 1024),
         cost_estimate=pl.CostEstimate(
             flops=20_000_000, bytes_accessed=2_700_000, transcendentals=0
         ),
@@ -191,7 +195,37 @@
     )(fluid, outer, inner)
 
 
-def sweep_z_kernel(lines_ref, out_ref, face_ref, left_ref, right_ref, flux_ref, new_ref, out_sem):
+def outer_peaks(floor_ref, ids_ref, code_ref, own_ref, below_ref, above_ref, peak_ref):
+    lane = lax.broadcasted_iota(jnp.int32, (8, LANES), 1)
+    lower = lane < LANES // 2
+
+    def ends(ref, k):
+        first = ref[0, k]
+        return [first, pltpu.roll(first, LANES // 2, 1), ref[1, k]]
+
+    states = [[own_ref[j, k] for k in range(5)] for j in range(9)]
+    for k in range(5):
+        for j, (b, a) in enumerate(zip(ends(below_ref, k), ends(above_ref, k))):
+            states[j][k] = jnp.where(lower, b, states[j][k])
+            states[6 + j][k] = jnp.where(lower, states[6 + j][k], a)
+    faces = [face_of(*states[j : j + 4]) for j in range(6)]
+    edges = [edges_of(states[j + 2], faces[j], faces[j + 1]) for j in range(5)]
+    fluxes = [flux_of(edges[j][1], edges[j + 1][0], 3) for j in range(4)]
+    tables = [updated(states[j + 3], fluxes[j], fluxes[j + 1])[4] for j in range(3)]
+    planes = lax.broadcasted_iota(jnp.int32, (8, LANES), 0)
+    for j in range(floor_ref.shape[0]):
+        ids = jnp.broadcast_to(ids_ref[j : j + 1, :], (8, LANES))
+        code = jnp.broadcast_to(code_ref[j : j + 1, :], (8, LANES))
+        value = jnp.zeros((8, LANES), jnp.float32)
+        for n, table in enumerate(tables):
+            picked = jnp.take_along_axis(table, ids, axis=1, mode="promise_in_bounds")
+            value = jnp.where(code == planes + 8 * n, picked, value)
+        raised = jnp.sum(value, axis=0, keepdims=True)
+        peak_ref[j : j + 1, :] = jnp.maximum(floor_ref[j : j + 1, :], raised)
+
+
+def sweep_z_kernel(lines_ref, floor_ref, ids_ref, code_ref, own_ref, below_ref, above_ref, out_ref, peaks_ref,
+                   face_ref, left_ref, right_ref, flux_ref, new_ref, peak_ref, out_sem, peak_sem):
     tiles, _, rows, _ = lines_ref.shape
     steps = rows // 8
     lane = lax.broadcasted_iota(jnp.int32, (8, LANES), 1)
@@ -235,7 +269,8 @@
                 place = pl.ds(t * LANES, LANES)
                 new_ref[k, 2 * q + half, :, place] = new[k][4 * half : 4 * half + 4]
 
-    sent = []
+    outer_peaks(floor_ref, ids_ref, code_ref, own_ref, below_ref, above_ref, peak_ref)
+    sent = [pltpu.make_async_copy(peak_ref, peaks_ref, peak_sem)]
     stages = (stage_face, stage_edges, stage_flux, stage_new)
     for step in range(steps + 3):
         for start in range(0, tiles, 4):
@@ -245,6 +280,8 @@
                     for t in range(start, start + 4):
                         stage(q, t)
         q = step - 3
+        if q == 0:
+            sent[0].start()
         if q >= 0:
             part = pl.ds(2 * q, 2)
             copy = pltpu.make_async_copy(new_ref.at[:, part], out_ref.at[:, part], out_sem.at[q])
@@ -254,22 +291,30 @@
         copy.wait()
 
 
-def sweep_z(lines, nx):
+def sweep_z(lines, floor, ids, code, own, below, above, nx):
     tiles, _, rows, _ = lines.shape
     shape = (5, nx, rows // nx, tiles * LANES)
     return pl.pallas_call(
         sweep_z_kernel,
-        out_shape=jax.ShapeDtypeStruct(shape, jnp.float32),
-        in_specs=[pl.BlockSpec(memory_space=pltpu.VMEM)],
-        out_specs=pl.BlockSpec(memory_space=pl.ANY),
+        out_shape=(
+            jax.ShapeDtypeStruct(shape, jnp.float32),
+            jax.ShapeDtypeStruct(floor.shape, jnp.float32),
+        ),
+        in_specs=[pl.BlockSpec(memory_space=pltpu.VMEM)] * 7,
+        out_specs=(pl.BlockSpec(memory_space=pl.ANY),) * 2,
         scratch_shapes=[pltpu.VMEM((2, tiles, 5, 8, LANES), jnp.float32)] * 4
-        + [pltpu.VMEM(shape, jnp.float32), pltpu.SemaphoreType.DMA((rows // 8,))],
+        + [
+            pltpu.VMEM(shape, jnp.float32),
+            pltpu.VMEM(floor.shape, jnp.float32),
+            pltpu.SemaphoreType.DMA((rows // 8,)),
+            pltpu.SemaphoreType.DMA,
+        ],
         compiler_params=pltpu.CompilerParams(vmem_limit_bytes=16 * 1024 * 1024),
         cost_estimate=pl.CostEstimate(
             flops=20_000_000, bytes_accessed=2_700_000, transcendentals=0
         ),
         name="sweep_z",
-    )(lines)
+    )(lines, floor, ids, code, own, below, above)
 
 
 def lines_of(states):
@@ -286,7 +331,8 @@
     return [updated(s, before(f), f) for s, f in zip(states, fluxes)]
 
 
-def inner_kernel(owner_ref, middle_ref, cell_ref, sample_ref, own_ref, up_ref, down_ref, press_ref):
+def inner_kernel(owner_ref, count_ref, middle_ref, cell_ref, peak_ref, floor_ref, ids_ref, code_ref, own_ref,
+                 up_ref, down_ref, press_ref):
     blocks, _, rows, _ = middle_ref.shape
     lane = lax.broadcasted_iota(jnp.int32, (8, LANES), 1)
     lower = lane < LANES // 2
@@ -327,91 +373,49 @@
         up_ref[1, k] = turned[1]
         down_ref[1, k] = turned[1]
     row_ids = lax.broadcasted_iota(jnp.int32, (rows, LANES), 0)
+    slot = lax.broadcasted_iota(jnp.int32, (1, LANES), 1)
     for j in range(blocks):
+        owner = owner_ref[j]
         cells = cell_ref[j : j + 1, :]
-        z_ids = jnp.broadcast_to(cells % LANES, (rows, LANES))
+        z = cells % LANES
         picked = jnp.take_along_axis(
-            press_ref[owner_ref[j]], z_ids, axis=1, mode="promise_in_bounds"
+            press_ref[owner], jnp.broadcast_to(z, (rows, LANES)), axis=1, mode="promise_in_bounds"
         )
         chosen = jnp.broadcast_to(cells // LANES, (rows, LANES)) == row_ids
-        sample_ref[j : j + 1, :] = jnp.sum(jnp.where(chosen, picked, 0.0), axis=0, keepdims=True)
-
-
-def inner_samples(owner, middle, cells):
+        sampled = jnp.sum(jnp.where(chosen, picked, 0.0), axis=0, keepdims=True)
+        upper = z >= LANES - 3
+        outer = upper | (z < 3)
+        live = slot < count_ref[j]
+        peak = peak_ref[j : j + 1, :]
+        raised = jnp.where(outer, peak, jnp.maximum(peak, sampled))
+        floor_ref[j : j + 1, :] = jnp.where(live, raised, 0.0)
+        ids_ref[j : j + 1, :] = 4 * owner + cells // LANES % 4 + jnp.where(upper, LANES // 2, 0)
+        table = jnp.where(upper, z - (LANES - 3), z)
+        code_ref[j : j + 1, :] = jnp.where(outer & live, 8 * table + cells // (4 * LANES), -1)
+
+
+def inner_samples(owner, count, middle, cells, peaks):
     blocks, _, rows, _ = middle.shape
     return pl.pallas_call(
         inner_kernel,
         out_shape=(
             jax.ShapeDtypeStruct(cells.shape, jnp.float32),
+            jax.ShapeDtypeStruct(cells.shape, jnp.int32),
+            jax.ShapeDtypeStruct(cells.shape, jnp.int32),
             jax.ShapeDtypeStruct((9, 5, 8, LANES), jnp.float32),
             jax.ShapeDtypeStruct((2, 5, 8, LANES), jnp.float32),
             jax.ShapeDtypeStruct((2, 5, 8, LANES), jnp.float32),
         ),
-        in_specs=[pl.BlockSpec(memory_space=pltpu.SMEM)]
-        + [pl.BlockSpec(memory_space=pltpu.VMEM)] * 2,
-        out_specs=(pl.BlockSpec(memory_space=pltpu.VMEM),) * 4,
+        in_specs=[pl.BlockSpec(memory_space=pltpu.SMEM)] * 2
+        + [pl.BlockSpec(memory_space=pltpu.VMEM)] * 3,
+        out_specs=(pl.BlockSpec(memory_space=pltpu.VMEM),) * 6,
         scratch_shapes=[pltpu.VMEM((blocks, rows, LANES), jnp.float32)],
         compiler_params=pltpu.CompilerParams(vmem_limit_bytes=16 * 1024 * 1024),
         cost_estimate=pl.CostEstimate(
             flops=20_000_000, bytes_accessed=1_600_000, transcendentals=0
         ),
         name="inner_samples",
-    )(owner, middle, cells)
-
-
-def tracers_kernel(owner_ref, count_ref, sample_ref, own_ref, below_ref, above_ref, cell_ref, peak_ref,
-                   out_ref):
-    blocks = sample_ref.shape[0]
-    lane = lax.broadcasted_iota(jnp.int32, (8, LANES), 1)
-    lower = lane < LANES // 2
-
-    def ends(ref, k):
-        first = ref[0, k]
-        return [first, pltpu.roll(first, LANES // 2, 1), ref[1, k]]
-
-    states = [[own_ref[j, k] for k in range(5)] for j in range(9)]
-    for k in range(5):
-        for j, (b, a) in enumerate(zip(ends(below_ref, k), ends(above_ref, k))):
-            states[j][k] = jnp.where(lower, b, states[j][k])
-            states[6 + j][k] = jnp.where(lower, states[6 + j][k], a)
-    faces = [face_of(*states[j : j + 4]) for j in range(6)]
-    edges = [edges_of(states[j + 2], faces[j], faces[j + 1]) for j in range(5)]
-    fluxes = [flux_of(edges[j][1], edges[j + 1][0], 3) for j in range(4)]
-    tables = [updated(states[j + 3], fluxes[j], fluxes[j + 1])[4] for j in range(3)]
-    planes = lax.broadcasted_iota(jnp.int32, (8, LANES), 0)
-    cells = cell_ref[...]
-    z_ids = cells % LANES
-    upper = z_ids >= LANES - 3
-    place = jnp.where(upper, z_ids - (LANES - 3), z_ids)
-    offset = cells // LANES % 4 + jnp.where(upper, LANES // 2, 0)
-    sampled = []
-    for j in range(blocks):
-        ids = jnp.broadcast_to(offset[j : j + 1] + 4 * owner_ref[j], (8, LANES))
-        spot = jnp.broadcast_to(place[j : j + 1], (8, LANES))
-        picked = [jnp.take_along_axis(t, ids, axis=1, mode="promise_in_bounds") for t in tables]
-        value = jnp.where(spot == 0, picked[0], jnp.where(spot == 1, picked[1], picked[2]))
-        chosen = jnp.broadcast_to(cells[j : j + 1] // (4 * LANES), (8, LANES)) == planes
-        sampled.append(jnp.sum(jnp.where(chosen, value, 0.0), axis=0, keepdims=True))
-    sampled = jnp.where(place < 3, jnp.concatenate(sampled, axis=0), sample_ref[...])
-    slot = lax.broadcasted_iota(jnp.int32, (1, LANES), 1)
-    raised = jnp.maximum(peak_ref[...], sampled)
-    for j in range(blocks):
-        out_ref[j : j + 1, :] = jnp.where(slot < count_ref[j], raised[j : j + 1, :], 0.0)
-
-
-def tracers(owner, count, sample, own, below, above, cells, peaks):
-    return pl.pallas_call(
-        tracers_kernel,
-        out_shape=jax.ShapeDtypeStruct(peaks.shape, jnp.float32),
-        in_specs=[pl.BlockSpec(memory_space=pltpu.SMEM)] * 2
-        + [pl.BlockSpec(memory_space=pltpu.VMEM)] * 6,
-        out_specs=pl.BlockSpec(memory_space=pltpu.VMEM),
-        compiler_params=pltpu.CompilerParams(vmem_limit_bytes=16 * 1024 * 1024),
-        cost_estimate=pl.CostEstimate(
-            flops=2_000_000, bytes_accessed=400_000, transcendentals=0
-        ),
-        name="tracers",
-    )(owner, count, sample, own, below, above, cells, peaks)
+    )(owner, count, middle, cells, peaks)
 
 
 def shifted(values, axis, step):
@@ -430,16 +434,14 @@
     outer = [((i + 1) % count, ((i ^ 1) + 1) % count) for i in range(count)]
     got_inner = lax.ppermute(jnp.where(odd, head, tail), "gy", inner)
     got_outer = lax.ppermute(jnp.where(odd, tail, head), "gy", outer)
-    middle = sweep_y(fluid_state, got_outer, got_inner, blocks)
+    middle = sweep_y(staged(fluid_state), got_outer, got_inner, blocks)
     lines = lax.all_to_all(middle, "gz", split_axis=0, concat_axis=0, tiled=True)
-    owner, cells = tracer_owner[0, 0], tracer_cell[0, 0]
-    sample, own, up, down = inner_samples(owner, middle, cells)
+    floor, ids, code, own, up, down = inner_samples(
+        tracer_owner[0, 0], tracer_count[0, 0], middle, tracer_cell[0, 0], tracer_peak[0, 0]
+    )
     above = shifted(down, "gz", -1)
     below = shifted(up, "gz", 1)
-    new_peak = tracers(
-        owner, tracer_count[0, 0], sample, own, below, above, cells, tracer_peak[0, 0]
-    )
-    new_state = sweep_z(lines, nx)
+    new_state, new_peak = sweep_z(lines, floor, ids, code, own, below, above, nx)
     return (new_state, new_peak[None, None])
 
 

time: 96.2 us -> 96.4 us (level)
  the two profiles are of different devices: /device:TPU:24 before, /device:TPU:31 now
where the time goes in v4:
time: 96.4 us; the launch traced here: 96 us
  waiting for transfers between devices  44.1 us (46%)
  starting transfers between devices  31.1 us (32%)
  Pallas kernels  19 us (20%)
  local copies, waits for them, and re-layouts  1.06 us (1%)
    ppermute x2, waiting for transfers between devices, shifted(): lax.ppermute(values, axis, [(i, (i + step) % count) for i in range(count)])  40.2 us
    all_to_all x1, starting transfers between devices, on_device(): lax.all_to_all(middle, 'gz', split_axis=0, concat_axis=0, tiled=True)  15 us
    pallas_call x1, Pallas kernels, inner_samples(): pl.pallas_call(inner_kernel, out_shape=(jax.ShapeDtypeStruct(cells.shape,...  11.1 us
    ppermute x1, starting transfers between devices, on_device(): got_outer = lax.ppermute(jnp.where(odd, tail, head), 'gy', outer)  7.04 us
    ppermute x2, starting transfers between devices, shifted(): lax.ppermute(values, axis, [(i, (i + step) % count) for i in range(count)])  6.49 us
    pallas_call x1, Pallas kernels, sweep_z(): pl.pallas_call(sweep_z_kernel, out_shape=(jax.ShapeDtypeStruct(shape, jnp...  3.64 us
    all_to_all x1, waiting for transfers between devices, on_device(): lax.all_to_all(middle, 'gz', split_axis=0, concat_axis=0, tiled=True)  3.38 us
    pallas_call x1, Pallas kernels, sweep_y(): pl.pallas_call(sweep_y_kernel, out_shape=jax.ShapeDtypeStruct((blocks, 5,...  2.92 us
  transfers between devices with their start and end apart: 5, of which 3 were waited for; matrix products, arithmetic and copies ran while one was open for 0% of the time, Pallas kernels for 13%

profile of v4, /device:TPU:31, one launch (start us, length us, event | category | flops | bytes accessed | tf_op | source)
XLA Modules:
  0.0 96.0 jit_solution(680246262402200138)
XLA Ops:
  0.6 1.0 %fusion = (f32[5,8,3,128]{3,2,1,0:T(4,128)S(1)}, f32[5,8,3,128]{3,2,1,0:T(4,128)S(1)}) fusion(f32[5,8,64,128]{3,2,1,0:T(8,128)} %fluid_ref.1), kind=kLoop, calls=%fused_computation.2 | loop fusion | bytes 245760 | tf_op jit(solution)/shard_map/slice | solution.py:430
  1.7 2.6 %collective-permute-start.1 = (f32[3,5,8,128]{3,2,1,0:T(8,128)S(1)}, f32[3,5,8,128]{3,2,1,0:T(8,128)S(1)}, u32[]{:S(2)}, u32[]{:S(2)}) collective-permute-start(f32[3,5,8,128]{3,2,1,0:T(8,128)S(1)} %get-tuple-element.20), channel_id=1, source_target_pairs={{0,16},{16,0},{32,48},{48,32},{64,80},{80,64},{96,112},{112,96},{1... | collective-permute-start | bytes 184328 | tf_op jit(solution)/shard_map/ppermute | solution.py:435
  4.3 7.0 %collective-permute-start = (f32[3,5,8,128]{3,2,1,0:T(8,128)S(1)}, f32[3,5,8,128]{3,2,1,0:T(8,128)S(1)}, u32[]{:S(2)}, u32[]{:S(2)}) collective-permute-start(f32[3,5,8,128]{3,2,1,0:T(8,128)S(1)} %get-tuple-element.21), channel_id=1, source_target_pairs={{16,32},{32,16},{48,64},{64,48},{80,96},{96,80},{112,128},{128,112... | collective-permute-start | bytes 184328 | tf_op jit(solution)/shard_map/ppermute | solution.py:436
  11.3 1.3 %stage.1.fluid_ref = f32[5,8,64,128]{3,2,1,0:T(8,128)S(1)} custom-call(f32[5,8,64,128]{3,2,1,0:T(8,128)} %fluid_ref.1), custom_call_target="tpu_custom_call" | custom-call | bytes 2700000 | tf_op jit(solution)/shard_map/stage/pallas_call | solution.py:166
  12.7 0.0 collective-permute-done.1.inner_ref
  12.7 0.5 collective-permute-done.outer_ref
  13.2 2.9 %sweep_y.1.middle_ref = f32[16,5,32,128]{3,2,1,0:T(8,128)} custom-call(f32[5,8,64,128]{3,2,1,0:T(8,128)S(1)} %stage.1.fluid_ref, f32[3,5,8,128]{3,2,1,0:T(8,128)S(1)} %collective-permute-done.outer_ref, f32[3,5,8,128]{3,2,1,0:T(8,128)S(1)} %collective-permute-done.1.inner_ref), custom_call_target="tpu_custom_call" | custom-call | flops 20000000 | bytes 2700000 | tf_op jit(solution)/shard_map/sweep_y/pallas_call | solution.py:181
  16.2 0.0 copy-start
  16.2 0.0 copy-start.1
  16.2 0.0 copy-start.2
  16.2 0.0 copy-start.3
  16.2 15.0 %all-to-all-start = ((f32[16,5,32,128]{3,2,1,0:T(8,128)}), f32[16,5,32,128]{3,2,1,0:T(8,128)S(1)}, u32[]{:S(2)}, u32[]{:S(2)}) async-start(f32[16,5,32,128]{3,2,1,0:T(8,128)} %sweep_y.1.middle_ref), calls=%async_computation | async-start | bytes 2621440 | tf_op jit(solution)/shard_map/all_to_all | solution.py:438
  31.2 0.0 copy-done
  31.2 0.0 copy-done.1
  31.2 0.0 copy-done.2
  31.2 0.0 copy-done.3
  31.2 11.1 %inner_samples.1 = (f32[16,128]{1,0:T(8,128)S(1)}, s32[16,128]{1,0:T(8,128)S(1)}, s32[16,128]{1,0:T(8,128)S(1)}, f32[9,5,8,128]{3,2,1,0:T(8,128)S(1)}, f32[2,5,8...) custom-call(s32[16]{0:T(128)S(1)} %bitcast.11, s32[16]{0:T(128)S(1)} %bitcast.12, ...), custom_call_target="tpu_custom_call" | custom-call | flops 20000000 | bytes 1600000 | tf_op jit(solution)/shard_map/inner_samples/pallas_call | solution.py:399
  42.4 3.3 %collective-permute-start.2 = (f32[2,5,8,128]{3,2,1,0:T(8,128)S(1)}, f32[2,5,8,128]{3,2,1,0:T(8,128)S(1)}, u32[]{:S(2)}, u32[]{:S(2)}) collective-permute-start(f32[2,5,8,128]{3,2,1,0:T(8,128)S(1)} %get-tuple-element.14), channel_id=1, source_target_pairs={{0,1},{1,2},{2,3},{3,4},{4,5},{5,6},{6,7},{7,8},{8,9},{9,10},{10,1... | collective-permute-start | bytes 122888 | tf_op jit(solution)/shard_map/ppermute | solution.py:423
  45.6 3.2 %collective-permute-start.3 = (f32[2,5,8,128]{3,2,1,0:T(8,128)S(1)}, f32[2,5,8,128]{3,2,1,0:T(8,128)S(1)}, u32[]{:S(2)}, u32[]{:S(2)}) collective-permute-start(f32[2,5,8,128]{3,2,1,0:T(8,128)S(1)} %get-tuple-element.15), channel_id=1, source_target_pairs={{0,15},{1,0},{2,1},{3,2},{4,3},{5,4},{6,5},{7,6},{8,7},{9,8},{10,9... | collective-permute-start | bytes 122888 | tf_op jit(solution)/shard_map/ppermute | solution.py:423
  48.9 40.2 %collective-permute-done.2.below_ref = f32[2,5,8,128]{3,2,1,0:T(8,128)S(1)} collective-permute-done((f32[2,5,8,128]{3,2,1,0:T(8,128)S(1)}, f32[2,5,8,128]{3,2,1,0:T(8,128)S(1)}, u32[]{:S(2)}, u32[]{:S(2)}) %collective-permute-start.2) | collective-permute-done | bytes 40992 | tf_op jit(solution)/shard_map/ppermute | solution.py:423
  89.0 0.0 collective-permute-done.3.above_ref
  89.0 3.4 %all-to-all-done.lines_ref = f32[16,5,32,128]{3,2,1,0:T(8,128)S(1)} async-done(((f32[16,5,32,128]{3,2,1,0:T(8,128)}), f32[16,5,32,128]{3,2,1,0:T(8,128)S(1)}, u32[]{:S(2)}, u32[]{:S(2)}) %all-to-all-start) | async-done | bytes 1310752 | tf_op jit(solution)/shard_map/all_to_all | solution.py:438
  92.4 3.6 %sweep_z.1 = (f32[5,8,4,2048]{3,2,1,0:T(4,128)}, f32[16,128]{1,0:T(8,128)}) custom-call(f32[16,5,32,128]{3,2,1,0:T(8,128)S(1)} %all-to-all-done.lines_ref, f32[16,128]{1,0:T(8,128)S(1)} %get-tuple-element.10.floor_ref, s32[16,128]{1,0:T(8,128)S(1)} %get-tuple-element.11.ids_ref, s32[16,128]{1,0:T(8,128)S(1)} %get-tuple-element.12.code_ref, ...), custom_call_target="tpu_custom_call" | custom-call | flops 20000000 | bytes 2700000 | tf_op jit(solution)/shard_map/sweep_z/pallas_call | solution.py:297
  (1 shorter events, 0.0 us)
Async XLA Ops:
  1.7 11.0 %collective-permute-start.1 = (f32[3,5,8,128]{3,2,1,0:T(8,128)S(1)}, f32[3,5,8,128]{3,2,1,0:T(8,128)S(1)}, u32[]{:S(2)}, u32[]{:S(2)}) collective-permute-start(f32[3,5,8,128]{3,2,1,0:T(8,128)S(1)} %get-tuple-element.20), channel_id=1, source_target_pairs={{0,16},{16,0},{32,48},{48,32},{64,80},{80,64},{96,112},{112,96},{1... | collective-permute-start | bytes 184328 | tf_op jit(solution)/shard_map/ppermute | solution.py:435
  4.3 8.9 %collective-permute-start = (f32[3,5,8,128]{3,2,1,0:T(8,128)S(1)}, f32[3,5,8,128]{3,2,1,0:T(8,128)S(1)}, u32[]{:S(2)}, u32[]{:S(2)}) collective-permute-start(f32[3,5,8,128]{3,2,1,0:T(8,128)S(1)} %get-tuple-element.21), channel_id=1, source_target_pairs={{16,32},{32,16},{48,64},{64,48},{80,96},{96,80},{112,128},{128,112... | collective-permute-start | bytes 184328 | tf_op jit(solution)/shard_map/ppermute | solution.py:436
  16.2 15.0 %copy-start = (s32[1,1,16,128]{3,2,1,0:T(8,128)S(1)}, s32[1,1,16,128]{3,2,1,0:T(8,128)}, u32[]{:S(2)}) copy-start(s32[1,1,16,128]{3,2,1,0:T(8,128)} %param.6) | copy-start | bytes 24580
  16.2 15.0 %copy-start.1 = (f32[1,1,16,128]{3,2,1,0:T(8,128)S(1)}, f32[1,1,16,128]{3,2,1,0:T(8,128)}, u32[]{:S(2)}) copy-start(f32[1,1,16,128]{3,2,1,0:T(8,128)} %param.9) | copy-start | bytes 24580
  16.2 15.0 %copy-start.2 = (s32[1,1,16]{2,1,0:T(1,128)S(1)}, s32[1,1,16]{2,1,0:T(1,128)}, u32[]{:S(2)}) copy-start(s32[1,1,16]{2,1,0:T(1,128)} %param.7) | copy-start | bytes 196
  16.2 15.0 %copy-start.3 = (s32[1,1,16]{2,1,0:T(1,128)S(1)}, s32[1,1,16]{2,1,0:T(1,128)}, u32[]{:S(2)}) copy-start(s32[1,1,16]{2,1,0:T(1,128)} %param.8) | copy-start | bytes 196
  16.2 76.2 %all-to-all-start = ((f32[16,5,32,128]{3,2,1,0:T(8,128)}), f32[16,5,32,128]{3,2,1,0:T(8,128)S(1)}, u32[]{:S(2)}, u32[]{:S(2)}) async-start(f32[16,5,32,128]{3,2,1,0:T(8,128)} %sweep_y.1.middle_ref), calls=%async_computation | async-start | bytes 2621440 | tf_op jit(solution)/shard_map/all_to_all | solution.py:438
  42.4 46.7 %collective-permute-start.2 = (f32[2,5,8,128]{3,2,1,0:T(8,128)S(1)}, f32[2,5,8,128]{3,2,1,0:T(8,128)S(1)}, u32[]{:S(2)}, u32[]{:S(2)}) collective-permute-start(f32[2,5,8,128]{3,2,1,0:T(8,128)S(1)} %get-tuple-element.14), channel_id=1, source_target_pairs={{0,1},{1,2},{2,3},{3,4},{4,5},{5,6},{6,7},{7,8},{8,9},{9,10},{10,1... | collective-permute-start | bytes 122888 | tf_op jit(solution)/shard_map/ppermute | solution.py:423
  45.6 43.4 %collective-permute-start.3 = (f32[2,5,8,128]{3,2,1,0:T(8,128)S(1)}, f32[2,5,8,128]{3,2,1,0:T(8,128)S(1)}, u32[]{:S(2)}, u32[]{:S(2)}) collective-permute-start(f32[2,5,8,128]{3,2,1,0:T(8,128)S(1)} %get-tuple-element.15), channel_id=1, source_target_pairs={{0,15},{1,0},{2,1},{3,2},{4,3},{5,4},{6,5},{7,6},{8,7},{9,8},{10,9... | collective-permute-start | bytes 122888 | tf_op jit(solution)/shard_map/ppermute | solution.py:423

commit v5 on v4

--- a/solution.py
+++ b/solution.py
@@ -93,7 +93,7 @@
     ]
 
 
-def sweep_y_kernel(fluid_ref, outer_ref, inner_ref, middle_ref, new_ref, out_sem):
+def sweep_y_kernel(fluid_ref, inner_ref, outer_ref, middle_ref, new_ref, out_sem):
     nx, rows_y = fluid_ref.shape[1:3]
     blocks = middle_ref.shape[0]
     chunks = 4
@@ -175,7 +175,7 @@
     )(fluid)
 
 
-def sweep_y(fluid, outer, inner, blocks):
+def sweep_y(fluid, inner, outer, blocks):
     nx, ny, nz = fluid.shape[1:]
     rows = nx * ny // blocks
     return pl.pallas_call(
@@ -192,7 +192,7 @@
             flops=20_000_000, bytes_accessed=2_700_000, transcendentals=0
         ),
         name="sweep_y",
-    )(fluid, outer, inner)
+    )(fluid, inner, outer)
 
 
 def outer_peaks(floor_ref, ids_ref, code_ref, own_ref, below_ref, above_ref, peak_ref):
@@ -434,7 +434,7 @@
     outer = [((i + 1) % count, ((i ^ 1) + 1) % count) for i in range(count)]
     got_inner = lax.ppermute(jnp.where(odd, head, tail), "gy", inner)
     got_outer = lax.ppermute(jnp.where(odd, tail, head), "gy", outer)
-    middle = sweep_y(staged(fluid_state), got_outer, got_inner, blocks)
+    middle = sweep_y(staged(fluid_state), got_inner, got_outer, blocks)
     lines = lax.all_to_all(middle, "gz", split_axis=0, concat_axis=0, tiled=True)
     floor, ids, code, own, up, down = inner_samples(
         tracer_owner[0, 0], tracer_count[0, 0], middle, tracer_cell[0, 0], tracer_peak[0, 0]

time: 96.4 us -> 95.6 us (level)
  the two profiles are of different devices: /device:TPU:31 before, /device:TPU:16 now
where the time goes in v5:
time: 95.6 us; the launch traced here: 95.2 us
  waiting for transfers between devices  46 us (48%)
  starting transfers between devices  28.3 us (30%)
  Pallas kernels  19 us (20%)
  local copies, waits for them, and re-layouts  1.06 us (1%)
    ppermute x2, waiting for transfers between devices, shifted(): lax.ppermute(values, axis, [(i, (i + step) % count) for i in range(count)])  42.3 us
    all_to_all x1, starting transfers between devices, on_device(): lax.all_to_all(middle, 'gz', split_axis=0, concat_axis=0, tiled=True)  15.3 us
    pallas_call x1, Pallas kernels, inner_samples(): pl.pallas_call(inner_kernel, out_shape=(jax.ShapeDtypeStruct(cells.shape,...  11.1 us
    ppermute x2, starting transfers between devices, shifted(): lax.ppermute(values, axis, [(i, (i + step) % count) for i in range(count)])  7.05 us
    ppermute x1, starting transfers between devices, on_device(): got_outer = lax.ppermute(jnp.where(odd, tail, head), 'gy', outer)  3.99 us
    pallas_call x1, Pallas kernels, sweep_z(): pl.pallas_call(sweep_z_kernel, out_shape=(jax.ShapeDtypeStruct(shape, jnp...  3.64 us
    all_to_all x1, waiting for transfers between devices, on_device(): lax.all_to_all(middle, 'gz', split_axis=0, concat_axis=0, tiled=True)  3.32 us
    pallas_call x1, Pallas kernels, sweep_y(): pl.pallas_call(sweep_y_kernel, out_shape=jax.ShapeDtypeStruct((blocks, 5,...  2.92 us
  transfers between devices with their start and end apart: 5, of which 3 were waited for; matrix products, arithmetic and copies ran while one was open for 0% of the time, Pallas kernels for 13%

profile of v5, /device:TPU:16, one launch (start us, length us, event | category | flops | bytes accessed | tf_op | source)
XLA Modules:
  0.0 95.2 jit_solution(16382209588105417022)
XLA Ops:
  0.6 1.0 %fusion = (f32[5,8,3,128]{3,2,1,0:T(4,128)S(1)}, f32[5,8,3,128]{3,2,1,0:T(4,128)S(1)}) fusion(f32[5,8,64,128]{3,2,1,0:T(8,128)} %fluid_ref.1), kind=kLoop, calls=%fused_computation.2 | loop fusion | bytes 245760 | tf_op jit(solution)/shard_map/slice | solution.py:429
  1.7 4.0 %collective-permute-start.1 = (f32[3,5,8,128]{3,2,1,0:T(8,128)S(1)}, f32[3,5,8,128]{3,2,1,0:T(8,128)S(1)}, u32[]{:S(2)}, u32[]{:S(2)}) collective-permute-start(f32[3,5,8,128]{3,2,1,0:T(8,128)S(1)} %get-tuple-element.20), channel_id=1, source_target_pairs={{16,32},{32,16},{48,64},{64,48},{80,96},{96,80},{112,128},{128,112... | collective-permute-start | bytes 184328 | tf_op jit(solution)/shard_map/ppermute | solution.py:436
  5.7 1.9 %collective-permute-start = (f32[3,5,8,128]{3,2,1,0:T(8,128)S(1)}, f32[3,5,8,128]{3,2,1,0:T(8,128)S(1)}, u32[]{:S(2)}, u32[]{:S(2)}) collective-permute-start(f32[3,5,8,128]{3,2,1,0:T(8,128)S(1)} %get-tuple-element.21), channel_id=1, source_target_pairs={{0,16},{16,0},{32,48},{48,32},{64,80},{80,64},{96,112},{112,96},{1... | collective-permute-start | bytes 184328 | tf_op jit(solution)/shard_map/ppermute | solution.py:435
  7.6 1.3 %stage.1.fluid_ref = f32[5,8,64,128]{3,2,1,0:T(8,128)S(1)} custom-call(f32[5,8,64,128]{3,2,1,0:T(8,128)} %fluid_ref.1), custom_call_target="tpu_custom_call" | custom-call | bytes 2700000 | tf_op jit(solution)/shard_map/stage/pallas_call | solution.py:166
  9.0 0.4 collective-permute-done.1.outer_ref
  9.3 0.0 collective-permute-done.inner_ref
  9.3 2.9 %sweep_y.1.middle_ref = f32[16,5,32,128]{3,2,1,0:T(8,128)} custom-call(f32[5,8,64,128]{3,2,1,0:T(8,128)S(1)} %stage.1.fluid_ref, f32[3,5,8,128]{3,2,1,0:T(8,128)S(1)} %collective-permute-done.inner_ref, f32[3,5,8,128]{3,2,1,0:T(8,128)S(1)} %collective-permute-done.1.outer_ref), custom_call_target="tpu_custom_call" | custom-call | flops 20000000 | bytes 2700000 | tf_op jit(solution)/shard_map/sweep_y/pallas_call | solution.py:181
  12.3 0.0 copy-start
  12.3 0.0 copy-start.1
  12.3 0.0 copy-start.2
  12.3 0.0 copy-start.3
  12.3 15.3 %all-to-all-start = ((f32[16,5,32,128]{3,2,1,0:T(8,128)}), f32[16,5,32,128]{3,2,1,0:T(8,128)S(1)}, u32[]{:S(2)}, u32[]{:S(2)}) async-start(f32[16,5,32,128]{3,2,1,0:T(8,128)} %sweep_y.1.middle_ref), calls=%async_computation | async-start | bytes 2621440 | tf_op jit(solution)/shard_map/all_to_all | solution.py:438
  27.7 0.0 copy-done
  27.7 0.0 copy-done.1
  27.7 0.0 copy-done.2
  27.7 0.0 copy-done.3
  27.7 11.1 %inner_samples.1 = (f32[16,128]{1,0:T(8,128)S(1)}, s32[16,128]{1,0:T(8,128)S(1)}, s32[16,128]{1,0:T(8,128)S(1)}, f32[9,5,8,128]{3,2,1,0:T(8,128)S(1)}, f32[2,5,8...) custom-call(s32[16]{0:T(128)S(1)} %bitcast.11, s32[16]{0:T(128)S(1)} %bitcast.12, ...), custom_call_target="tpu_custom_call" | custom-call | flops 20000000 | bytes 1600000 | tf_op jit(solution)/shard_map/inner_samples/pallas_call | solution.py:399
  38.8 3.8 %collective-permute-start.2 = (f32[2,5,8,128]{3,2,1,0:T(8,128)S(1)}, f32[2,5,8,128]{3,2,1,0:T(8,128)S(1)}, u32[]{:S(2)}, u32[]{:S(2)}) collective-permute-start(f32[2,5,8,128]{3,2,1,0:T(8,128)S(1)} %get-tuple-element.14), channel_id=1, source_target_pairs={{0,1},{1,2},{2,3},{3,4},{4,5},{5,6},{6,7},{7,8},{8,9},{9,10},{10,1... | collective-permute-start | bytes 122888 | tf_op jit(solution)/shard_map/ppermute | solution.py:423
  42.7 3.2 %collective-permute-start.3 = (f32[2,5,8,128]{3,2,1,0:T(8,128)S(1)}, f32[2,5,8,128]{3,2,1,0:T(8,128)S(1)}, u32[]{:S(2)}, u32[]{:S(2)}) collective-permute-start(f32[2,5,8,128]{3,2,1,0:T(8,128)S(1)} %get-tuple-element.15), channel_id=1, source_target_pairs={{0,15},{1,0},{2,1},{3,2},{4,3},{5,4},{6,5},{7,6},{8,7},{9,8},{10,9... | collective-permute-start | bytes 122888 | tf_op jit(solution)/shard_map/ppermute | solution.py:423
  45.9 42.3 %collective-permute-done.2.below_ref = f32[2,5,8,128]{3,2,1,0:T(8,128)S(1)} collective-permute-done((f32[2,5,8,128]{3,2,1,0:T(8,128)S(1)}, f32[2,5,8,128]{3,2,1,0:T(8,128)S(1)}, u32[]{:S(2)}, u32[]{:S(2)}) %collective-permute-start.2) | collective-permute-done | bytes 40992 | tf_op jit(solution)/shard_map/ppermute | solution.py:423
  88.2 0.0 collective-permute-done.3.above_ref
  88.2 3.3 %all-to-all-done.lines_ref = f32[16,5,32,128]{3,2,1,0:T(8,128)S(1)} async-done(((f32[16,5,32,128]{3,2,1,0:T(8,128)}), f32[16,5,32,128]{3,2,1,0:T(8,128)S(1)}, u32[]{:S(2)}, u32[]{:S(2)}) %all-to-all-start) | async-done | bytes 1310752 | tf_op jit(solution)/shard_map/all_to_all | solution.py:438
  91.5 3.6 %sweep_z.1 = (f32[5,8,4,2048]{3,2,1,0:T(4,128)}, f32[16,128]{1,0:T(8,128)}) custom-call(f32[16,5,32,128]{3,2,1,0:T(8,128)S(1)} %all-to-all-done.lines_ref, f32[16,128]{1,0:T(8,128)S(1)} %get-tuple-element.10.floor_ref, s32[16,128]{1,0:T(8,128)S(1)} %get-tuple-element.11.ids_ref, s32[16,128]{1,0:T(8,128)S(1)} %get-tuple-element.12.code_ref, ...), custom_call_target="tpu_custom_call" | custom-call | flops 20000000 | bytes 2700000 | tf_op jit(solution)/shard_map/sweep_z/pallas_call | solution.py:297
  (1 shorter events, 0.0 us)
Async XLA Ops:
  1.7 7.7 %collective-permute-start.1 = (f32[3,5,8,128]{3,2,1,0:T(8,128)S(1)}, f32[3,5,8,128]{3,2,1,0:T(8,128)S(1)}, u32[]{:S(2)}, u32[]{:S(2)}) collective-permute-start(f32[3,5,8,128]{3,2,1,0:T(8,128)S(1)} %get-tuple-element.20), channel_id=1, source_target_pairs={{16,32},{32,16},{48,64},{64,48},{80,96},{96,80},{112,128},{128,112... | collective-permute-start | bytes 184328 | tf_op jit(solution)/shard_map/ppermute | solution.py:436
  5.7 3.7 %collective-permute-start = (f32[3,5,8,128]{3,2,1,0:T(8,128)S(1)}, f32[3,5,8,128]{3,2,1,0:T(8,128)S(1)}, u32[]{:S(2)}, u32[]{:S(2)}) collective-permute-start(f32[3,5,8,128]{3,2,1,0:T(8,128)S(1)} %get-tuple-element.21), channel_id=1, source_target_pairs={{0,16},{16,0},{32,48},{48,32},{64,80},{80,64},{96,112},{112,96},{1... | collective-permute-start | bytes 184328 | tf_op jit(solution)/shard_map/ppermute | solution.py:435
  12.3 15.4 %copy-start = (s32[1,1,16,128]{3,2,1,0:T(8,128)S(1)}, s32[1,1,16,128]{3,2,1,0:T(8,128)}, u32[]{:S(2)}) copy-start(s32[1,1,16,128]{3,2,1,0:T(8,128)} %param.6) | copy-start | bytes 24580
  12.3 15.4 %copy-start.1 = (f32[1,1,16,128]{3,2,1,0:T(8,128)S(1)}, f32[1,1,16,128]{3,2,1,0:T(8,128)}, u32[]{:S(2)}) copy-start(f32[1,1,16,128]{3,2,1,0:T(8,128)} %param.9) | copy-start | bytes 24580
  12.3 15.4 %copy-start.2 = (s32[1,1,16]{2,1,0:T(1,128)S(1)}, s32[1,1,16]{2,1,0:T(1,128)}, u32[]{:S(2)}) copy-start(s32[1,1,16]{2,1,0:T(1,128)} %param.7) | copy-start | bytes 196
  12.3 15.4 %copy-start.3 = (s32[1,1,16]{2,1,0:T(1,128)S(1)}, s32[1,1,16]{2,1,0:T(1,128)}, u32[]{:S(2)}) copy-start(s32[1,1,16]{2,1,0:T(1,128)} %param.8) | copy-start | bytes 196
  12.3 79.2 %all-to-all-start = ((f32[16,5,32,128]{3,2,1,0:T(8,128)}), f32[16,5,32,128]{3,2,1,0:T(8,128)S(1)}, u32[]{:S(2)}, u32[]{:S(2)}) async-start(f32[16,5,32,128]{3,2,1,0:T(8,128)} %sweep_y.1.middle_ref), calls=%async_computation | async-start | bytes 2621440 | tf_op jit(solution)/shard_map/all_to_all | solution.py:438
  38.8 49.4 %collective-permute-start.2 = (f32[2,5,8,128]{3,2,1,0:T(8,128)S(1)}, f32[2,5,8,128]{3,2,1,0:T(8,128)S(1)}, u32[]{:S(2)}, u32[]{:S(2)}) collective-permute-start(f32[2,5,8,128]{3,2,1,0:T(8,128)S(1)} %get-tuple-element.14), channel_id=1, source_target_pairs={{0,1},{1,2},{2,3},{3,4},{4,5},{5,6},{6,7},{7,8},{8,9},{9,10},{10,1... | collective-permute-start | bytes 122888 | tf_op jit(solution)/shard_map/ppermute | solution.py:423
  42.7 45.5 %collective-permute-start.3 = (f32[2,5,8,128]{3,2,1,0:T(8,128)S(1)}, f32[2,5,8,128]{3,2,1,0:T(8,128)S(1)}, u32[]{:S(2)}, u32[]{:S(2)}) collective-permute-start(f32[2,5,8,128]{3,2,1,0:T(8,128)S(1)} %get-tuple-element.15), channel_id=1, source_target_pairs={{0,15},{1,0},{2,1},{3,2},{4,3},{5,4},{6,5},{7,6},{8,7},{9,8},{10,9... | collective-permute-start | bytes 122888 | tf_op jit(solution)/shard_map/ppermute | solution.py:423

commit v6 on v5

--- a/solution.py
+++ b/solution.py
@@ -224,8 +224,8 @@
         peak_ref[j : j + 1, :] = jnp.maximum(floor_ref[j : j + 1, :], raised)
 
 
-def sweep_z_kernel(lines_ref, floor_ref, ids_ref, code_ref, own_ref, below_ref, above_ref, out_ref, peaks_ref,
-                   face_ref, left_ref, right_ref, flux_ref, new_ref, peak_ref, out_sem, peak_sem):
+def sweep_z_kernel(lines_ref, floor_ref, ids_ref, code_ref, own_ref, below_ref, above_ref, band_ref,
+                   out_ref, peaks_ref, mid_ref, face_ref, left_ref, right_ref, flux_ref, new_ref, peak_ref, out_sem, peak_sem):
     tiles, _, rows, _ = lines_ref.shape
     steps = rows // 8
     lane = lax.broadcasted_iota(jnp.int32, (8, LANES), 1)
@@ -240,14 +240,38 @@
         for k in range(5):
             ref[q % 2, t, k] = values[k]
 
+    def halves(values):
+        high = values.astype(jnp.bfloat16)
+        return high, (values - high.astype(jnp.float32)).astype(jnp.bfloat16)
+
+    def stage_mid(q):
+        wide = lax.broadcasted_iota(jnp.int32, (8 * tiles, LANES), 1)
+        rows_x, rows_b = [], []
+        for k in range(5):
+            here = jnp.concatenate([lines_ref[t, k, 8 * q : 8 * q + 8, :] for t in range(tiles)], axis=0)
+            before = jnp.concatenate([here[-8:], here[:-8]], axis=0)
+            following = jnp.concatenate([here[8:], here[:8]], axis=0)
+            rows_x.append(here)
+            rows_b.append(jnp.where(wide == LANES - 1, before, following))
+        x_high, x_low = halves(jnp.concatenate(rows_x, axis=0))
+        b_high, b_low = halves(jnp.concatenate(rows_b, axis=0))
+        mid_ref[q % 2] = jnp.dot(
+            jnp.concatenate([x_high, b_high, x_low, b_low], axis=1),
+            band_ref[...],
+            preferred_element_type=jnp.float32,
+        )
+
     def stage_face(q, t):
-        before, here, following = [cell(q, t + d) for d in (-1, 0, 1)]
-        second = [
-            pltpu.roll(jnp.where(lane < 2, f, h), LANES - 2, 1) for h, f in zip(here, following)
-        ]
-        put(face_ref, q, t, face_of(
-            lane_before(here, before, lane), here, lane_after(here, following, lane), second
-        ))
+        here = cell(q, t)
+        found = []
+        for k in range(5):
+            part = pl.ds(8 * (k * tiles + t), 8)
+            mid = (1.0 / 12.0) * mid_ref[q % 2, part, :LANES]
+            after = mid_ref[q % 2, part, LANES:]
+            found.append(
+                jnp.minimum(jnp.maximum(mid, jnp.minimum(here[k], after)), jnp.maximum(here[k], after))
+            )
+        put(face_ref, q, t, found)
 
     def stage_edges(q, t):
         face = get(face_ref, q, t)
@@ -272,7 +296,10 @@
     outer_peaks(floor_ref, ids_ref, code_ref, own_ref, below_ref, above_ref, peak_ref)
     sent = [pltpu.make_async_copy(peak_ref, peaks_ref, peak_sem)]
     stages = (stage_face, stage_edges, stage_flux, stage_new)
+    stage_mid(0)
     for step in range(steps + 3):
+        if step + 1 < steps:
+            stage_mid(step + 1)
         for start in range(0, tiles, 4):
             for age, stage in enumerate(stages):
                 q = step - age
@@ -291,7 +318,7 @@
         copy.wait()
 
 
-def sweep_z(lines, floor, ids, code, own, below, above, nx):
+def sweep_z(lines, floor, ids, code, own, below, above, band, nx):
     tiles, _, rows, _ = lines.shape
     shape = (5, nx, rows // nx, tiles * LANES)
     return pl.pallas_call(
@@ -300,9 +327,10 @@
             jax.ShapeDtypeStruct(shape, jnp.float32),
             jax.ShapeDtypeStruct(floor.shape, jnp.float32),
         ),
-        in_specs=[pl.BlockSpec(memory_space=pltpu.VMEM)] * 7,
+        in_specs=[pl.BlockSpec(memory_space=pltpu.VMEM)] * 8,
         out_specs=(pl.BlockSpec(memory_space=pl.ANY),) * 2,
-        scratch_shapes=[pltpu.VMEM((2, tiles, 5, 8, LANES), jnp.float32)] * 4
+        scratch_shapes=[pltpu.VMEM((2, 5 * 8 * tiles, 2 * LANES), jnp.float32)]
+        + [pltpu.VMEM((2, tiles, 5, 8, LANES), jnp.float32)] * 4
         + [
             pltpu.VMEM(shape, jnp.float32),
             pltpu.VMEM(floor.shape, jnp.float32),
@@ -314,7 +342,7 @@
             flops=20_000_000, bytes_accessed=2_700_000, transcendentals=0
         ),
         name="sweep_z",
-    )(lines, floor, ids, code, own, below, above)
+    )(lines, floor, ids, code, own, below, above, band)
 
 
 def lines_of(states):
@@ -331,8 +359,22 @@
     return [updated(s, before(f), f) for s, f in zip(states, fluxes)]
 
 
+def band_matrix():
+    source = lax.broadcasted_iota(jnp.int32, (4 * LANES, 2 * LANES), 0) % (2 * LANES)
+    target = lax.broadcasted_iota(jnp.int32, (4 * LANES, 2 * LANES), 1)
+    beside = source >= LANES
+    cell = jnp.where(beside, source - LANES, source)
+    cell = jnp.where(beside, jnp.where(cell == LANES - 1, -1, cell + LANES), cell)
+    used = jnp.logical_not(beside) | (cell < LANES + 2)
+    faces = target < LANES
+    step = cell - jnp.where(faces, target, target - LANES)
+    face = jnp.where((step == 0) | (step == 1), 7.0, jnp.where((step == -1) | (step == 2), -1.0, 0.0))
+    value = jnp.where(faces, face, jnp.where(step == 1, 1.0, 0.0))
+    return jnp.where(used, value, 0.0).astype(jnp.bfloat16)
+
+
 def inner_kernel(owner_ref, count_ref, middle_ref, cell_ref, peak_ref, floor_ref, ids_ref, code_ref, own_ref,
-                 up_ref, down_ref, press_ref):
+                 up_ref, down_ref, band_ref, press_ref):
     blocks, _, rows, _ = middle_ref.shape
     lane = lax.broadcasted_iota(jnp.int32, (8, LANES), 1)
     lower = lane < LANES // 2
@@ -372,6 +414,7 @@
         down_ref[0, k] = jnp.where(lower, own[4], turned[0])
         up_ref[1, k] = turned[1]
         down_ref[1, k] = turned[1]
+    band_ref[...] = band_matrix()
     row_ids = lax.broadcasted_iota(jnp.int32, (rows, LANES), 0)
     slot = lax.broadcasted_iota(jnp.int32, (1, LANES), 1)
     for j in range(blocks):
@@ -405,10 +448,11 @@
             jax.ShapeDtypeStruct((9, 5, 8, LANES), jnp.float32),
             jax.ShapeDtypeStruct((2, 5, 8, LANES), jnp.float32),
             jax.ShapeDtypeStruct((2, 5, 8, LANES), jnp.float32),
+            jax.ShapeDtypeStruct((4 * LANES, 2 * LANES), jnp.bfloat16),
         ),
         in_specs=[pl.BlockSpec(memory_space=pltpu.SMEM)] * 2
         + [pl.BlockSpec(memory_space=pltpu.VMEM)] * 3,
-        out_specs=(pl.BlockSpec(memory_space=pltpu.VMEM),) * 6,
+        out_specs=(pl.BlockSpec(memory_space=pltpu.VMEM),) * 7,
         scratch_shapes=[pltpu.VMEM((blocks, rows, LANES), jnp.float32)],
         compiler_params=pltpu.CompilerParams(vmem_limit_bytes=16 * 1024 * 1024),
         cost_estimate=pl.CostEstimate(
@@ -436,12 +480,12 @@
     got_outer = lax.ppermute(jnp.where(odd, tail, head), "gy", outer)
     middle = sweep_y(staged(fluid_state), got_inner, got_outer, blocks)
     lines = lax.all_to_all(middle, "gz", split_axis=0, concat_axis=0, tiled=True)
-    floor, ids, code, own, up, down = inner_samples(
+    floor, ids, code, own, up, down, band = inner_samples(
         tracer_owner[0, 0], tracer_count[0, 0], middle, tracer_cell[0, 0], tracer_peak[0, 0]
     )
     above = shifted(down, "gz", -1)
     below = shifted(up, "gz", 1)
-    new_state, new_peak = sweep_z(lines, floor, ids, code, own, below, above, nx)
+    new_state, new_peak = sweep_z(lines, floor, ids, code, own, below, above, band, nx)
     return (new_state, new_peak[None, None])
 
 

time: 95.6 us -> 95.3 us (level)
  the two profiles are of different devices: /device:TPU:16 before, /device:TPU:8 now
where the time goes in v6:
time: 95.3 us; the launch traced here: 94.9 us
  waiting for transfers between devices  45.9 us (48%)
  starting transfers between devices  28.3 us (30%)
  Pallas kernels  18.8 us (20%)
  local copies, waits for them, and re-layouts  1.06 us (1%)
    ppermute x2, waiting for transfers between devices, shifted(): lax.ppermute(values, axis, [(i, (i + step) % count) for i in range(count)])  42.1 us
    all_to_all x1, starting transfers between devices, on_device(): lax.all_to_all(middle, 'gz', split_axis=0, concat_axis=0, tiled=True)  15.3 us
    pallas_call x1, Pallas kernels, inner_samples(): pl.pallas_call(inner_kernel, out_shape=(jax.ShapeDtypeStruct(cells.shape,...  11.3 us
    ppermute x2, starting transfers between devices, shifted(): lax.ppermute(values, axis, [(i, (i + step) % count) for i in range(count)])  7.05 us
    ppermute x1, starting transfers between devices, on_device(): got_outer = lax.ppermute(jnp.where(odd, tail, head), 'gy', outer)  3.99 us
    pallas_call x1, Pallas kernels, sweep_z(): pl.pallas_call(sweep_z_kernel, out_shape=(jax.ShapeDtypeStruct(shape, jnp...  3.34 us
    all_to_all x1, waiting for transfers between devices, on_device(): lax.all_to_all(middle, 'gz', split_axis=0, concat_axis=0, tiled=True)  3.32 us
    pallas_call x1, Pallas kernels, sweep_y(): pl.pallas_call(sweep_y_kernel, out_shape=jax.ShapeDtypeStruct((blocks, 5,...  2.92 us
  transfers between devices with their start and end apart: 5, of which 3 were waited for; matrix products, arithmetic and copies ran while one was open for 0% of the time, Pallas kernels for 13%

profile of v6, /device:TPU:8, one launch (start us, length us, event | category | flops | bytes accessed | tf_op | source)
XLA Modules:
  0.0 94.9 jit_solution(1271498002715912762)
XLA Ops:
  0.6 1.0 %fusion = (f32[5,8,3,128]{3,2,1,0:T(4,128)S(1)}, f32[5,8,3,128]{3,2,1,0:T(4,128)S(1)}) fusion(f32[5,8,64,128]{3,2,1,0:T(8,128)} %fluid_ref.1), kind=kLoop, calls=%fused_computation.2 | loop fusion | bytes 245760 | tf_op jit(solution)/shard_map/slice | solution.py:473
  1.7 4.0 %collective-permute-start.1 = (f32[3,5,8,128]{3,2,1,0:T(8,128)S(1)}, f32[3,5,8,128]{3,2,1,0:T(8,128)S(1)}, u32[]{:S(2)}, u32[]{:S(2)}) collective-permute-start(f32[3,5,8,128]{3,2,1,0:T(8,128)S(1)} %get-tuple-element.22), channel_id=1, source_target_pairs={{16,32},{32,16},{48,64},{64,48},{80,96},{96,80},{112,128},{128,112... | collective-permute-start | bytes 184328 | tf_op jit(solution)/shard_map/ppermute | solution.py:480
  5.7 1.9 %collective-permute-start = (f32[3,5,8,128]{3,2,1,0:T(8,128)S(1)}, f32[3,5,8,128]{3,2,1,0:T(8,128)S(1)}, u32[]{:S(2)}, u32[]{:S(2)}) collective-permute-start(f32[3,5,8,128]{3,2,1,0:T(8,128)S(1)} %get-tuple-element.23), channel_id=1, source_target_pairs={{0,16},{16,0},{32,48},{48,32},{64,80},{80,64},{96,112},{112,96},{1... | collective-permute-start | bytes 184328 | tf_op jit(solution)/shard_map/ppermute | solution.py:479
  7.6 1.3 %stage.1.fluid_ref = f32[5,8,64,128]{3,2,1,0:T(8,128)S(1)} custom-call(f32[5,8,64,128]{3,2,1,0:T(8,128)} %fluid_ref.1), custom_call_target="tpu_custom_call" | custom-call | bytes 2700000 | tf_op jit(solution)/shard_map/stage/pallas_call | solution.py:166
  9.0 0.4 collective-permute-done.1.outer_ref
  9.3 0.0 collective-permute-done.inner_ref
  9.3 2.9 %sweep_y.1.middle_ref = f32[16,5,32,128]{3,2,1,0:T(8,128)} custom-call(f32[5,8,64,128]{3,2,1,0:T(8,128)S(1)} %stage.1.fluid_ref, f32[3,5,8,128]{3,2,1,0:T(8,128)S(1)} %collective-permute-done.inner_ref, f32[3,5,8,128]{3,2,1,0:T(8,128)S(1)} %collective-permute-done.1.outer_ref), custom_call_target="tpu_custom_call" | custom-call | flops 20000000 | bytes 2700000 | tf_op jit(solution)/shard_map/sweep_y/pallas_call | solution.py:181
  12.3 0.0 copy-start
  12.3 0.0 copy-start.1
  12.3 0.0 copy-start.2
  12.3 0.0 copy-start.3
  12.3 15.3 %all-to-all-start = ((f32[16,5,32,128]{3,2,1,0:T(8,128)}), f32[16,5,32,128]{3,2,1,0:T(8,128)S(1)}, u32[]{:S(2)}, u32[]{:S(2)}) async-start(f32[16,5,32,128]{3,2,1,0:T(8,128)} %sweep_y.1.middle_ref), calls=%async_computation | async-start | bytes 2621440 | tf_op jit(solution)/shard_map/all_to_all | solution.py:482
  27.7 0.0 copy-done
  27.7 0.0 copy-done.1
  27.7 0.0 copy-done.2
  27.7 0.0 copy-done.3
  27.7 11.3 %inner_samples.1 = (f32[16,128]{1,0:T(8,128)S(1)}, s32[16,128]{1,0:T(8,128)S(1)}, s32[16,128]{1,0:T(8,128)S(1)}, f32[9,5,8,128]{3,2,1,0:T(8,128)S(1)}, f32[2,5,8...) custom-call(s32[16]{0:T(128)S(1)} %bitcast.11, s32[16]{0:T(128)S(1)} %bitcast.12, ...), custom_call_target="tpu_custom_call" | custom-call | flops 20000000 | bytes 1600000 | tf_op jit(solution)/shard_map/inner_samples/pallas_call | solution.py:442
  39.0 3.8 %collective-permute-start.2 = (f32[2,5,8,128]{3,2,1,0:T(8,128)S(1)}, f32[2,5,8,128]{3,2,1,0:T(8,128)S(1)}, u32[]{:S(2)}, u32[]{:S(2)}) collective-permute-start(f32[2,5,8,128]{3,2,1,0:T(8,128)S(1)} %get-tuple-element.15), channel_id=1, source_target_pairs={{0,1},{1,2},{2,3},{3,4},{4,5},{5,6},{6,7},{7,8},{8,9},{9,10},{10,1... | collective-permute-start | bytes 122888 | tf_op jit(solution)/shard_map/ppermute | solution.py:467
  42.8 3.2 %collective-permute-start.3 = (f32[2,5,8,128]{3,2,1,0:T(8,128)S(1)}, f32[2,5,8,128]{3,2,1,0:T(8,128)S(1)}, u32[]{:S(2)}, u32[]{:S(2)}) collective-permute-start(f32[2,5,8,128]{3,2,1,0:T(8,128)S(1)} %get-tuple-element.16), channel_id=1, source_target_pairs={{0,15},{1,0},{2,1},{3,2},{4,3},{5,4},{6,5},{7,6},{8,7},{9,8},{10,9... | collective-permute-start | bytes 122888 | tf_op jit(solution)/shard_map/ppermute | solution.py:467
  46.1 42.1 %collective-permute-done.2.below_ref = f32[2,5,8,128]{3,2,1,0:T(8,128)S(1)} collective-permute-done((f32[2,5,8,128]{3,2,1,0:T(8,128)S(1)}, f32[2,5,8,128]{3,2,1,0:T(8,128)S(1)}, u32[]{:S(2)}, u32[]{:S(2)}) %collective-permute-start.2) | collective-permute-done | bytes 40992 | tf_op jit(solution)/shard_map/ppermute | solution.py:467
  88.2 0.0 collective-permute-done.3.above_ref
  88.2 3.3 %all-to-all-done.lines_ref = f32[16,5,32,128]{3,2,1,0:T(8,128)S(1)} async-done(((f32[16,5,32,128]{3,2,1,0:T(8,128)}), f32[16,5,32,128]{3,2,1,0:T(8,128)S(1)}, u32[]{:S(2)}, u32[]{:S(2)}) %all-to-all-start) | async-done | bytes 1310752 | tf_op jit(solution)/shard_map/all_to_all | solution.py:482
  91.5 3.3 %sweep_z.1 = (f32[5,8,4,2048]{3,2,1,0:T(4,128)}, f32[16,128]{1,0:T(8,128)}) custom-call(f32[16,5,32,128]{3,2,1,0:T(8,128)S(1)} %all-to-all-done.lines_ref, f32[16,128]{1,0:T(8,128)S(1)} %get-tuple-element.11.floor_ref, s32[16,128]{1,0:T(8,128)S(1)} %get-tuple-element.12.ids_ref, s32[16,128]{1,0:T(8,128)S(1)} %get-tuple-element.13.code_ref, ...), custom_call_target="tpu_custom_call" | custom-call | flops 20000000 | bytes 2700000 | tf_op jit(solution)/shard_map/sweep_z/pallas_call | solution.py:324
  (1 shorter events, 0.0 us)
Async XLA Ops:
  1.7 7.7 %collective-permute-start.1 = (f32[3,5,8,128]{3,2,1,0:T(8,128)S(1)}, f32[3,5,8,128]{3,2,1,0:T(8,128)S(1)}, u32[]{:S(2)}, u32[]{:S(2)}) collective-permute-start(f32[3,5,8,128]{3,2,1,0:T(8,128)S(1)} %get-tuple-element.22), channel_id=1, source_target_pairs={{16,32},{32,16},{48,64},{64,48},{80,96},{96,80},{112,128},{128,112... | collective-permute-start | bytes 184328 | tf_op jit(solution)/shard_map/ppermute | solution.py:480
  5.7 3.7 %collective-permute-start = (f32[3,5,8,128]{3,2,1,0:T(8,128)S(1)}, f32[3,5,8,128]{3,2,1,0:T(8,128)S(1)}, u32[]{:S(2)}, u32[]{:S(2)}) collective-permute-start(f32[3,5,8,128]{3,2,1,0:T(8,128)S(1)} %get-tuple-element.23), channel_id=1, source_target_pairs={{0,16},{16,0},{32,48},{48,32},{64,80},{80,64},{96,112},{112,96},{1... | collective-permute-start | bytes 184328 | tf_op jit(solution)/shard_map/ppermute | solution.py:479
  12.3 15.4 %copy-start = (s32[1,1,16,128]{3,2,1,0:T(8,128)S(1)}, s32[1,1,16,128]{3,2,1,0:T(8,128)}, u32[]{:S(2)}) copy-start(s32[1,1,16,128]{3,2,1,0:T(8,128)} %param.6) | copy-start | bytes 24580
  12.3 15.4 %copy-start.1 = (f32[1,1,16,128]{3,2,1,0:T(8,128)S(1)}, f32[1,1,16,128]{3,2,1,0:T(8,128)}, u32[]{:S(2)}) copy-start(f32[1,1,16,128]{3,2,1,0:T(8,128)} %param.9) | copy-start | bytes 24580
  12.3 15.4 %copy-start.2 = (s32[1,1,16]{2,1,0:T(1,128)S(1)}, s32[1,1,16]{2,1,0:T(1,128)}, u32[]{:S(2)}) copy-start(s32[1,1,16]{2,1,0:T(1,128)} %param.7) | copy-start | bytes 196
  12.3 15.4 %copy-start.3 = (s32[1,1,16]{2,1,0:T(1,128)S(1)}, s32[1,1,16]{2,1,0:T(1,128)}, u32[]{:S(2)}) copy-start(s32[1,1,16]{2,1,0:T(1,128)} %param.8) | copy-start | bytes 196
  12.3 79.2 %all-to-all-start = ((f32[16,5,32,128]{3,2,1,0:T(8,128)}), f32[16,5,32,128]{3,2,1,0:T(8,128)S(1)}, u32[]{:S(2)}, u32[]{:S(2)}) async-start(f32[16,5,32,128]{3,2,1,0:T(8,128)} %sweep_y.1.middle_ref), calls=%async_computation | async-start | bytes 2621440 | tf_op jit(solution)/shard_map/all_to_all | solution.py:482
  39.0 49.2 %collective-permute-start.2 = (f32[2,5,8,128]{3,2,1,0:T(8,128)S(1)}, f32[2,5,8,128]{3,2,1,0:T(8,128)S(1)}, u32[]{:S(2)}, u32[]{:S(2)}) collective-permute-start(f32[2,5,8,128]{3,2,1,0:T(8,128)S(1)} %get-tuple-element.15), channel_id=1, source_target_pairs={{0,1},{1,2},{2,3},{3,4},{4,5},{5,6},{6,7},{7,8},{8,9},{9,10},{10,1... | collective-permute-start | bytes 122888 | tf_op jit(solution)/shard_map/ppermute | solution.py:467
  42.8 45.4 %collective-permute-start.3 = (f32[2,5,8,128]{3,2,1,0:T(8,128)S(1)}, f32[2,5,8,128]{3,2,1,0:T(8,128)S(1)}, u32[]{:S(2)}, u32[]{:S(2)}) collective-permute-start(f32[2,5,8,128]{3,2,1,0:T(8,128)S(1)} %get-tuple-element.16), channel_id=1, source_target_pairs={{0,15},{1,0},{2,1},{3,2},{4,3},{5,4},{6,5},{7,6},{8,7},{9,8},{10,9... | collective-permute-start | bytes 122888 | tf_op jit(solution)/shard_map/ppermute | solution.py:467

commit v7 on v6

--- a/solution.py
+++ b/solution.py
@@ -200,8 +200,10 @@
     lower = lane < LANES // 2
 
     def ends(ref, k):
-        first = ref[0, k]
-        return [first, pltpu.roll(first, LANES // 2, 1), ref[1, k]]
+        first, third = ref[k], ref[5 + k // 2]
+        if k % 2 == 1:
+            third = pltpu.roll(third, LANES // 2, 1)
+        return [first, pltpu.roll(first, LANES // 2, 1), third]
 
     states = [[own_ref[j, k] for k in range(5)] for j in range(9)]
     for k in range(5):
@@ -410,10 +412,15 @@
         for j in range(9):
             own_ref[j, k] = own[j]
         turned = [pltpu.roll(v, LANES // 2, 1) for v in (own[3], own[5])]
-        up_ref[0, k] = jnp.where(lower, turned[0], own[4])
-        down_ref[0, k] = jnp.where(lower, own[4], turned[0])
-        up_ref[1, k] = turned[1]
-        down_ref[1, k] = turned[1]
+        up_ref[k] = jnp.where(lower, turned[0], own[4])
+        down_ref[k] = jnp.where(lower, own[4], turned[0])
+        if k % 2 == 0:
+            even = turned[1]
+            up_ref[5 + k // 2] = even
+            down_ref[5 + k // 2] = even
+        else:
+            up_ref[5 + k // 2] = jnp.where(lower, even, own[5])
+            down_ref[5 + k // 2] = jnp.where(lower, own[5], even)
     band_ref[...] = band_matrix()
     row_ids = lax.broadcasted_iota(jnp.int32, (rows, LANES), 0)
     slot = lax.broadcasted_iota(jnp.int32, (1, LANES), 1)
@@ -446,8 +453,8 @@
             jax.ShapeDtypeStruct(cells.shape, jnp.int32),
             jax.ShapeDtypeStruct(cells.shape, jnp.int32),
             jax.ShapeDtypeStruct((9, 5, 8, LANES), jnp.float32),
-            jax.ShapeDtypeStruct((2, 5, 8, LANES), jnp.float32),
-            jax.ShapeDtypeStruct((2, 5, 8, LANES), jnp.float32),
+            jax.ShapeDtypeStruct((8, 8, LANES), jnp.float32),
+            jax.ShapeDtypeStruct((8, 8, LANES), jnp.float32),
             jax.ShapeDtypeStruct((4 * LANES, 2 * LANES), jnp.bfloat16),
         ),
         in_specs=[pl.BlockSpec(memory_space=pltpu.SMEM)] * 2

time: 95.3 us -> 95.4 us (level)
  the two profiles are of different devices: /device:TPU:8 before, /device:TPU:16 now
where the time goes in v7:
time: 95.4 us; the launch traced here: 95 us
  waiting for transfers between devices  46 us (48%)
  starting transfers between devices  28.3 us (30%)
  Pallas kernels  18.9 us (20%)
  local copies, waits for them, and re-layouts  1.06 us (1%)
    ppermute x2, waiting for transfers between devices, shifted(): lax.ppermute(values, axis, [(i, (i + step) % count) for i in range(count)])  41.8 us
    all_to_all x1, starting transfers between devices, on_device(): lax.all_to_all(middle, 'gz', split_axis=0, concat_axis=0, tiled=True)  15.3 us
    pallas_call x1, Pallas kernels, inner_samples(): pl.pallas_call(inner_kernel, out_shape=(jax.ShapeDtypeStruct(cells.shape,...  11.3 us
    ppermute x2, starting transfers between devices, shifted(): lax.ppermute(values, axis, [(i, (i + step) % count) for i in range(count)])  7.05 us
    ppermute x1, starting transfers between devices, on_device(): got_outer = lax.ppermute(jnp.where(odd, tail, head), 'gy', outer)  3.99 us
    all_to_all x1, waiting for transfers between devices, on_device(): lax.all_to_all(middle, 'gz', split_axis=0, concat_axis=0, tiled=True)  3.78 us
    pallas_call x1, Pallas kernels, sweep_z(): pl.pallas_call(sweep_z_kernel, out_shape=(jax.ShapeDtypeStruct(shape, jnp...  3.35 us
    pallas_call x1, Pallas kernels, sweep_y(): pl.pallas_call(sweep_y_kernel, out_shape=jax.ShapeDtypeStruct((blocks, 5,...  2.92 us
  transfers between devices with their start and end apart: 5, of which 3 were waited for; matrix products, arithmetic and copies ran while one was open for 0% of the time, Pallas kernels for 13%

profile of v7, /device:TPU:16, one launch (start us, length us, event | category | flops | bytes accessed | tf_op | source)
XLA Modules:
  0.0 95.0 jit_solution(2347534066490977786)
XLA Ops:
  0.6 1.0 %fusion = (f32[5,8,3,128]{3,2,1,0:T(4,128)S(1)}, f32[5,8,3,128]{3,2,1,0:T(4,128)S(1)}) fusion(f32[5,8,64,128]{3,2,1,0:T(8,128)} %fluid_ref.1), kind=kLoop, calls=%fused_computation.2 | loop fusion | bytes 245760 | tf_op jit(solution)/shard_map/slice | solution.py:480
  1.7 4.0 %collective-permute-start.1 = (f32[3,5,8,128]{3,2,1,0:T(8,128)S(1)}, f32[3,5,8,128]{3,2,1,0:T(8,128)S(1)}, u32[]{:S(2)}, u32[]{:S(2)}) collective-permute-start(f32[3,5,8,128]{3,2,1,0:T(8,128)S(1)} %get-tuple-element.22), channel_id=1, source_target_pairs={{16,32},{32,16},{48,64},{64,48},{80,96},{96,80},{112,128},{128,112... | collective-permute-start | bytes 184328 | tf_op jit(solution)/shard_map/ppermute | solution.py:487
  5.7 1.9 %collective-permute-start = (f32[3,5,8,128]{3,2,1,0:T(8,128)S(1)}, f32[3,5,8,128]{3,2,1,0:T(8,128)S(1)}, u32[]{:S(2)}, u32[]{:S(2)}) collective-permute-start(f32[3,5,8,128]{3,2,1,0:T(8,128)S(1)} %get-tuple-element.23), channel_id=1, source_target_pairs={{0,16},{16,0},{32,48},{48,32},{64,80},{80,64},{96,112},{112,96},{1... | collective-permute-start | bytes 184328 | tf_op jit(solution)/shard_map/ppermute | solution.py:486
  7.6 1.3 %stage.1.fluid_ref = f32[5,8,64,128]{3,2,1,0:T(8,128)S(1)} custom-call(f32[5,8,64,128]{3,2,1,0:T(8,128)} %fluid_ref.1), custom_call_target="tpu_custom_call" | custom-call | bytes 2700000 | tf_op jit(solution)/shard_map/stage/pallas_call | solution.py:166
  9.0 0.4 collective-permute-done.1.outer_ref
  9.3 0.0 collective-permute-done.inner_ref
  9.3 2.9 %sweep_y.1.middle_ref = f32[16,5,32,128]{3,2,1,0:T(8,128)} custom-call(f32[5,8,64,128]{3,2,1,0:T(8,128)S(1)} %stage.1.fluid_ref, f32[3,5,8,128]{3,2,1,0:T(8,128)S(1)} %collective-permute-done.inner_ref, f32[3,5,8,128]{3,2,1,0:T(8,128)S(1)} %collective-permute-done.1.outer_ref), custom_call_target="tpu_custom_call" | custom-call | flops 20000000 | bytes 2700000 | tf_op jit(solution)/shard_map/sweep_y/pallas_call | solution.py:181
  12.3 0.0 copy-start
  12.3 0.0 copy-start.1
  12.3 0.0 copy-start.2
  12.3 0.0 copy-start.3
  12.3 15.3 %all-to-all-start = ((f32[16,5,32,128]{3,2,1,0:T(8,128)}), f32[16,5,32,128]{3,2,1,0:T(8,128)S(1)}, u32[]{:S(2)}, u32[]{:S(2)}) async-start(f32[16,5,32,128]{3,2,1,0:T(8,128)} %sweep_y.1.middle_ref), calls=%async_computation | async-start | bytes 2621440 | tf_op jit(solution)/shard_map/all_to_all | solution.py:489
  27.7 0.0 copy-done
  27.7 0.0 copy-done.1
  27.7 0.0 copy-done.2
  27.7 0.0 copy-done.3
  27.7 11.3 %inner_samples.1 = (f32[16,128]{1,0:T(8,128)S(1)}, s32[16,128]{1,0:T(8,128)S(1)}, s32[16,128]{1,0:T(8,128)S(1)}, f32[9,5,8,128]{3,2,1,0:T(8,128)S(1)}, f32[8,8,1...) custom-call(s32[16]{0:T(128)S(1)} %bitcast.11, s32[16]{0:T(128)S(1)} %bitcast.12, ...), custom_call_target="tpu_custom_call" | custom-call | flops 20000000 | bytes 1600000 | tf_op jit(solution)/shard_map/inner_samples/pallas_call | solution.py:449
  39.0 3.8 %collective-permute-start.2 = (f32[8,8,128]{2,1,0:T(8,128)S(1)}, f32[8,8,128]{2,1,0:T(8,128)S(1)}, u32[]{:S(2)}, u32[]{:S(2)}) collective-permute-start(f32[8,8,128]{2,1,0:T(8,128)S(1)} %get-tuple-element.15), channel_id=1, source_target_pairs={{0,1},{1,2},{2,3},{3,4},{4,5},{5,6},{6,7},{7,8},{8,9},{9,10},{10,1... | collective-permute-start | bytes 98312 | tf_op jit(solution)/shard_map/ppermute | solution.py:474
  42.8 3.2 %collective-permute-start.3 = (f32[8,8,128]{2,1,0:T(8,128)S(1)}, f32[8,8,128]{2,1,0:T(8,128)S(1)}, u32[]{:S(2)}, u32[]{:S(2)}) collective-permute-start(f32[8,8,128]{2,1,0:T(8,128)S(1)} %get-tuple-element.16), channel_id=1, source_target_pairs={{0,15},{1,0},{2,1},{3,2},{4,3},{5,4},{6,5},{7,6},{8,7},{9,8},{10,9... | collective-permute-start | bytes 98312 | tf_op jit(solution)/shard_map/ppermute | solution.py:474
  46.0 41.8 %collective-permute-done.2.below_ref = f32[8,8,128]{2,1,0:T(8,128)S(1)} collective-permute-done((f32[8,8,128]{2,1,0:T(8,128)S(1)}, f32[8,8,128]{2,1,0:T(8,128)S(1)}, u32[]{:S(2)}, u32[]{:S(2)}) %collective-permute-start.2) | collective-permute-done | bytes 32800 | tf_op jit(solution)/shard_map/ppermute | solution.py:474
  87.9 0.0 collective-permute-done.3.above_ref
  87.9 3.8 %all-to-all-done.lines_ref = f32[16,5,32,128]{3,2,1,0:T(8,128)S(1)} async-done(((f32[16,5,32,128]{3,2,1,0:T(8,128)}), f32[16,5,32,128]{3,2,1,0:T(8,128)S(1)}, u32[]{:S(2)}, u32[]{:S(2)}) %all-to-all-start) | async-done | bytes 1310752 | tf_op jit(solution)/shard_map/all_to_all | solution.py:489
  91.7 3.4 %sweep_z.1 = (f32[5,8,4,2048]{3,2,1,0:T(4,128)}, f32[16,128]{1,0:T(8,128)}) custom-call(f32[16,5,32,128]{3,2,1,0:T(8,128)S(1)} %all-to-all-done.lines_ref, f32[16,128]{1,0:T(8,128)S(1)} %get-tuple-element.11.floor_ref, s32[16,128]{1,0:T(8,128)S(1)} %get-tuple-element.12.ids_ref, s32[16,128]{1,0:T(8,128)S(1)} %get-tuple-element.13.code_ref, ...), custom_call_target="tpu_custom_call" | custom-call | flops 20000000 | bytes 2700000 | tf_op jit(solution)/shard_map/sweep_z/pallas_call | solution.py:326
  (1 shorter events, 0.0 us)
Async XLA Ops:
  1.7 7.7 %collective-permute-start.1 = (f32[3,5,8,128]{3,2,1,0:T(8,128)S(1)}, f32[3,5,8,128]{3,2,1,0:T(8,128)S(1)}, u32[]{:S(2)}, u32[]{:S(2)}) collective-permute-start(f32[3,5,8,128]{3,2,1,0:T(8,128)S(1)} %get-tuple-element.22), channel_id=1, source_target_pairs={{16,32},{32,16},{48,64},{64,48},{80,96},{96,80},{112,128},{128,112... | collective-permute-start | bytes 184328 | tf_op jit(solution)/shard_map/ppermute | solution.py:487
  5.7 3.7 %collective-permute-start = (f32[3,5,8,128]{3,2,1,0:T(8,128)S(1)}, f32[3,5,8,128]{3,2,1,0:T(8,128)S(1)}, u32[]{:S(2)}, u32[]{:S(2)}) collective-permute-start(f32[3,5,8,128]{3,2,1,0:T(8,128)S(1)} %get-tuple-element.23), channel_id=1, source_target_pairs={{0,16},{16,0},{32,48},{48,32},{64,80},{80,64},{96,112},{112,96},{1... | collective-permute-start | bytes 184328 | tf_op jit(solution)/shard_map/ppermute | solution.py:486
  12.3 15.4 %copy-start = (s32[1,1,16,128]{3,2,1,0:T(8,128)S(1)}, s32[1,1,16,128]{3,2,1,0:T(8,128)}, u32[]{:S(2)}) copy-start(s32[1,1,16,128]{3,2,1,0:T(8,128)} %param.6) | copy-start | bytes 24580
  12.3 15.4 %copy-start.1 = (f32[1,1,16,128]{3,2,1,0:T(8,128)S(1)}, f32[1,1,16,128]{3,2,1,0:T(8,128)}, u32[]{:S(2)}) copy-start(f32[1,1,16,128]{3,2,1,0:T(8,128)} %param.9) | copy-start | bytes 24580
  12.3 15.4 %copy-start.2 = (s32[1,1,16]{2,1,0:T(1,128)S(1)}, s32[1,1,16]{2,1,0:T(1,128)}, u32[]{:S(2)}) copy-start(s32[1,1,16]{2,1,0:T(1,128)} %param.7) | copy-start | bytes 196
  12.3 15.4 %copy-start.3 = (s32[1,1,16]{2,1,0:T(1,128)S(1)}, s32[1,1,16]{2,1,0:T(1,128)}, u32[]{:S(2)}) copy-start(s32[1,1,16]{2,1,0:T(1,128)} %param.8) | copy-start | bytes 196
  12.3 79.3 %all-to-all-start = ((f32[16,5,32,128]{3,2,1,0:T(8,128)}), f32[16,5,32,128]{3,2,1,0:T(8,128)S(1)}, u32[]{:S(2)}, u32[]{:S(2)}) async-start(f32[16,5,32,128]{3,2,1,0:T(8,128)} %sweep_y.1.middle_ref), calls=%async_computation | async-start | bytes 2621440 | tf_op jit(solution)/shard_map/all_to_all | solution.py:489
  39.0 48.9 %collective-permute-start.2 = (f32[8,8,128]{2,1,0:T(8,128)S(1)}, f32[8,8,128]{2,1,0:T(8,128)S(1)}, u32[]{:S(2)}, u32[]{:S(2)}) collective-permute-start(f32[8,8,128]{2,1,0:T(8,128)S(1)} %get-tuple-element.15), channel_id=1, source_target_pairs={{0,1},{1,2},{2,3},{3,4},{4,5},{5,6},{6,7},{7,8},{8,9},{9,10},{10,1... | collective-permute-start | bytes 98312 | tf_op jit(solution)/shard_map/ppermute | solution.py:474
  42.8 45.1 %collective-permute-start.3 = (f32[8,8,128]{2,1,0:T(8,128)S(1)}, f32[8,8,128]{2,1,0:T(8,128)S(1)}, u32[]{:S(2)}, u32[]{:S(2)}) collective-permute-start(f32[8,8,128]{2,1,0:T(8,128)S(1)} %get-tuple-element.16), channel_id=1, source_target_pairs={{0,15},{1,0},{2,1},{3,2},{4,3},{5,4},{6,5},{7,6},{8,7},{9,8},{10,9... | collective-permute-start | bytes 98312 | tf_op jit(solution)/shard_map/ppermute | solution.py:474
